TPU v7x, 128 devices: a whole 4x4x4 slice. The times are simulated.
128 devices in a mesh: tm: 32 (over y_hi, z, x), chan: 4 (over y_lo, core).
Axes of the slice: x: 4, y: 4 (y_hi: 2, y_lo: 2; y = y_hi * 2 + y_lo), z: 4, core: 2. Of those that a mesh axis runs over, the one named last changes fastest.
Arguments:
- signal: bfloat16 [128, 131072], P('chan', 'tm'), may hold values from -6 to 6
- cotangent: bfloat16 [128, 131072], P('chan', 'tm'), may hold values from -6 to 6
- log_step: float32 [128], P('chan'), may hold values from -5.8 to -3.5
- damping: float32 [128, 32], P('chan'), may hold values from 0.001 to 3
- frequency: float32 [128, 32], P('chan'), may hold values from 0.05 to 0.5
- coef_re: float32 [128, 32], P('chan'), may hold values from -0.9 to 0.9
- coef_im: float32 [128, 32], P('chan'), may hold values from -0.9 to 0.9
- skip_gain: float32 [128], P('chan'), may hold values from -3 to 3
- mix_weight: bfloat16 [128, 128], P('chan'), may hold values from -0.5 to 0.5
- embed_table: float32 [200, 128], P(None, 'chan'), may hold values from -1.8 to 1.8
- diffusion_step: int32 [1], replicated, may hold values from 0 to 199
Outputs:
- grad_signal: bfloat16 [128, 131072], P('chan', 'tm')
- grad_kernel: float32 [128, 131072], P('chan', 'tm')
- grad_log_step: float32 [128], P('chan')
- grad_damping: float32 [128, 32], P('chan')
- grad_frequency: float32 [128, 32], P('chan')
- grad_coef_re: float32 [128, 32], P('chan')
- grad_coef_im: float32 [128, 32], P('chan')
- grad_skip: float32 [128], P('chan')
- grad_mix: float32 [128, 128], P('chan')
- grad_table: float32 [200, 128], P(None, 'chan')
All inputs are finite; a program needn't handle non-finite values.
Results may differ from a plain program's by a relative error of at most 0.0034.
Values may be sent and summed in bfloat16 or wider, within the bound.
No kernel may reach another device: no remote copies, remote signals or barrier semaphores. Data moves between devices by JAX's collectives and lax.ppermute only.
A program may use at most 128 MiB of HBM per device.

v0:
```python
import functools

import jax
import jax.numpy as jnp
import numpy as np
from jax import lax
from jax.experimental import pallas as pl
from jax.experimental.pallas import tpu as pltpu
from jax.sharding import PartitionSpec as P

HIGHEST = lax.Precision.HIGHEST
F32 = jnp.float32
BF16 = jnp.bfloat16

CH = 32
MODES = 32
BLOCK = 4096
LN = 128
CK = BLOCK // LN
LANE_CH = LN // MODES
GROUPS = CH // LANE_CH
RANKS = 32
COLS = 512
PER = COLS // LN
ROWS = RANKS * BLOCK // COLS
SEND1 = 64
SEND2 = 56
SEND3 = 40
NT = (((1,), (1,)), ((), ()))
NN = (((1,), (0,)), ((), ()))
PARAMS = pltpu.CompilerParams(vmem_limit_bytes=40 * 1024 * 1024)


def mode_terms(log_step, damping, frequency, coef_re, coef_im):
    step_size = jnp.exp(log_step)
    decay_rate = step_size * damping
    turn_rate = step_size * frequency
    half_sine = jnp.sin(0.5 * turn_rate)
    grow_real = jnp.expm1(-decay_rate) * jnp.cos(turn_rate) - 2.0 * half_sine * half_sine
    grow_imag = jnp.exp(-decay_rate) * jnp.sin(turn_rate)
    spread = damping * damping + frequency * frequency
    hold_real = (frequency * grow_imag - damping * grow_real) / spread
    hold_imag = -(frequency * grow_real + damping * grow_imag) / spread
    weight_real = coef_re * hold_real - coef_im * hold_imag
    weight_imag = coef_re * hold_imag + coef_im * hold_real
    return (decay_rate, turn_rate, weight_real, weight_imag)


def cmul(ar, ai, br, bi):
    return ar * br - ai * bi, ar * bi + ai * br


def split(values):
    high = values.astype(BF16)
    return high, (values - high.astype(F32)).astype(BF16)


def dot(left, right, dims=NN):
    return lax.dot_general(left, right, dims, preferred_element_type=F32)


def dot3(left, right, dims=NN):
    lh, ll = left
    rh, rl = right
    return dot(lh, rh, dims) + dot(ll, rh, dims) + dot(lh, rl, dims)


def sin_cos(x):
    y = x * x
    s = 1.0
    for k in (210.0, 156.0, 110.0, 72.0, 42.0, 20.0, 6.0):
        s = 1.0 - y * s * (1.0 / k)
    c = 1.0
    for k in (240.0, 182.0, 132.0, 90.0, 56.0, 30.0, 12.0, 2.0):
        c = 1.0 - y * c * (1.0 / k)
    return x * s, c


def power(decay, turn, steps):
    size = jnp.exp(-decay * steps)
    s, c = sin_cos(turn * steps)
    return size * c, size * s


def doublings(decay, turn):
    return [power(decay, turn, float(k)) for k in (8, 16, 32, 64)]


def rising(decay, turn, doubles, g):
    rows = lax.broadcasted_iota(jnp.int32, (8, LN), 0).astype(F32)
    tr, ti = power(decay[g : g + 1], turn[g : g + 1], rows)
    for zr, zi in doubles:
        nr, ni = cmul(tr, ti, zr[g : g + 1], zi[g : g + 1])
        tr, ti = jnp.concatenate([tr, nr], 0), jnp.concatenate([ti, ni], 0)
    return tr, ti


def falling(decay, turn, doubles, g):
    rows = 7.0 - lax.broadcasted_iota(jnp.int32, (8, LN), 0).astype(F32)
    tr, ti = power(decay[g : g + 1], turn[g : g + 1], rows)
    for zr, zi in doubles:
        nr, ni = cmul(tr, ti, zr[g : g + 1], zi[g : g + 1])
        tr, ti = jnp.concatenate([nr, tr], 0), jnp.concatenate([ni, ti], 0)
    return tr, ti


def lane_channel(shape):
    return lax.broadcasted_iota(jnp.int32, shape, 1) // MODES


def gather_group(products):
    owner = lane_channel((CK, LN))
    real, imag = products[:, :LN], products[:, LN:]
    out_r, out_i = real[:CK], imag[:CK]
    for k in range(1, LANE_CH):
        mine = owner == k
        out_r = jnp.where(mine, real[k * CK : (k + 1) * CK], out_r)
        out_i = jnp.where(mine, imag[k * CK : (k + 1) * CK], out_i)
    return out_r, out_i


def spread_group(state_r, state_i, table):
    owner = lane_channel((CK, LN))
    zero = jnp.zeros((CK, LN), F32)
    left = jnp.concatenate(
        [
            jnp.concatenate(
                [jnp.where(owner == k, state_r, zero), jnp.where(owner == k, -state_i, zero)], 1
            )
            for k in range(LANE_CH)
        ],
        0,
    )
    return dot3(split(left), split(table), NT)


def scan_states(sr_ref, si_ref, power_r, power_i, start_r, start_i, order, keep):
    hr, hi = start_r, start_i
    for i in order:
        rows = pl.ds(i * GROUPS, GROUPS)
        own_r, own_i = sr_ref[rows, :], si_ref[rows, :]
        if keep:
            sr_ref[rows, :] = hr
            si_ref[rows, :] = hi
        nr, ni = cmul(power_r, power_i, hr, hi)
        hr, hi = nr + own_r, ni + own_i
    return hr, hi


def toeplitz(taps_row):
    rows = jnp.broadcast_to(taps_row, (LN, LN))
    turned = pltpu.roll(rows, 0, 1, stride=1, stride_axis=0)
    lag = lax.broadcasted_iota(jnp.int32, (LN, LN), 1) - lax.broadcasted_iota(
        jnp.int32, (LN, LN), 0
    )
    return jnp.where(lag >= 0, turned, 0.0)


def group_taps(terms, table, g):
    real = 2.0 * (terms[2][g : g + 1] * table[0] - terms[3][g : g + 1] * table[1])
    owner = (
        lane_channel((8, LN)) == lax.broadcasted_iota(jnp.int32, (8, LN), 0)
    ).astype(BF16)
    high, low = split(real)
    return dot(owner, high, NT) + dot(owner, low, NT)


def first_kernel(signal_ref, terms_ref, embed_ref, send_ref, sr_ref, si_ref, rows_ref):
    for i in range(CK):
        rows_ref[pl.ds(i, CH, stride=CK), :] = signal_ref[:, i * LN : (i + 1) * LN].astype(F32)
    decay, turn = terms_ref[0], terms_ref[1]
    doubles = doublings(decay, turn)
    for g in range(GROUPS):
        x = rows_ref[g * LN : (g + 1) * LN, :].astype(BF16)
        fr, fi = falling(decay, turn, doubles, g)
        table = jnp.concatenate([fr, fi], 1)
        th, tl = split(table)
        pr, pi = gather_group(dot(x, th) + dot(x, tl))
        level = embed_ref[g : g + 1]
        sr_ref[pl.ds(g, CK, stride=GROUPS), :] = pr + level * jnp.sum(fr, 0, keepdims=True)
        si_ref[pl.ds(g, CK, stride=GROUPS), :] = pi + level * jnp.sum(fi, 0, keepdims=True)
        for k in range(LANE_CH):
            send_ref[g * LANE_CH + k, :CK, :] = x[k * CK : (k + 1) * CK]
    zr, zi = power(decay, turn, float(LN))
    zero = jnp.zeros((GROUPS, LN), F32)
    hr, hi = scan_states(sr_ref, si_ref, zr, zi, zero, zero, range(CK), False)
    high, low = split(jnp.concatenate([hr, hi], 0))
    packed = jnp.concatenate([high, low], 0)
    for d in range(RANKS):
        send_ref[d, CK:SEND1, :] = packed


def first(signal, terms, embed_lanes):
    return pl.pallas_call(
        first_kernel,
        out_shape=(
            jax.ShapeDtypeStruct((RANKS, SEND1, LN), BF16),
            jax.ShapeDtypeStruct((CK * GROUPS, LN), F32),
            jax.ShapeDtypeStruct((CK * GROUPS, LN), F32),
        ),
        scratch_shapes=[pltpu.VMEM((CH * CK, LN), F32)],
        compiler_params=PARAMS,
        name="block_states",
    )(signal, terms, embed_lanes)


def within_kernel(x_ref, terms_ref, embed_ref, c0, c1, c2, c3, pick_ref, out_ref, act_ref):
    terms = terms_ref[0], terms_ref[1], terms_ref[2], terms_ref[3]
    doubles = doublings(terms[0], terms[1])
    for g in range(GROUPS):
        taps = group_taps(terms, rising(terms[0], terms[1], doubles, g), g)
        for k in range(LANE_CH):
            c = g * LANE_CH + k
            matrix = toeplitz(taps[k : k + 1])
            high, low = split(matrix)
            x = x_ref[c, :CK, :]
            level = embed_ref[c : c + 1, :]
            out_ref[c * CK : (c + 1) * CK, :] = (
                dot(x, high) + dot(x, low) + level * jnp.sum(matrix, 0, keepdims=True)
            )
    weights = jnp.concatenate([c[:, BLOCK:] for c in (c0, c1, c2, c3)], 0)
    weights = dot(pick_ref[...], weights, NT).astype(BF16)
    for i in range(CK):
        cols = slice(i * LN, (i + 1) * LN)
        cot = jnp.concatenate([c[:, cols] for c in (c0, c1, c2, c3)], 0)
        act_ref[pl.ds(i, CH, stride=CK), :] = dot(weights, cot)


def within(send, terms, embed_rows, parts, pick):
    return pl.pallas_call(
        within_kernel,
        out_shape=(
            jax.ShapeDtypeStruct((CH * CK, LN), F32),
            jax.ShapeDtypeStruct((CH * CK, LN), F32),
        ),
        compiler_params=PARAMS,
        name="within_chunks",
    )(send, terms, embed_rows, *parts, pick)


def gelu_both(x):
    scale = np.float32(np.sqrt(2.0 / np.pi))
    square = x * x
    t = jnp.tanh(scale * (x + 0.044715 * (square * x)))
    half = 0.5 * (1.0 + t)
    slope = half + 0.5 * x * (1.0 - t * t) * (scale * (1.0 + (3.0 * 0.044715) * square))
    return x * half, slope


def entering(states, table_r, table_i):
    hr = jnp.zeros((GROUPS, LN), F32)
    hi = jnp.zeros((GROUPS, LN), F32)
    for d in range(RANKS):
        sr, si = states(d)
        nr, ni = cmul(table_r[d], table_i[d], sr, si)
        hr, hi = hr + nr, hi + ni
    return hr, hi


def second_kernel(
    got_ref, x_ref, terms_ref, embed_ref, skip_ref, far_r, far_i, sr_in, si_in, out_ref, act_ref,
    c0, c1, c2, c3, send_ref, sr_ref, si_ref, activation_ref, flat_ref,
):
    terms = terms_ref[0], terms_ref[1], terms_ref[2], terms_ref[3]
    decay, turn = terms[0], terms[1]
    doubles = doublings(decay, turn)
    zr, zi = power(decay, turn, float(LN))
    one_r, one_i = power(decay, turn, 1.0)
    ur, ui = cmul(2.0 * terms[2], 2.0 * terms[3], one_r, one_i)

    def states(d):
        packed = got_ref[d, CK:SEND1, :].astype(F32)
        values = packed[: 2 * GROUPS] + packed[2 * GROUPS :]
        return values[:GROUPS], values[GROUPS:]

    start = entering(states, far_r, far_i)
    sr_ref[...] = sr_in[...]
    si_ref[...] = si_in[...]
    scan_states(sr_ref, si_ref, zr, zi, start[0], start[1], range(CK), True)
    for g in range(GROUPS):
        every = pl.ds(g, CK, stride=GROUPS)
        er, ei = rising(decay, turn, doubles, g)
        wr, wi = cmul(er, ei, ur[g : g + 1], ui[g : g + 1])
        inter = spread_group(sr_ref[every, :], si_ref[every, :], jnp.concatenate([wr, wi], 1))
        left = []
        for k in range(LANE_CH):
            c = g * LANE_CH + k
            rows = slice(c * CK, (c + 1) * CK)
            x = x_ref[c, :CK, :].astype(F32) + embed_ref[c : c + 1, :]
            mixed = out_ref[rows, :] + inter[k * CK : (k + 1) * CK] + skip_ref[c : c + 1, :] * x
            act, slope = gelu_both(mixed)
            activation_ref[rows, :] = act
            grad = act_ref[rows, :] * slope
            send_ref[c, :CK, :] = grad
            left.append(grad)
        products = dot3(split(jnp.concatenate(left, 0)), split(jnp.concatenate([er, ei], 1)))
        pr, pi = gather_group(products)
        sr_ref[every, :] = pr
        si_ref[every, :] = pi
    zero = jnp.zeros((GROUPS, LN), F32)
    hr, hi = scan_states(sr_ref, si_ref, zr, zi, zero, zero, range(CK - 1, -1, -1), False)
    for i in range(CK):
        flat_ref[:, i * LN : (i + 1) * LN] = activation_ref[pl.ds(i, CH, stride=CK), :].astype(BF16)
    flat = flat_ref[...]
    mix = jnp.concatenate([dot(flat, c[:, :BLOCK], NT) for c in (c0, c1, c2, c3)], 1)
    for d in range(RANKS):
        send_ref[d, CK : CK + GROUPS, :] = hr
        send_ref[d, CK + GROUPS : CK + 2 * GROUPS, :] = hi
        send_ref[d, CK + 2 * GROUPS :, :] = jnp.broadcast_to(mix[d : d + 1], (8, LN))


def second(got, send, terms, embed_rows, skip_rows, far, sr, si, out, grad_act, parts):
    return pl.pallas_call(
        second_kernel,
        out_shape=(
            jax.ShapeDtypeStruct((RANKS, SEND2, LN), F32),
            jax.ShapeDtypeStruct((CK * GROUPS, LN), F32),
            jax.ShapeDtypeStruct((CK * GROUPS, LN), F32),
        ),
        scratch_shapes=[pltpu.VMEM((CH * CK, LN), F32), pltpu.VMEM((CH, BLOCK), BF16)],
        compiler_params=PARAMS,
        name="activation_and_states",
    )(got, send, terms, embed_rows, skip_rows, far[0], far[1], sr, si, out, grad_act, *parts)


def back_kernel(send_ref, terms_ref, out_ref):
    terms = terms_ref[0], terms_ref[1], terms_ref[2], terms_ref[3]
    doubles = doublings(terms[0], terms[1])
    for g in range(GROUPS):
        taps = group_taps(terms, rising(terms[0], terms[1], doubles, g), g)
        for k in range(LANE_CH):
            c = g * LANE_CH + k
            out_ref[c * CK : (c + 1) * CK, :] = dot3(
                split(send_ref[c, :CK, :]), split(toeplitz(taps[k : k + 1])), NT
            )


def back(send, terms):
    return pl.pallas_call(
        back_kernel,
        out_shape=jax.ShapeDtypeStruct((CH * CK, LN), F32),
        compiler_params=PARAMS,
        name="back_within_chunks",
    )(send, terms)


def signal_kernel(
    got_ref, send_ref, terms_ref, skip_ref, far_r, far_i, sr_in, si_in, back_ref, cot_ref,
    out_ref, part_ref, sr_ref, si_ref, rows_ref,
):
    terms = terms_ref[0], terms_ref[1], terms_ref[2], terms_ref[3]
    decay, turn = terms[0], terms[1]
    doubles = doublings(decay, turn)
    zr, zi = power(decay, turn, float(LN))
    one_r, one_i = power(decay, turn, 1.0)
    ur, ui = cmul(2.0 * terms[2], 2.0 * terms[3], one_r, one_i)

    def states(d):
        return got_ref[d, CK : CK + GROUPS, :], got_ref[d, CK + GROUPS : CK + 2 * GROUPS, :]

    start = entering(states, far_r, far_i)
    sr_ref[...] = sr_in[...]
    si_ref[...] = si_in[...]
    scan_states(sr_ref, si_ref, zr, zi, start[0], start[1], range(CK - 1, -1, -1), True)
    for g in range(GROUPS):
        every = pl.ds(g, CK, stride=GROUPS)
        fr, fi = falling(decay, turn, doubles, g)
        wr, wi = cmul(fr, fi, ur[g : g + 1], ui[g : g + 1])
        inter = spread_group(sr_ref[every, :], si_ref[every, :], jnp.concatenate([wr, wi], 1))
        for k in range(LANE_CH):
            c = g * LANE_CH + k
            rows = slice(c * CK, (c + 1) * CK)
            grad = (
                back_ref[rows, :]
                + inter[k * CK : (k + 1) * CK]
                + skip_ref[c : c + 1, :] * send_ref[c, :CK, :]
            )
            rows_ref[rows, :] = grad
    total = jnp.zeros((CH, LN), F32)
    for i in range(CK):
        cols = slice(i * LN, (i + 1) * LN)
        grad = rows_ref[pl.ds(i, CH, stride=CK), :]
        total = total + grad
        out_ref[:, cols] = (cot_ref[:, cols].astype(F32) + grad).astype(BF16)
    part_ref[...] = total


def signal_grad(got, send, terms, skip_rows, far, sr, si, back_out, cotangent):
    return pl.pallas_call(
        signal_kernel,
        out_shape=(
            jax.ShapeDtypeStruct((CH, BLOCK), BF16),
            jax.ShapeDtypeStruct((CH, LN), F32),
        ),
        scratch_shapes=[
            pltpu.VMEM((CK * GROUPS, LN), F32),
            pltpu.VMEM((CK * GROUPS, LN), F32),
            pltpu.VMEM((CH * CK, LN), F32),
        ],
        compiler_params=PARAMS,
        name="signal_gradient",
    )(got, send, terms, skip_rows, far[0], far[1], sr, si, back_out, cotangent)


def dft_tables():
    full_len = RANKS * BLOCK
    row = np.arange(ROWS)
    time_row = (row % RANKS) * (BLOCK // COLS) + row // RANKS
    first_ids = np.arange(ROWS)
    column = np.arange(COLS)
    angle1 = (
        2.0 * np.pi * (((4 * first_ids[:, None] + 1) * time_row[None, :]) % (4 * ROWS)) / (4 * ROWS)
    )
    angle_t = 2.0 * np.pi * ((4 * first_ids[:, None] + 1) * column[None, :]) / (4 * full_len)
    angle2 = 2.0 * np.pi * ((column[:, None] * column[None, :]) % COLS) / COLS

    def halves(values):
        values = values.astype(np.float32)
        high = values.astype(BF16)
        return high, (values - high.astype(np.float32)).astype(BF16)

    stage1 = np.concatenate([np.cos(angle1), -np.sin(angle1)], 0)
    stage2 = np.concatenate([np.cos(angle2), np.sin(angle2)], 1)
    twiddle = np.stack([np.cos(angle_t), np.sin(angle_t)]).astype(np.float32)
    return halves(stage1), halves(stage1.T / full_len), halves(stage2), twiddle


def gather_rows(ref, stride, base):
    return jnp.concatenate(
        [
            jnp.concatenate(
                [
                    ref[pl.ds(base + piece * PER + q, RANKS, stride=stride), :]
                    for q in range(PER)
                ],
                1,
            )
            for piece in range(BLOCK // COLS)
        ],
        0,
    )


def forward_dft(rows, d1h, d1l, d2h, d2l, twiddle):
    xh, xl = split(rows)
    a = dot(d1h[...], xh) + dot(d1h[...], xl) + dot(d1l[...], xh)
    ar, ai = cmul(a[:ROWS], a[ROWS:], twiddle[0], -twiddle[1])
    p = dot3(split(jnp.concatenate([ar, ai], 0)), (d2h[...], d2l[...]))
    return p[:ROWS, :COLS] + p[ROWS:, COLS:], p[ROWS:, :COLS] - p[:ROWS, COLS:]


def inverse_dft(pr, pi, d1th, d1tl, d2h, d2l, twiddle):
    p = dot3(split(jnp.concatenate([pr, pi], 0)), (d2h[...], d2l[...]))
    br, bi = p[:ROWS, :COLS] - p[ROWS:, COLS:], p[ROWS:, :COLS] + p[:ROWS, COLS:]
    br, bi = cmul(br, bi, twiddle[0], twiddle[1])
    bh, bl = split(jnp.concatenate([br, bi], 0))
    return dot(d1th[...], bh) + dot(d1th[...], bl) + dot(d1tl[...], bh)


def spectrum_kernel(got_ref, embed_ref, d1h, d1l, d2h, d2l, twiddle, spec_ref, rows_ref, flat_ref):
    for d in range(RANKS):
        flat_ref[d * CK : (d + 1) * CK, :] = got_ref[d, :CK, :].astype(F32) + embed_ref[...]
    rows = gather_rows(flat_ref, CK, 0)
    rows_ref[...] = rows
    xr, xi = forward_dft(rows, d1h, d1l, d2h, d2l, twiddle)
    spec_ref[0] = xr
    spec_ref[1] = xi


def spectrum(got, embed_mine, tables):
    (d1h, d1l), unused, (d2h, d2l), twiddle = tables
    return pl.pallas_call(
        spectrum_kernel,
        out_shape=(
            jax.ShapeDtypeStruct((2, ROWS, COLS), F32),
            jax.ShapeDtypeStruct((ROWS, COLS), F32),
        ),
        scratch_shapes=[pltpu.VMEM((RANKS * CK, LN), F32)],
        compiler_params=PARAMS,
        name="input_spectrum",
    )(got, embed_mine, d1h, d1l, d2h, d2l, twiddle)


def correlate_kernel(
    got_ref, spec_ref, rows_ref, d1h, d1l, d1th, d1tl, d2h, d2l, twiddle, column_ref, turn_ref,
    pull_ref, send_ref, small_ref,
):
    g_rows = gather_rows(got_ref, SEND2, 0)
    gr, gi = forward_dft(g_rows, d1h, d1l, d2h, d2l, twiddle)
    xr, xi = spec_ref[0], spec_ref[1]
    pr = xr * gr + xi * gi
    pi = xr * gi - xi * gr
    kernel_rows = inverse_dft(pr, pi, d1th, d1tl, d2h, d2l, twiddle)
    for piece in range(BLOCK // COLS):
        for q in range(PER):
            send_ref[pl.ds(piece * PER + q, RANKS, stride=SEND3), :] = kernel_rows[
                piece * RANKS : (piece + 1) * RANKS, q * LN : (q + 1) * LN
            ]
    inner = dot3(split(kernel_rows), split(column_ref[...]))
    rr, ri = turn_ref[0], turn_ref[1]
    ids = lax.broadcasted_iota(jnp.int32, (ROWS, LN), 0)
    starts = ((ids % RANKS) * BLOCK + (ids // RANKS) * COLS).astype(F32)

    def total(values):
        return jnp.sum(values, 0, keepdims=True)

    by_r, by_i = rr * inner, ri * inner
    u, v = total(by_r), total(by_i)
    su, sv = total(starts * by_r), total(starts * by_i)

    def block(row, k):
        lanes = lax.broadcasted_iota(jnp.int32, (1, LN), 1)
        moved = pltpu.roll(row, (LN - k * MODES) % LN, 1) if k else row
        return jnp.where(lanes < MODES, moved, 0.0)

    cos_sum = block(u, 0) - block(v, 1)
    sin_sum = block(u, 1) + block(v, 0)
    cos_moment = block(u, 2) - block(v, 3) + block(su, 0) - block(sv, 1)
    sin_moment = block(u, 3) + block(v, 2) + block(su, 1) + block(sv, 0)
    grads = jnp.zeros((1, LN), F32)
    step = jnp.zeros((1, LN), F32)
    for k, value in enumerate((cos_sum, sin_sum, cos_moment, sin_moment)):
        wide = value
        for m in range(1, LANE_CH):
            wide = wide + pltpu.roll(value, m * MODES, 1)
        grads = grads + pull_ref[k : k + 1, :] * wide
        step = step + pull_ref[4 + k : 5 + k, :] * value
    step_sum = jnp.sum(step, 1, keepdims=True)
    skip_sum = jnp.sum(total(rows_ref[...] * g_rows), 1, keepdims=True)
    lanes = lax.broadcasted_iota(jnp.int32, (1, LN), 1)
    scalars = jnp.where(lanes == 0, step_sum, 0.0) + jnp.where(lanes == 1, skip_sum, 0.0)
    small_ref[...] = jnp.concatenate([grads, scalars, jnp.zeros((6, LN), F32)], 0)
    for d in range(RANKS):
        send_ref[d * SEND3 + CK : (d + 1) * SEND3, :] = small_ref[...]


def correlate(got, spec, rows, tables, column, turns, pull):
    (d1h, d1l), (d1th, d1tl), (d2h, d2l), twiddle = tables
    return pl.pallas_call(
        correlate_kernel,
        out_shape=(
            jax.ShapeDtypeStruct((RANKS * SEND3, LN), F32),
            jax.ShapeDtypeStruct((8, LN), F32),
        ),
        compiler_params=PARAMS,
        name="correlation",
    )(
        got.reshape(RANKS * SEND2, LN), spec, rows, d1h, d1l, d1th, d1tl, d2h, d2l, twiddle,
        column, turns, pull,
    )


def exchange(values):
    return lax.all_to_all(values, "tm", split_axis=0, concat_axis=0, tiled=True)


def mode_powers(decay_rate, turn_rate, positions):
    size = jnp.exp(-decay_rate * positions)
    turned = turn_rate * positions
    return size * jnp.cos(turned), size * jnp.sin(turned)


def shards(
    signal,
    cotangent,
    log_step,
    damping,
    frequency,
    coef_re,
    coef_im,
    skip_gain,
    mix_weight,
    embed_table,
    diffusion_step,
):
    me = lax.axis_index("tm")
    group = lax.axis_index("chan")
    tables = dft_tables()

    def swap(values, mask):
        return lax.ppermute(values, "chan", [(i, i ^ mask) for i in range(4)])

    own = jnp.concatenate([cotangent, mix_weight], 1)
    across = swap(own, 2)
    near = swap(own, 1)
    diagonal = swap(across, 1)
    parts = (own, near, across, diagonal)

    embed_row = lax.dynamic_slice_in_dim(embed_table, diffusion_step[0], 1, 0)[0]

    def on_lanes(values):
        return values.reshape(GROUPS, LN)

    def widened(values):
        return on_lanes(jnp.broadcast_to(values[:, None], (CH, MODES)))

    terms = jnp.stack(
        mode_terms(
            widened(log_step), on_lanes(damping), on_lanes(frequency), on_lanes(coef_re),
            on_lanes(coef_im),
        )
    )
    embed_lanes = widened(embed_row)
    embed_rows = jnp.broadcast_to(embed_row[:, None], (CH, LN))
    skip_rows = jnp.broadcast_to(skip_gain[:, None], (CH, LN))

    send1, sr, si = first(signal, terms, embed_lanes)
    got1 = exchange(send1)

    pick = (
        lax.broadcasted_iota(jnp.int32, (CH, 4 * CH), 1)
        == group * CH + lax.broadcasted_iota(jnp.int32, (CH, 4 * CH), 0)
    ).astype(BF16)
    out, grad_act = within(send1, terms, embed_rows, parts, pick)

    rank_ids = lax.iota(jnp.int32, RANKS)

    def far_powers(distance):
        keep = (distance >= 0).astype(F32)[:, None, None]
        steps = (jnp.maximum(distance, 0) * BLOCK).astype(F32)[:, None, None]
        pr, pi = mode_powers(terms[0][None], terms[1][None], steps)
        return pr * keep, pi * keep

    send2, br, bi = second(
        got1, send1, terms, embed_rows, skip_rows, far_powers(me - 1 - rank_ids), sr, si, out,
        grad_act, parts,
    )
    got2 = exchange(send2)
    back_out = back(send2, terms)

    def mine(values):
        return lax.dynamic_slice_in_dim(values, me, 1, 0)

    spec, x_rows = spectrum(
        got1, jnp.broadcast_to(mine(embed_row)[:, None], (CK, LN)), tables
    )

    raw = (
        jnp.broadcast_to(mine(log_step)[:, None], (1, MODES)),
        mine(damping), mine(frequency), mine(coef_re), mine(coef_im),
    )
    (d, th, mr, mi), pull = jax.vjp(mode_terms, *raw)
    zero = jnp.zeros_like(d)
    pulled = [
        pull((zero, zero, zero + 2.0, zero)),
        pull((zero, zero, zero, zero - 2.0)),
        pull((-2.0 * mr, -2.0 * mi, zero, zero)),
        pull((2.0 * mi, -2.0 * mr, zero, zero)),
    ]
    pull_table = jnp.concatenate(
        [jnp.concatenate(p[1:], 1) for p in pulled]
        + [jnp.pad(p[0], ((0, 0), (0, LN - MODES))) for p in pulled],
        0,
    )
    col = lax.broadcasted_iota(jnp.int32, (COLS, 1), 0).astype(F32)
    cr, ci = mode_powers(d, th, col)
    column = jnp.concatenate([cr, ci, cr * col, ci * col], 1)
    row_ids = lax.broadcasted_iota(jnp.int32, (ROWS, 1), 0)
    row_start = ((row_ids % RANKS) * BLOCK + (row_ids // RANKS) * COLS).astype(F32)
    rr, ri = mode_powers(jnp.tile(d, (1, 4)), jnp.tile(th, (1, 4)), row_start)
    send3, small = correlate(got2, spec, x_rows, tables, column, jnp.stack([rr, ri]), pull_table)

    grad_signal, part = signal_grad(
        got2, send2, terms, skip_rows, far_powers(rank_ids - me - 1), br, bi, back_out, cotangent
    )
    mix_sum = jnp.sum(got2[:, CK + 2 * GROUPS, :], axis=0).reshape(4, CH)
    mix_row = jnp.concatenate([mix_sum[:1]] + [swap(mix_sum[m : m + 1], m) for m in range(1, 4)], 1)
    extra = jnp.concatenate(
        [mix_row, jnp.pad(jnp.sum(part, 1)[None], ((0, 0), (0, LN - CH)))], 0
    )
    send3 = send3.reshape(RANKS, SEND3, LN)
    send3 = send3.at[:, CK + 2 : CK + 4, :].set(jnp.broadcast_to(extra, (RANKS, 2, LN)))
    got3 = exchange(send3)

    grad_kernel = got3[:, :CK, :].reshape(CH, BLOCK)
    grads = got3[:, CK, :]
    scalars = got3[:, CK + 1, :]
    mixes = got3[:, CK + 2, :].reshape(CH, 4, CH)
    grad_mix = jnp.concatenate(
        [
            lax.dynamic_index_in_dim(mixes, group ^ cg, 1, keepdims=False).T
            for cg in range(4)
        ],
        1,
    )
    table_row = jnp.sum(got3[:, CK + 3, :CH], 0)
    chosen = (lax.iota(jnp.int32, embed_table.shape[0]) == diffusion_step[0]).astype(F32)
    grad_table = chosen[:, None] * table_row[None, :]
    pieces = [grads[:, k * MODES : (k + 1) * MODES] for k in range(4)]
    return (
        grad_signal,
        grad_kernel,
        scalars[:, 0],
        pieces[0],
        pieces[1],
        pieces[2],
        pieces[3],
        scalars[:, 1],
        grad_mix,
        grad_table,
    )


def solution(mesh):
    placed = (
        P("chan", "tm"),
        P("chan", "tm"),
        P("chan"),
        P("chan", None),
        P("chan", None),
        P("chan", None),
        P("chan", None),
        P("chan"),
        P("chan", None),
        P(None, "chan"),
        P(),
    )
    return jax.shard_map(
        shards,
        mesh=mesh,
        in_specs=placed,
        out_specs=(
            P("chan", "tm"),
            P("chan", "tm"),
            P("chan"),
            P("chan", None),
            P("chan", None),
            P("chan", None),
            P("chan", None),
            P("chan"),
            P("chan", None),
            P(None, "chan"),
        ),
        check_vma=False,
    )
```

profile of v0, /device:TPU:0, one launch (start us, length us, event | category | flops | bytes accessed | tf_op | source)
XLA Modules:
  0.0 117.1 jit_solution(1547453678353190235)
XLA Ops:
  0.7 1.0 constant_dynamic-update-slice_fusion.1
  1.8 1.7 %collective-permute-start.1 = (bf16[32,4224]{1,0:T(8,128)(2,1)S(1)}, bf16[32,4224]{1,0:T(8,128)(2,1)S(1)}, u32[]{:S(2)}, u32[]{:S(2)}) collective-permute-start(bf16[32,4224]{1,0:T(8,128)(2,1)S(1)} %constant_dynamic-update-slice_fusion.c0), channel_id=1, source_target_pairs={{0,2},{1,3},{2,0},{3,1},{4,6},{5,7},{6,4},{7,5},{8,10},{9,11},{10,... | collective-permute-start | bytes 811016 | tf_op jit(solution)/shard_map/ppermute | solution.py:581
  5.3 1.9 %block_states.1 = (bf16[32,64,128]{2,1,0:T(8,128)(2,1)}, f32[256,128]{1,0:T(8,128)S(1)}, f32[256,128]{1,0:T(8,128)S(1)}) custom-call(bf16[32,4096]{1,0:T(8,128)(2,1)S(1)} %copy-done.19, f32[4,8,128]{2,1,0:T(8,128)S(1)} %pad_maximum_fusion.2.terms_ref, f32[8,128]{1,0:T(8,128)S(1)} %broadcast_in_dim.27.embed_ref), custom_call_target="tpu_custom_call" | custom-call | tf_op jit(solution)/shard_map/block_states/pallas_call | solution.py:194
  7.1 10.5 %all-to-all-start = ((bf16[32,64,128]{2,1,0:T(8,128)(2,1)}), bf16[32,64,128]{2,1,0:T(8,128)(2,1)S(1)}, u32[]{:S(2)}, u32[]{:S(2)}) async-start(bf16[32,64,128]{2,1,0:T(8,128)(2,1)} %get-tuple-element.35.x_ref), calls=%async_computation | async-start | bytes 1048576 | tf_op jit(solution)/shard_map/all_to_all | solution.py:554
  21.5 1.8 %fusion.9 = (f32[32,8,128]{2,1,0:T(8,128)}, f32[32,8,128]{2,1,0:T(8,128)}, f32[32,8,128]{2,1,0:T(8,128)S(1)}, f32[32,8,128]{2,1,0:T(8,128)S(1)}) fusion(f32[32]{0:T(128)S(1)} %get-tuple-element.158, f32[32]{0:T(128)S(1)} %get-tuple-element.160, f32[8,128]{1,0:T(8,128)S(1)} %get-tuple-element.122, f32[8,128]{1,0:T(8,128)S(1)} %get-tuple-element.121, ...), kind=kLoop, calls=%fused_computation.21 | loop fusion | flops 393216 | bytes 532992 | tf_op jit(solution)/shard_map/mul | solution.py:622
  23.4 4.1 %within_chunks.1 = (f32[1024,128]{1,0:T(8,128)S(1)}, f32[1024,128]{1,0:T(8,128)S(1)}) custom-call(bf16[32,64,128]{2,1,0:T(8,128)(2,1)} %get-tuple-element.35.x_ref, f32[4,8,128]{2,1,0:T(8,128)S(1)} %pad_maximum_fusion.2.terms_ref, f32[32,128]{1,0:T(8,128)S(1)} %broadcast_in_dim.29.embed_ref, bf16[32,4224]{1,0:T(8,128)(2,1)S(1)} %constant_dynamic-update-slice_fusion.c0, ...), custom_call_target="tpu_custom_call" | custom-call | tf_op jit(solution)/shard_map/within_chunks/pallas_call | solution.py:230
  27.5 3.9 %all-to-all-done.got_ref = bf16[32,64,128]{2,1,0:T(8,128)(2,1)S(1)} async-done(((bf16[32,64,128]{2,1,0:T(8,128)(2,1)}), bf16[32,64,128]{2,1,0:T(8,128)(2,1)S(1)}, u32[]{:S(2)}, u32[]{:S(2)}) %all-to-all-start) | async-done | bytes 524320 | tf_op jit(solution)/shard_map/all_to_all | solution.py:554
  31.3 0.7 copy-done.36
  32.0 4.4 %activation_and_states.1 = (f32[32,56,128]{2,1,0:T(8,128)}, f32[256,128]{1,0:T(8,128)S(1)}, f32[256,128]{1,0:T(8,128)S(1)}) custom-call(bf16[32,64,128]{2,1,0:T(8,128)(2,1)S(1)} %all-to-all-done.got_ref, bf16[32,64,128]{2,1,0:T(8,128)(2,1)} %get-tuple-element.35.x_ref, f32[4,8,128]{2,1,0:T(8,128)S(1)} %pad_maximum_fusion.2.terms_ref, ...), custom_call_target="tpu_custom_call" | custom-call | tf_op jit(solution)/shard_map/activation_and_states/pallas_call | solution.py:313
  37.7 6.0 %all-to-all-start.1 = ((f32[32,56,128]{2,1,0:T(8,128)}), f32[32,56,128]{2,1,0:T(8,128)S(1)}, u32[]{:S(2)}, u32[]{:S(2)}) async-start(f32[32,56,128]{2,1,0:T(8,128)} %get-tuple-element.40.send_ref), calls=%async_computation.1 | async-start | bytes 1835008 | tf_op jit(solution)/shard_map/all_to_all | solution.py:554
  44.3 0.7 pad_maximum_fusion.1.turn_ref
  45.0 1.9 %fusion = (f32[512,32]{1,0:T(8,128)S(1)}, f32[512,32]{1,0:T(8,128)S(1)}, f32[512,32]{1,0:T(8,128)S(1)}, f32[512,32]{1,0:T(8,128)S(1)}) fusion(f32[32]{0:T(128)} %bitcast.50, f32[32]{0:T(128)} %bitcast.48, f32[512]{0:T(512)S(1)} %iota_convert_fusion), kind=kLoop, calls=%fused_computation.3 | loop fusion | flops 98304 | bytes 264448 | tf_op jit(solution)/shard_map/mul | solution.py:560
  46.9 1.0 pad_maximum_fusion.column_ref
  47.9 0.6 broadcast_in_dim.63.embed_ref
  48.6 0.9 copy-done.6
  49.5 0.9 copy-done.8
  50.5 2.8 %input_spectrum.1 = (f32[2,256,512]{2,1,0:T(8,128)S(1)}, f32[256,512]{1,0:T(8,128)S(1)}) custom-call(bf16[32,64,128]{2,1,0:T(8,128)(2,1)S(1)} %all-to-all-done.got_ref, f32[32,128]{1,0:T(8,128)S(1)} %broadcast_in_dim.63.embed_ref, bf16[512,256]{1,0:T(8,128)(2,1)S(1)} %copy-done.6, bf16[512,256]{1,0:T(8,128)(2,1)S(1)} %copy-done.8, ...), custom_call_target="tpu_custom_call" | custom-call | tf_op jit(solution)/shard_map/input_spectrum/pallas_call | solution.py:472
  53.3 1.0 copy-done.4
  54.3 0.8 copy-done.13
  55.0 5.0 %back_within_chunks.1.back_ref = f32[1024,128]{1,0:T(8,128)S(1)} custom-call(f32[32,56,128]{2,1,0:T(8,128)} %get-tuple-element.40.send_ref, f32[4,8,128]{2,1,0:T(8,128)S(1)} %pad_maximum_fusion.2.terms_ref), custom_call_target="tpu_custom_call" | custom-call | tf_op jit(solution)/shard_map/back_within_chunks/pallas_call | solution.py:339
  60.0 1.1 all-to-all-done.1.got_ref
  61.1 0.9 copy-done.11
  62.0 0.9 copy-done.15
  62.9 0.9 copy-done.16
  63.8 0.7 copy-done.21
  64.6 0.9 copy-done.23
  65.5 0.9 copy-done.25
  66.4 3.1 %signal_gradient.1 = (bf16[32,4096]{1,0:T(8,128)(2,1)}, f32[32,128]{1,0:T(8,128)S(1)}) custom-call(f32[32,56,128]{2,1,0:T(8,128)S(1)} %all-to-all-done.1.got_ref, f32[32,56,128]{2,1,0:T(8,128)} %get-tuple-element.40.send_ref, f32[4,8,128]{2,1,0:T(8,128)S(1)} %pad_maximum_fusion.2.terms_ref, f32[32,128]{1,0:T(8,128)S(1)} %copy-done.21, ...), custom_call_target="tpu_custom_call" | custom-call | tf_op jit(solution)/shard_map/signal_gradient/pallas_call | solution.py:389
  70.1 0.8 reduce_sum.28
  71.3 1.6 %collective-permute-start.5 = (f32[1,32]{1,0:T(1,128)S(1)}, f32[1,32]{1,0:T(1,128)S(1)}, u32[]{:S(2)}, u32[]{:S(2)}) collective-permute-start(f32[1,32]{1,0:T(1,128)S(1)} %get-tuple-element.153), channel_id=1, source_target_pairs={{0,3},{1,2},{2,1},{3,0},{4,7},{5,6},{6,5},{7,4},{8,11},{9,10},{10,... | collective-permute-start | bytes 392 | tf_op jit(solution)/shard_map/ppermute | solution.py:581
  73.0 1.2 %copy-done.3 = f32[2,256,512]{2,1,0:T(8,128)S(1)} copy-done((f32[2,256,512]{2,1,0:T(8,128)S(1)}, f32[2,256,512]{2,1,0:T(8,128)}, u32[]{:S(2)}) %copy-start.3) | copy-done | bytes 1048600
  74.2 1.2 %copy-done.5 = f32[2,256,512]{2,1,0:T(8,128)S(1)} copy-done((f32[2,256,512]{2,1,0:T(8,128)S(1)}, f32[2,256,512]{2,1,0:T(8,128)}, u32[]{:S(2)}) %copy-start.5) | copy-done | bytes 1048600
  75.4 0.9 copy-done.7
  76.4 0.9 copy-done.9
  77.3 0.9 copy-done.10
  78.3 0.9 copy-done.12
  79.2 1.0 copy-done.14
  80.3 0.9 copy-done.17
  81.2 0.9 copy-done.18
  82.2 6.3 %correlation.1 = (f32[1280,128]{1,0:T(8,128)}, f32[8,128]{1,0:T(8,128)}) custom-call(f32[1792,128]{1,0:T(8,128)S(1)} %bitcast.38, f32[2,256,512]{2,1,0:T(8,128)S(1)} %copy-done.5, f32[256,512]{1,0:T(8,128)S(1)} %copy-done.14, bf16[512,256]{1,0:T(8,128)(2,1)S(1)} %copy-done.7, bf16[512,256]{1,0:T(8,128)(2,1)S(1)} %copy-done.9, ...), custom_call_target="tpu_custom_call" | custom-call | tf_op jit(solution)/shard_map/correlation/pallas_call | solution.py:539
  88.5 0.7 broadcast_dynamic-update-slice_fusion
  89.2 8.6 %all-to-all-start.2 = ((f32[32,40,128]{2,1,0:T(8,128)}), f32[32,40,128]{2,1,0:T(8,128)S(1)}, u32[]{:S(2)}, u32[]{:S(2)}) async-start(f32[32,40,128]{2,1,0:T(8,128)} %broadcast_dynamic-update-slice_fusion), calls=%async_computation.2 | async-start | bytes 1310720 | tf_op jit(solution)/shard_map/all_to_all | solution.py:554
  97.8 14.7 %all-to-all-done.2 = f32[32,40,128]{2,1,0:T(8,128)S(1)} async-done(((f32[32,40,128]{2,1,0:T(8,128)}), f32[32,40,128]{2,1,0:T(8,128)S(1)}, u32[]{:S(2)}, u32[]{:S(2)}) %all-to-all-start.2) | async-done | bytes 655392 | tf_op jit(solution)/shard_map/all_to_all | solution.py:554
  113.2 1.1 copy.50
  114.3 0.7 fusion.34
  115.0 0.7 slice_reduce_fusion.2
  115.7 0.7 broadcast_multiply_fusion.2
  116.4 0.7 pad_maximum_fusion.3
  (131 shorter events, 7.9 us)
Async XLA Ops:
  0.6 1.1 copy-start.35
  0.7 2.9 %copy-start.37 = (f32[32]{0:T(128)S(1)}, f32[32]{0:T(128)}, u32[]{:S(2)}) copy-start(f32[32]{0:T(128)} %param.22) | copy-start | bytes 388
  0.7 3.1 %copy-start.31 = (f32[32,32]{1,0:T(8,128)S(1)}, f32[32,32]{1,0:T(8,128)}, u32[]{:S(2)}) copy-start(f32[32,32]{1,0:T(8,128)} %param.25) | copy-start | bytes 12292
  0.7 3.2 %copy-start.30 = (f32[32,32]{1,0:T(8,128)S(1)}, f32[32,32]{1,0:T(8,128)}, u32[]{:S(2)}) copy-start(f32[32,32]{1,0:T(8,128)} %param.26) | copy-start | bytes 12292
  0.7 3.2 %copy-start.29 = (f32[32,32]{1,0:T(8,128)S(1)}, f32[32,32]{1,0:T(8,128)}, u32[]{:S(2)}) copy-start(f32[32,32]{1,0:T(8,128)} %param.23) | copy-start | bytes 12292
  0.7 3.3 %copy-start.28 = (f32[32,32]{1,0:T(8,128)S(1)}, f32[32,32]{1,0:T(8,128)}, u32[]{:S(2)}) copy-start(f32[32,32]{1,0:T(8,128)} %param.24) | copy-start | bytes 12292
  0.7 4.0 %copy-start.33 = (f32[200,32]{0,1:T(8,128)S(1)}, f32[200,32]{0,1:T(8,128)}, u32[]{:S(2)}) copy-start(f32[200,32]{0,1:T(8,128)} %param.29) | copy-start | bytes 76804
  1.7 3.5 %copy-start.19 = (bf16[32,4096]{1,0:T(8,128)(2,1)S(1)}, bf16[32,4096]{1,0:T(8,128)(2,1)}, u32[]{:S(2)}) copy-start(bf16[32,4096]{1,0:T(8,128)(2,1)} %signal_ref.1) | copy-start | bytes 786436
  1.8 18.0 %collective-permute-start.1 = (bf16[32,4224]{1,0:T(8,128)(2,1)S(1)}, bf16[32,4224]{1,0:T(8,128)(2,1)S(1)}, u32[]{:S(2)}, u32[]{:S(2)}) collective-permute-start(bf16[32,4224]{1,0:T(8,128)(2,1)S(1)} %constant_dynamic-update-slice_fusion.c0), channel_id=1, source_target_pairs={{0,2},{1,3},{2,0},{3,1},{4,6},{5,7},{6,4},{7,5},{8,10},{9,11},{10,... | collective-permute-start | bytes 811016 | tf_op jit(solution)/shard_map/ppermute | solution.py:581
  3.5 19.8 %collective-permute-start = (bf16[32,4224]{1,0:T(8,128)(2,1)S(1)}, bf16[32,4224]{1,0:T(8,128)(2,1)S(1)}, u32[]{:S(2)}, u32[]{:S(2)}) collective-permute-start(bf16[32,4224]{1,0:T(8,128)(2,1)S(1)} %constant_dynamic-update-slice_fusion.c0), channel_id=1, source_target_pairs={{0,1},{1,0},{2,3},{3,2},{4,5},{5,4},{6,7},{7,6},{8,9},{9,8},{10,11... | collective-permute-start | bytes 811016 | tf_op jit(solution)/shard_map/ppermute | solution.py:581
  7.1 24.2 %all-to-all-start = ((bf16[32,64,128]{2,1,0:T(8,128)(2,1)}), bf16[32,64,128]{2,1,0:T(8,128)(2,1)S(1)}, u32[]{:S(2)}, u32[]{:S(2)}) async-start(bf16[32,64,128]{2,1,0:T(8,128)(2,1)} %get-tuple-element.35.x_ref), calls=%async_computation | async-start | bytes 1048576 | tf_op jit(solution)/shard_map/all_to_all | solution.py:554
  19.3 0.9 copy-start.32
  19.4 0.7 copy-start.34
  19.8 3.5 %collective-permute-start.2 = (bf16[32,4224]{1,0:T(8,128)(2,1)S(1)}, bf16[32,4224]{1,0:T(8,128)(2,1)S(1)}, u32[]{:S(2)}, u32[]{:S(2)}) collective-permute-start(bf16[32,4224]{1,0:T(8,128)(2,1)S(1)} %collective-permute-done.1.c2), channel_id=1, source_target_pairs={{0,1},{1,0},{2,3},{3,2},{4,5},{5,4},{6,7},{7,6},{8,9},{9,8},{10,11... | collective-permute-start | bytes 811016 | tf_op jit(solution)/shard_map/ppermute | solution.py:581
  31.3 0.7 copy-start.36
  32.0 4.4 %copy-start.20 = (f32[32,128]{1,0:T(8,128)}, f32[32,128]{1,0:T(8,128)S(1)}, u32[]{:S(2)}) copy-start(f32[32,128]{1,0:T(8,128)S(1)} %broadcast_in_dim.30.skip_ref) | copy-start | bytes 49156
  36.4 0.6 copy-start.22
  37.1 0.6 copy-start.24
  37.7 23.4 %all-to-all-start.1 = ((f32[32,56,128]{2,1,0:T(8,128)}), f32[32,56,128]{2,1,0:T(8,128)S(1)}, u32[]{:S(2)}, u32[]{:S(2)}) async-start(f32[32,56,128]{2,1,0:T(8,128)} %get-tuple-element.40.send_ref), calls=%async_computation.1 | async-start | bytes 1835008 | tf_op jit(solution)/shard_map/all_to_all | solution.py:554
  43.7 4.8 %copy-start.2 = (f32[2,256,512]{2,1,0:T(8,128)S(1)}, f32[2,256,512]{2,1,0:T(8,128)}, u32[]{:S(2)}) copy-start(f32[2,256,512]{2,1,0:T(8,128)} %constant.142.clone.twiddle) | copy-start | bytes 3145732
  45.0 3.5 %copy-start = (bf16[512,1024]{1,0:T(8,128)(2,1)S(1)}, bf16[512,1024]{1,0:T(8,128)(2,1)}, u32[]{:S(2)}) copy-start(bf16[512,1024]{1,0:T(8,128)(2,1)} %constant.140.clone.d2h) | copy-start | bytes 3145732
  45.0 3.5 %copy-start.1 = (bf16[512,1024]{1,0:T(8,128)(2,1)S(1)}, bf16[512,1024]{1,0:T(8,128)(2,1)}, u32[]{:S(2)}) copy-start(bf16[512,1024]{1,0:T(8,128)(2,1)} %constant.141.clone.d2l) | copy-start | bytes 3145732
  48.6 1.0 copy-start.6
  49.5 0.9 copy-start.8
  53.2 1.0 copy-start.4
  54.3 0.8 copy-start.13
  61.1 1.0 copy-start.11
  62.0 0.9 copy-start.15
  62.9 0.9 copy-start.16
  63.8 0.7 copy-start.21
  64.6 0.9 copy-start.23
  65.5 0.9 copy-start.25
  69.5 0.6 copy-start.27
  71.1 17.4 %collective-permute-start.3 = (f32[1,32]{1,0:T(1,128)S(1)}, f32[1,32]{1,0:T(1,128)S(1)}, u32[]{:S(2)}, u32[]{:S(2)}) collective-permute-start(f32[1,32]{1,0:T(1,128)S(1)} %get-tuple-element.155), channel_id=1, source_target_pairs={{0,1},{1,0},{2,3},{3,2},{4,5},{5,4},{6,7},{7,6},{8,9},{9,8},{10,11... | collective-permute-start | bytes 392 | tf_op jit(solution)/shard_map/ppermute | solution.py:581
  71.1 1.9 %copy-start.26 = (f32[8,128]{1,0:T(8,128)S(1)}, f32[8,128]{1,0:T(8,128)}, u32[]{:S(2)}) copy-start(f32[8,128]{1,0:T(8,128)} %concatenate.38.pull_ref) | copy-start | bytes 12292
  71.1 17.3 %collective-permute-start.4 = (f32[1,32]{1,0:T(1,128)S(1)}, f32[1,32]{1,0:T(1,128)S(1)}, u32[]{:S(2)}, u32[]{:S(2)}) collective-permute-start(f32[1,32]{1,0:T(1,128)S(1)} %get-tuple-element.154), channel_id=1, source_target_pairs={{0,2},{1,3},{2,0},{3,1},{4,6},{5,7},{6,4},{7,5},{8,10},{9,11},{10,... | collective-permute-start | bytes 392 | tf_op jit(solution)/shard_map/ppermute | solution.py:581
  71.3 17.1 %collective-permute-start.5 = (f32[1,32]{1,0:T(1,128)S(1)}, f32[1,32]{1,0:T(1,128)S(1)}, u32[]{:S(2)}, u32[]{:S(2)}) collective-permute-start(f32[1,32]{1,0:T(1,128)S(1)} %get-tuple-element.153), channel_id=1, source_target_pairs={{0,3},{1,2},{2,1},{3,0},{4,7},{5,6},{6,5},{7,4},{8,11},{9,10},{10,... | collective-permute-start | bytes 392 | tf_op jit(solution)/shard_map/ppermute | solution.py:581
  73.0 1.2 %copy-start.3 = (f32[2,256,512]{2,1,0:T(8,128)S(1)}, f32[2,256,512]{2,1,0:T(8,128)}, u32[]{:S(2)}) copy-start(f32[2,256,512]{2,1,0:T(8,128)} %constant.142.clone.twiddle) | copy-start | bytes 3145732
  74.2 1.2 %copy-start.5 = (f32[2,256,512]{2,1,0:T(8,128)S(1)}, f32[2,256,512]{2,1,0:T(8,128)}, u32[]{:S(2)}) copy-start(f32[2,256,512]{2,1,0:T(8,128)} %copy-done.4) | copy-start | bytes 3145732
  75.4 0.9 copy-start.7
  76.4 0.9 copy-start.9
  77.3 0.9 copy-start.10
  78.3 0.9 copy-start.12
  79.2 1.0 copy-start.14
  80.3 0.9 copy-start.17
  81.2 0.9 copy-start.18
  89.2 23.4 %all-to-all-start.2 = ((f32[32,40,128]{2,1,0:T(8,128)}), f32[32,40,128]{2,1,0:T(8,128)S(1)}, u32[]{:S(2)}, u32[]{:S(2)}) async-start(f32[32,40,128]{2,1,0:T(8,128)} %broadcast_dynamic-update-slice_fusion), calls=%async_computation.2 | async-start | bytes 1310720 | tf_op jit(solution)/shard_map/all_to_all | solution.py:554
where the time goes:
time: 118 us; the launch traced here: 117 us
  local copies, waits for them, and re-layouts  29.6 us (25%)
  starting transfers between devices  29 us (25%)
  Pallas kernels  27.5 us (23%)
  waiting for transfers between devices  19.6 us (17%)
  other arithmetic  8.93 us (8%)
  between operations  2.5 us (2%)
    all_to_all x3, starting transfers between devices, exchange(): return lax.all_to_all(values, 'tm', split_axis=0, concat_axis=0, tiled=True)  25.1 us
    unnamed x78, local copies, waits for them, and re-layouts  22.9 us
    all_to_all x3, waiting for transfers between devices, exchange(): return lax.all_to_all(values, 'tm', split_axis=0, concat_axis=0, tiled=True)  19.6 us
    pallas_call x1, Pallas kernels, correlate(): pl.pallas_call(correlate_kernel, out_shape=(jax.ShapeDtypeStruct((RANKS *...  6.25 us
    pallas_call x1, Pallas kernels, back(): pl.pallas_call(back_kernel, out_shape=jax.ShapeDtypeStruct((CH * CK, LN),...  4.97 us
    pallas_call x1, Pallas kernels, second(): pl.pallas_call(second_kernel, out_shape=(jax.ShapeDtypeStruct((RANKS, SEN...  4.39 us
    pallas_call x1, Pallas kernels, within(): pl.pallas_call(within_kernel, out_shape=(jax.ShapeDtypeStruct((CH * CK, L...  4.09 us
    ppermute x6, starting transfers between devices, swap(): return lax.ppermute(values, 'chan', [(i, i ^ mask) for i in range(4)])  3.87 us
  transfers between devices with their start and end apart: 9, of which 3 were waited for; matrix products, arithmetic and copies ran while one was open for 9% of the time, Pallas kernels for 17%

commit v1 on v0

v1 whole, which is shorter than its diff:
```python
import functools

import jax
import jax.numpy as jnp
import numpy as np
from jax import lax
from jax.experimental import pallas as pl
from jax.experimental.pallas import tpu as pltpu
from jax.sharding import PartitionSpec as P

HIGHEST = lax.Precision.HIGHEST
F32 = jnp.float32
BF16 = jnp.bfloat16

CH = 32
MODES = 32
BLOCK = 4096
LN = 128
CK = BLOCK // LN
LANE_CH = LN // MODES
GROUPS = CH // LANE_CH
RANKS = 32
COLS = 512
PER = COLS // LN
ROWS = RANKS * BLOCK // COLS
SEND1 = 64
SEND2 = 64
SEND3 = 80
NT = (((1,), (1,)), ((), ()))
NN = (((1,), (0,)), ((), ()))
PARAMS = pltpu.CompilerParams(vmem_limit_bytes=56 * 1024 * 1024)
SMEM = pl.BlockSpec(memory_space=pltpu.SMEM)
VMEM = pl.BlockSpec(memory_space=pltpu.VMEM)
ANY = pl.BlockSpec(memory_space=pl.ANY)


def expm1_small(x):
    r = 1.0
    for k in (7.0, 6.0, 5.0, 4.0, 3.0, 2.0):
        r = 1.0 + x * r * (1.0 / k)
    return x * r


def mode_terms(step_size, damping, frequency, coef_re, coef_im):
    decay_rate = step_size * damping
    turn_rate = step_size * frequency
    half_sine = jnp.sin(0.5 * turn_rate)
    grow_real = expm1_small(-decay_rate) * jnp.cos(turn_rate) - 2.0 * half_sine * half_sine
    grow_imag = jnp.exp(-decay_rate) * jnp.sin(turn_rate)
    inverse = 1.0 / (damping * damping + frequency * frequency)
    hold_real = (frequency * grow_imag - damping * grow_real) * inverse
    hold_imag = -(frequency * grow_real + damping * grow_imag) * inverse
    weight_real = coef_re * hold_real - coef_im * hold_imag
    weight_imag = coef_re * hold_imag + coef_im * hold_real
    return (decay_rate, turn_rate, weight_real, weight_imag)


def cmul(ar, ai, br, bi):
    return ar * br - ai * bi, ar * bi + ai * br


def split(values):
    high = values.astype(BF16)
    return high, (values - high.astype(F32)).astype(BF16)


def dot(left, right, dims=NN):
    return lax.dot_general(left, right, dims, preferred_element_type=F32)


def dot3(left, right, dims=NN):
    lh, ll = left
    rh, rl = right
    return dot(lh, rh, dims) + dot(ll, rh, dims) + dot(lh, rl, dims)


def started(sems, *pairs):
    copies = [pltpu.make_async_copy(a, b, sems.at[k]) for k, (a, b) in enumerate(pairs)]
    for copy in copies:
        copy.start()
    return copies


def sin_cos(x):
    y = x * x
    s = 1.0
    for k in (210.0, 156.0, 110.0, 72.0, 42.0, 20.0, 6.0):
        s = 1.0 - y * s * (1.0 / k)
    c = 1.0
    for k in (240.0, 182.0, 132.0, 90.0, 56.0, 30.0, 12.0, 2.0):
        c = 1.0 - y * c * (1.0 / k)
    return x * s, c


def power(decay, turn, steps):
    size = jnp.exp(-decay * steps)
    s, c = sin_cos(turn * steps)
    return size * c, size * s


def doublings(decay, turn):
    return [power(decay, turn, float(k)) for k in (8, 16, 32, 64)]


def rising(decay, turn, doubles, g):
    rows = lax.broadcasted_iota(jnp.int32, (8, LN), 0).astype(F32)
    tr, ti = power(decay[g : g + 1], turn[g : g + 1], rows)
    for zr, zi in doubles:
        nr, ni = cmul(tr, ti, zr[g : g + 1], zi[g : g + 1])
        tr, ti = jnp.concatenate([tr, nr], 0), jnp.concatenate([ti, ni], 0)
    return tr, ti


def falling(decay, turn, doubles, g):
    rows = 7.0 - lax.broadcasted_iota(jnp.int32, (8, LN), 0).astype(F32)
    tr, ti = power(decay[g : g + 1], turn[g : g + 1], rows)
    for zr, zi in doubles:
        nr, ni = cmul(tr, ti, zr[g : g + 1], zi[g : g + 1])
        tr, ti = jnp.concatenate([nr, tr], 0), jnp.concatenate([ni, ti], 0)
    return tr, ti


def lane_channel(shape):
    return lax.broadcasted_iota(jnp.int32, shape, 1) // MODES


def gather_group(products):
    owner = lane_channel((CK, LN))
    real, imag = products[:, :LN], products[:, LN:]
    out_r, out_i = real[:CK], imag[:CK]
    for k in range(1, LANE_CH):
        mine = owner == k
        out_r = jnp.where(mine, real[k * CK : (k + 1) * CK], out_r)
        out_i = jnp.where(mine, imag[k * CK : (k + 1) * CK], out_i)
    return out_r, out_i


def spread_group(state_r, state_i, table):
    owner = lane_channel((CK, LN))
    zero = jnp.zeros((CK, LN), F32)
    left = jnp.concatenate(
        [
            jnp.concatenate(
                [jnp.where(owner == k, state_r, zero), jnp.where(owner == k, -state_i, zero)], 1
            )
            for k in range(LANE_CH)
        ],
        0,
    )
    return dot3(split(left), split(table), NT)


def scan_states(sr_ref, si_ref, power_r, power_i, start_r, start_i, order, keep):
    hr, hi = start_r, start_i
    for i in order:
        rows = pl.ds(i * GROUPS, GROUPS)
        own_r, own_i = sr_ref[rows, :], si_ref[rows, :]
        if keep:
            sr_ref[rows, :] = hr
            si_ref[rows, :] = hi
        nr, ni = cmul(power_r, power_i, hr, hi)
        hr, hi = nr + own_r, ni + own_i
    return hr, hi


def toeplitz(taps_row):
    rows = jnp.broadcast_to(taps_row, (LN, LN))
    turned = pltpu.roll(rows, 0, 1, stride=1, stride_axis=0)
    lag = lax.broadcasted_iota(jnp.int32, (LN, LN), 1) - lax.broadcasted_iota(
        jnp.int32, (LN, LN), 0
    )
    return jnp.where(lag >= 0, turned, 0.0)


def group_taps(terms, table, g):
    real = 2.0 * (terms[2][g : g + 1] * table[0] - terms[3][g : g + 1] * table[1])
    owner = (
        lane_channel((8, LN)) == lax.broadcasted_iota(jnp.int32, (8, LN), 0)
    ).astype(BF16)
    high, low = split(real)
    return dot(owner, high, NT) + dot(owner, low, NT)


def packed_lanes(ref):
    return jnp.concatenate([ref[pl.ds(k, GROUPS, stride=LANE_CH), :] for k in range(LANE_CH)], 1)


def as_column(row):
    shape = (CH, CH)
    same = lax.broadcasted_iota(jnp.int32, shape, 0) == lax.broadcasted_iota(jnp.int32, shape, 1)
    return jnp.sum(jnp.where(same, row, 0.0), 1, keepdims=True)


def first_kernel(
    step_ref, signal_hbm, cot_hbm, mix_hbm, size_ref, damping_ref, frequency_ref, re_ref, im_ref,
    skip_ref, table_ref, send_hbm, own_hbm, sr_ref, si_ref, terms_ref, raw_ref, wide_ref,
    signal_ref, own_ref, send_ref, rows_ref, pack_ref, sems, out_sems,
):
    loads = started(
        sems,
        (signal_hbm, signal_ref),
        (cot_hbm, own_ref.at[:, pl.ds(0, BLOCK)]),
        (mix_hbm, own_ref.at[:, pl.ds(BLOCK, LN)]),
    )
    picked = lax.broadcasted_iota(jnp.int32, table_ref.shape, 1) == step_ref[0]
    embed = jnp.sum(jnp.where(picked, table_ref[...], 0.0), 1, keepdims=True)
    wide_ref[0] = jnp.broadcast_to(embed, (CH, LN))
    wide_ref[1] = jnp.broadcast_to(as_column(skip_ref[...]), (CH, LN))
    pack_ref[...] = jnp.broadcast_to(embed, (CH, MODES))
    embed_lanes = packed_lanes(pack_ref)
    pack_ref[...] = jnp.broadcast_to(as_column(jnp.exp(size_ref[...])), (CH, MODES))
    raw = [packed_lanes(r) for r in (pack_ref, damping_ref, frequency_ref, re_ref, im_ref)]
    for k in range(5):
        raw_ref[k] = raw[k]
    terms = mode_terms(*raw)
    for k in range(4):
        terms_ref[k] = terms[k]
    decay, turn = terms[0], terms[1]
    doubles = doublings(decay, turn)
    loads[0].wait()
    for i in range(CK):
        rows_ref[pl.ds(i, CH, stride=CK), :] = signal_ref[:, i * LN : (i + 1) * LN].astype(F32)
    for c in range(CH):
        send_ref[c, :CK, :] = rows_ref[c * CK : (c + 1) * CK, :].astype(BF16)
    loads[1].wait()
    loads[2].wait()
    stores = started(
        out_sems,
        (send_ref.at[:, pl.ds(0, CK), :], send_hbm.at[:, pl.ds(0, CK), :]),
        (own_ref, own_hbm),
    )
    for g in range(GROUPS):
        x = rows_ref[g * LN : (g + 1) * LN, :].astype(BF16)
        fr, fi = falling(decay, turn, doubles, g)
        table = jnp.concatenate([fr, fi], 1)
        th, tl = split(table)
        pr, pi = gather_group(dot(x, th) + dot(x, tl))
        level = embed_lanes[g : g + 1]
        sr_ref[pl.ds(g, CK, stride=GROUPS), :] = pr + level * jnp.sum(fr, 0, keepdims=True)
        si_ref[pl.ds(g, CK, stride=GROUPS), :] = pi + level * jnp.sum(fi, 0, keepdims=True)
    zr, zi = power(decay, turn, float(LN))
    zero = jnp.zeros((GROUPS, LN), F32)
    hr, hi = scan_states(sr_ref, si_ref, zr, zi, zero, zero, range(CK), False)
    packed = packed_states(hr, hi)
    for d in range(RANKS):
        send_ref[d, CK:, :] = packed
    last = pltpu.make_async_copy(
        send_ref.at[:, pl.ds(CK, CK), :], send_hbm.at[:, pl.ds(CK, CK), :], out_sems.at[2]
    )
    last.start()
    for copy in stores + [last]:
        copy.wait()


def packed_states(hr, hi):
    high, low = split(jnp.concatenate([hr, hi], 0))
    return jnp.concatenate([high, low], 0)


def unpacked_states(packed):
    packed = packed.astype(F32)
    values = packed[: 2 * GROUPS] + packed[2 * GROUPS :]
    return values[:GROUPS], values[GROUPS:]


def first(step, signal, cotangent, mix_weight, sizes, params, skip, table):
    return pl.pallas_call(
        first_kernel,
        in_specs=[SMEM] + [ANY] * 3 + [VMEM] * 7,
        out_specs=[ANY] * 2 + [VMEM] * 5,
        out_shape=(
            jax.ShapeDtypeStruct((RANKS, SEND1, LN), BF16),
            jax.ShapeDtypeStruct((CH, BLOCK + LN), BF16),
            jax.ShapeDtypeStruct((CK * GROUPS, LN), F32),
            jax.ShapeDtypeStruct((CK * GROUPS, LN), F32),
            jax.ShapeDtypeStruct((4, GROUPS, LN), F32),
            jax.ShapeDtypeStruct((5, GROUPS, LN), F32),
            jax.ShapeDtypeStruct((2, CH, LN), F32),
        ),
        scratch_shapes=[
            pltpu.VMEM((CH, BLOCK), BF16),
            pltpu.VMEM((CH, BLOCK + LN), BF16),
            pltpu.VMEM((RANKS, SEND1, LN), BF16),
            pltpu.VMEM((CH * CK, LN), F32),
            pltpu.VMEM((CH, MODES), F32),
            pltpu.SemaphoreType.DMA((3,)),
            pltpu.SemaphoreType.DMA((3,)),
        ],
        compiler_params=PARAMS,
        name="block_states",
    )(step, signal, cotangent, mix_weight, sizes, *params, skip, table)


def far_power(decay, turn, blocks):
    size = jnp.exp(-decay * (BLOCK * blocks))
    angle = turn * (BLOCK * blocks)
    return size * jnp.cos(angle), size * jnp.sin(angle)


def within_kernel(x_hbm, terms_ref, wide_ref, out_ref, far_r, far_i, x_ref, sems):
    loads = started(sems, (x_hbm.at[:, pl.ds(0, CK), :], x_ref))
    terms = terms_ref[0], terms_ref[1], terms_ref[2], terms_ref[3]
    decay, turn = terms[0], terms[1]
    near = [far_power(decay, turn, float(b)) for b in range(4)]
    for a in range(RANKS // 4):
        base = far_power(decay, turn, float(4 * a))
        for b in range(4):
            pr, pi = cmul(base[0], base[1], near[b][0], near[b][1]) if a and b else (
                base if a else near[b]
            )
            far_r[4 * a + b] = pr
            far_i[4 * a + b] = pi
    doubles = doublings(decay, turn)
    loads[0].wait()
    for g in range(GROUPS):
        taps = group_taps(terms, rising(decay, turn, doubles, g), g)
        for k in range(LANE_CH):
            c = g * LANE_CH + k
            matrix = toeplitz(taps[k : k + 1])
            high, low = split(matrix)
            x = x_ref[c]
            level = wide_ref[0, c : c + 1, :]
            out_ref[c * CK : (c + 1) * CK, :] = (
                dot(x, high) + dot(x, low) + level * jnp.sum(matrix, 0, keepdims=True)
            )


def within(send, terms, wide):
    return pl.pallas_call(
        within_kernel,
        in_specs=[ANY, VMEM, VMEM],
        out_shape=(
            jax.ShapeDtypeStruct((CH * CK, LN), F32),
            jax.ShapeDtypeStruct((RANKS, GROUPS, LN), F32),
            jax.ShapeDtypeStruct((RANKS, GROUPS, LN), F32),
        ),
        scratch_shapes=[pltpu.VMEM((CH, CK, LN), BF16), pltpu.SemaphoreType.DMA((1,))],
        compiler_params=PARAMS,
        name="within_chunks",
    )(send, terms, wide)


def mixed_back(group, parts, act_ref):
    mine = lax.broadcasted_iota(jnp.int32, (CH, LN), 1) == group * CH + lax.broadcasted_iota(
        jnp.int32, (CH, LN), 0
    )
    weights = jnp.concatenate([c[:, BLOCK:] for c in parts], 0)
    weights = dot(mine.astype(BF16), weights, NT).astype(BF16)
    for i in range(CK):
        cols = slice(i * LN, (i + 1) * LN)
        cot = jnp.concatenate([c[:, cols] for c in parts], 0)
        act_ref[pl.ds(i, CH, stride=CK), :] = dot(weights, cot)


def gelu_both(x):
    scale = np.float32(np.sqrt(2.0 / np.pi))
    square = x * x
    t = jnp.tanh(scale * (x + 0.044715 * (square * x)))
    half = 0.5 * (1.0 + t)
    slope = half + 0.5 * x * (1.0 - t * t) * (scale * (1.0 + (3.0 * 0.044715) * square))
    return x * half, slope


def entering(states, table_r, table_i, distance):
    hr = jnp.zeros((GROUPS, LN), F32)
    hi = jnp.zeros((GROUPS, LN), F32)
    for d in range(RANKS):
        steps = distance(d)
        sr, si = states(d)
        at = jnp.maximum(steps, 0)
        nr, ni = cmul(table_r[at], table_i[at], sr, si)
        hr = jnp.where(steps >= 0, hr + nr, hr)
        hi = jnp.where(steps >= 0, hi + ni, hi)
    return hr, hi


def second_kernel(
    me_ref, group_ref, c0h, c1h, c2h, c3h, out_hbm, got_hbm, x_hbm, terms_ref, wide_ref, far_r,
    far_i, sr_in, si_in, send_hbm, grad_hbm, mix_ref, sr_ref, si_ref,
    c0, c1, c2, c3, flat_ref, out_ref, got_ref, x_ref, act_ref, activation_ref, send_ref, grad_ref, sems, out_sems,
):
    loads = started(
        sems,
        (got_hbm.at[:, pl.ds(CK, CK), :], got_ref),
        (c0h, c0), (c1h, c1), (c2h, c2), (c3h, c3),
        (x_hbm.at[:, pl.ds(0, CK), :], x_ref),
        (out_hbm, out_ref),
    )
    me = me_ref[0]
    terms = terms_ref[0], terms_ref[1], terms_ref[2], terms_ref[3]
    decay, turn = terms[0], terms[1]
    doubles = doublings(decay, turn)
    zr, zi = power(decay, turn, float(LN))
    one_r, one_i = power(decay, turn, 1.0)
    ur, ui = cmul(2.0 * terms[2], 2.0 * terms[3], one_r, one_i)
    sr_ref[...] = sr_in[...]
    si_ref[...] = si_in[...]
    loads[0].wait()
    start = entering(lambda d: unpacked_states(got_ref[d]), far_r, far_i, lambda d: me - 1 - d)
    scan_states(sr_ref, si_ref, zr, zi, start[0], start[1], range(CK), True)
    for copy in loads[1:5]:
        copy.wait()
    mixed_back(group_ref[0], (c0, c1, c2, c3), act_ref)
    for copy in loads[5:]:
        copy.wait()
    stores = []
    for g in range(GROUPS):
        every = pl.ds(g, CK, stride=GROUPS)
        er, ei = rising(decay, turn, doubles, g)
        wr, wi = cmul(er, ei, ur[g : g + 1], ui[g : g + 1])
        inter = spread_group(sr_ref[every, :], si_ref[every, :], jnp.concatenate([wr, wi], 1))
        left = []
        for k in range(LANE_CH):
            c = g * LANE_CH + k
            rows = slice(c * CK, (c + 1) * CK)
            x = x_ref[c].astype(F32) + wide_ref[0, c : c + 1, :]
            mixed = out_ref[rows, :] + inter[k * CK : (k + 1) * CK] + wide_ref[1, c : c + 1, :] * x
            act, slope = gelu_both(mixed)
            activation_ref[rows, :] = act
            grad = act_ref[rows, :] * slope
            grad_ref[rows, :] = grad
            send_ref[c, :CK, :] = grad.astype(BF16)
            left.append(grad)
        stores.append(
            pltpu.make_async_copy(
                send_ref.at[pl.ds(g * LANE_CH, LANE_CH), pl.ds(0, CK), :],
                send_hbm.at[pl.ds(g * LANE_CH, LANE_CH), pl.ds(0, CK), :],
                out_sems.at[g],
            )
        )
        stores[-1].start()
        products = dot3(split(jnp.concatenate(left, 0)), split(jnp.concatenate([er, ei], 1)))
        pr, pi = gather_group(products)
        sr_ref[every, :] = pr
        si_ref[every, :] = pi
    zero = jnp.zeros((GROUPS, LN), F32)
    hr, hi = scan_states(sr_ref, si_ref, zr, zi, zero, zero, range(CK - 1, -1, -1), False)
    packed = packed_states(hr, hi)
    for d in range(RANKS):
        send_ref[d, CK:, :] = packed
    stores.append(
        pltpu.make_async_copy(
            send_ref.at[:, pl.ds(CK, CK), :], send_hbm.at[:, pl.ds(CK, CK), :],
            out_sems.at[GROUPS],
        )
    )
    stores[-1].start()
    stores.append(pltpu.make_async_copy(grad_ref, grad_hbm, out_sems.at[GROUPS + 1]))
    stores[-1].start()
    for i in range(CK):
        flat_ref[:, i * LN : (i + 1) * LN] = activation_ref[pl.ds(i, CH, stride=CK), :].astype(BF16)
    flat = flat_ref[...]
    mix_ref[...] = jnp.concatenate([dot(flat, c[:, :BLOCK], NT) for c in (c0, c1, c2, c3)], 1)
    for copy in stores:
        copy.wait()


def second(me, group, parts, out, got, send, terms, wide, far, sr, si):
    return pl.pallas_call(
        second_kernel,
        in_specs=[SMEM] * 2 + [ANY] * 7 + [VMEM] * 6,
        out_specs=[ANY] * 2 + [VMEM] * 3,
        out_shape=(
            jax.ShapeDtypeStruct((RANKS, SEND2, LN), BF16),
            jax.ShapeDtypeStruct((CH * CK, LN), F32),
            jax.ShapeDtypeStruct((CH, LN), F32),
            jax.ShapeDtypeStruct((CK * GROUPS, LN), F32),
            jax.ShapeDtypeStruct((CK * GROUPS, LN), F32),
        ),
        scratch_shapes=[pltpu.VMEM((CH, BLOCK + LN), BF16)] * 4
        + [
            pltpu.VMEM((CH, BLOCK), BF16),
            pltpu.VMEM((CH * CK, LN), F32),
            pltpu.VMEM((RANKS, CK, LN), BF16),
            pltpu.VMEM((CH, CK, LN), BF16),
            pltpu.VMEM((CH * CK, LN), F32),
            pltpu.VMEM((CH * CK, LN), F32),
            pltpu.VMEM((RANKS, SEND2, LN), BF16),
            pltpu.VMEM((CH * CK, LN), F32),
            pltpu.SemaphoreType.DMA((7,)),
            pltpu.SemaphoreType.DMA((GROUPS + 2,)),
        ],
        compiler_params=PARAMS,
        name="activation_and_states",
    )(me, group, *parts, out, got, send, terms, wide, far[0], far[1], sr, si)


def signal_kernel(
    me_ref, got_hbm, send_hbm, cot_hbm, after_hbm, terms_ref, wide_ref, far_r, far_i, sr_in, si_in,
    out_ref, sr_ref, si_ref, rows_ref, got_ref, send_ref, cot_ref, sems,
):
    loads = started(
        sems,
        (got_hbm.at[:, pl.ds(CK, CK), :], got_ref),
        (send_hbm, send_ref),
        (cot_hbm, cot_ref),
    )
    me = me_ref[0]
    terms = terms_ref[0], terms_ref[1], terms_ref[2], terms_ref[3]
    decay, turn = terms[0], terms[1]
    doubles = doublings(decay, turn)
    zr, zi = power(decay, turn, float(LN))
    one_r, one_i = power(decay, turn, 1.0)
    ur, ui = cmul(2.0 * terms[2], 2.0 * terms[3], one_r, one_i)

    sr_ref[...] = sr_in[...]
    si_ref[...] = si_in[...]
    loads[0].wait()
    start = entering(lambda d: unpacked_states(got_ref[d]), far_r, far_i, lambda d: d - me - 1)
    scan_states(sr_ref, si_ref, zr, zi, start[0], start[1], range(CK - 1, -1, -1), True)
    for copy in loads[1:]:
        copy.wait()
    for g in range(GROUPS):
        every = pl.ds(g, CK, stride=GROUPS)
        fr, fi = falling(decay, turn, doubles, g)
        wr, wi = cmul(fr, fi, ur[g : g + 1], ui[g : g + 1])
        inter = spread_group(sr_ref[every, :], si_ref[every, :], jnp.concatenate([wr, wi], 1))
        taps = group_taps(terms, rising(decay, turn, doubles, g), g)
        for k in range(LANE_CH):
            c = g * LANE_CH + k
            grad = send_ref[c * CK : (c + 1) * CK, :]
            rows_ref[c * CK : (c + 1) * CK, :] = (
                dot3(split(grad), split(toeplitz(taps[k : k + 1])), NT)
                + inter[k * CK : (k + 1) * CK]
                + wide_ref[1, c : c + 1, :] * grad
            )
    for i in range(CK):
        cols = slice(i * LN, (i + 1) * LN)
        out_ref[:, cols] = (
            cot_ref[:, cols].astype(F32) + rows_ref[pl.ds(i, CH, stride=CK), :]
        ).astype(BF16)


def signal_grad(me, got, send, terms, wide, far, sr, si, cotangent, after):
    return pl.pallas_call(
        signal_kernel,
        in_specs=[SMEM] + [ANY] * 4 + [VMEM] * 6,
        out_shape=jax.ShapeDtypeStruct((CH, BLOCK), BF16),
        scratch_shapes=[
            pltpu.VMEM((CK * GROUPS, LN), F32),
            pltpu.VMEM((CK * GROUPS, LN), F32),
            pltpu.VMEM((CH * CK, LN), F32),
            pltpu.VMEM((RANKS, CK, LN), BF16),
            pltpu.VMEM((CH * CK, LN), F32),
            pltpu.VMEM((CH, BLOCK), BF16),
            pltpu.SemaphoreType.DMA((3,)),
        ],
        compiler_params=PARAMS,
        name="signal_gradient",
    )(me, got, send, cotangent, after, terms, wide, far[0], far[1], sr, si)


def dft_tables():
    full_len = RANKS * BLOCK
    row = np.arange(ROWS)
    time_row = (row % RANKS) * (BLOCK // COLS) + row // RANKS
    first_ids = np.arange(ROWS)
    column = np.arange(COLS)
    angle1 = (
        2.0 * np.pi * (((4 * first_ids[:, None] + 1) * time_row[None, :]) % (4 * ROWS)) / (4 * ROWS)
    )
    angle_t = 2.0 * np.pi * ((4 * first_ids[:, None] + 1) * column[None, :]) / (4 * full_len)
    lane = np.arange(LN)
    angle2 = 2.0 * np.pi * ((lane[:, None] * lane[None, :]) % LN) / LN
    angle_p = 2.0 * np.pi * np.arange(PER)[:, None] * lane[None, :] / COLS

    def halves(values):
        values = values.astype(np.float32)
        high = values.astype(BF16)
        return high, (values - high.astype(np.float32)).astype(BF16)

    stage1 = np.concatenate([np.cos(angle1), -np.sin(angle1)], 0)
    cos2, sin2 = np.cos(angle2), np.sin(angle2)
    stage2 = np.concatenate(
        [np.concatenate([cos2, -sin2], 1), np.concatenate([sin2, cos2], 1)], 0
    )
    twiddle = np.stack([np.cos(angle_t), np.sin(angle_t)]).astype(np.float32)
    steps = np.concatenate([np.cos(angle_p), np.sin(angle_p)], 0).astype(np.float32)
    return halves(stage1), halves(stage1.T / full_len), halves(stage2), twiddle, steps


def gather_rows(ref, stride, base):
    return jnp.concatenate(
        [
            jnp.concatenate(
                [
                    ref[pl.ds(base + piece * PER + q, RANKS, stride=stride), :]
                    for q in range(PER)
                ],
                1,
            )
            for piece in range(BLOCK // COLS)
        ],
        0,
    )


def butterfly(parts, sign):
    (r0, i0), (r1, i1), (r2, i2), (r3, i3) = parts
    sr, si, dr, di = r0 + r2, i0 + i2, r0 - r2, i0 - i2
    tr, ti, er, ei = r1 + r3, i1 + i3, r1 - r3, i1 - i3
    if sign > 0:
        er, ei = -er, -ei
    return (sr + tr, si + ti), (dr + ei, di - er), (sr - tr, si - ti), (dr - ei, di + er)


def forward_dft(rows, exact, d1h, d1l, d2h, d2l, twiddle, steps, wait1, wait2):
    xh, xl = split(rows)
    wait1()
    a = dot(d1h[...], xh) + dot(d1l[...], xh)
    if not exact:
        a = a + dot(d1h[...], xl)
    wait2()
    parts = []
    for q in range(PER):
        cols = slice(q * LN, (q + 1) * LN)
        parts.append(cmul(a[:ROWS, cols], a[ROWS:, cols], twiddle[0, :, cols], -twiddle[1, :, cols]))
    out = []
    for p, (ur, ui) in enumerate(butterfly(parts, -1)):
        if p:
            ur, ui = cmul(ur, ui, steps[p : p + 1, :], -steps[PER + p : PER + p + 1, :])
        out.append(jnp.concatenate([ur, ui], 1))
    return dot3(split(jnp.concatenate(out, 0)), (d2h[...], d2l[...]))


def inverse_dft(spec, d1th, d1tl, d2h, d2l, twiddle, steps):
    v = dot3(split(spec), (d2h[...], d2l[...]), NT)
    parts = []
    for p in range(PER):
        vr, vi = v[p * ROWS : (p + 1) * ROWS, :LN], v[p * ROWS : (p + 1) * ROWS, LN:]
        if p:
            vr, vi = cmul(vr, vi, steps[p : p + 1, :], steps[PER + p : PER + p + 1, :])
        parts.append((vr, vi))
    real, imag = [], []
    for q, (br, bi) in enumerate(butterfly(parts, 1)):
        cols = slice(q * LN, (q + 1) * LN)
        br, bi = cmul(br, bi, twiddle[0, :, cols], twiddle[1, :, cols])
        real.append(br)
        imag.append(bi)
    bh, bl = split(
        jnp.concatenate([jnp.concatenate(real, 1), jnp.concatenate(imag, 1)], 0)
    )
    return dot(d1th[...], bh) + dot(d1th[...], bl) + dot(d1tl[...], bh)


def lane_block(row):
    return lax.broadcasted_iota(jnp.int32, row.shape, 1) // MODES


def repeated(row):
    row = jnp.where(lane_block(row) == 0, row, 0.0)
    total = row
    for m in range(1, LANE_CH):
        total = total + pltpu.roll(row, m * MODES, 1)
    return total


def by_block(rows):
    result = rows[0]
    for m in range(1, LANE_CH):
        result = jnp.where(lane_block(result) == m, rows[m], result)
    return result


def waiting(copies):
    def wait():
        for copy in copies:
            copy.wait()

    return wait


def spectrum_kernel(
    me_ref, got_hbm, d1h_hbm, d1l_hbm, twiddle_hbm, d2h_hbm, d2l_hbm, after_hbm,
    steps_ref, wide_ref, raw_ref, spec_ref, column_ref, turn_ref, pull_ref,
    got_ref, d1h, d1l, twiddle, d2h, d2l, rows_ref, sems,
):
    loads = started(
        sems,
        (got_hbm.at[:, pl.ds(0, CK), :], got_ref),
        (d1h_hbm, d1h), (d1l_hbm, d1l), (twiddle_hbm, twiddle), (d2h_hbm, d2h), (d2l_hbm, d2l),
    )
    me = me_ref[0]
    embed = wide_ref[0, pl.ds(me, 1), :]
    loads[0].wait()
    for d in range(RANKS):
        rows_ref[d * CK : (d + 1) * CK, :] = got_ref[d].astype(F32) + embed
    rows = gather_rows(rows_ref, CK, 0)
    spec_ref[...] = forward_dft(
        rows, False, d1h, d1l, d2h, d2l, twiddle, steps_ref, waiting(loads[1:3]),
        waiting(loads[3:6]),
    )

    at, shift = me // LANE_CH, (me % LANE_CH) * MODES

    def own(k):
        row = jnp.broadcast_to(raw_ref[k, pl.ds(at, 1), :], (8, LN))
        return repeated(pltpu.roll(row, (LN - shift) % LN, 1)[:1])

    raw = [own(k) for k in range(5)]
    (d, th, mr, mi), pull = jax.vjp(mode_terms, *raw)
    zero = jnp.zeros((1, LN), F32)
    pulled = [
        pull((zero, zero, zero + 2.0, zero)),
        pull((zero, zero, zero, zero - 2.0)),
        pull((-2.0 * mr, -2.0 * mi, zero, zero)),
        pull((2.0 * mi, -2.0 * mr, zero, zero)),
    ]
    inverse = 1.0 / (raw[1] * raw[1] + raw[2] * raw[2])
    qr, qi = cmul(raw[3], raw[4], raw[1] * inverse, raw[2] * inverse)
    one_r, one_i = power(d, th, 1.0)
    er, ei = cmul(qr, qi, one_r, one_i)
    first_lanes = lane_block(zero) == 0
    pull_ref[...] = jnp.concatenate(
        [by_block(p[1:]) for p in pulled]
        + [jnp.where(first_lanes, p[0] * raw[0], 0.0) for p in pulled]
        + [jnp.where(first_lanes, v, 0.0) for v in (2.0 * qr, -2.0 * er, 2.0 * ei)]
        + [wide_ref[1, pl.ds(me, 1), :]]
        + [jnp.zeros((4, LN), F32)],
        0,
    )
    steps = lax.broadcasted_iota(jnp.int32, (8, LN), 0).astype(F32)
    cr, ci = power(d, th, steps)
    for k in (8, 16, 32, 64, 128, 256):
        zr, zi = far_power(d, th, float(k) / BLOCK)
        nr, ni = cmul(cr, ci, zr, zi)
        cr, ci = jnp.concatenate([cr, nr], 0), jnp.concatenate([ci, ni], 0)
    col = lax.broadcasted_iota(jnp.int32, (COLS, LN), 0).astype(F32)
    block = lane_block(col)
    table = jnp.where(block % 2 == 0, cr, ci)
    column_ref[...] = jnp.where(block < 2, table, table * col)
    ranks = lax.broadcasted_iota(jnp.int32, (RANKS, LN), 0).astype(F32)
    br, bi = far_power(d, th, ranks)
    for piece in range(BLOCK // COLS):
        zr, zi = far_power(d, th, float(piece * COLS) / BLOCK)
        nr, ni = cmul(br, bi, zr, zi) if piece else (br, bi)
        turn_ref[0, piece * RANKS : (piece + 1) * RANKS, :] = nr
        turn_ref[1, piece * RANKS : (piece + 1) * RANKS, :] = ni


def spectrum(me, got, after, wide, raw, tables):
    (d1h, d1l), unused, (d2h, d2l), twiddle, steps = tables
    return pl.pallas_call(
        spectrum_kernel,
        in_specs=[SMEM] + [ANY] * 7 + [VMEM] * 3,
        out_shape=(
            jax.ShapeDtypeStruct((PER * ROWS, 2 * LN), F32),
            jax.ShapeDtypeStruct((COLS, LN), F32),
            jax.ShapeDtypeStruct((2, ROWS, LN), F32),
            jax.ShapeDtypeStruct((16, LN), F32),
        ),
        scratch_shapes=[
            pltpu.VMEM((RANKS, CK, LN), BF16),
            pltpu.VMEM((2 * ROWS, ROWS), BF16),
            pltpu.VMEM((2 * ROWS, ROWS), BF16),
            pltpu.VMEM((2, ROWS, COLS), F32),
            pltpu.VMEM((2 * LN, 2 * LN), BF16),
            pltpu.VMEM((2 * LN, 2 * LN), BF16),
            pltpu.VMEM((RANKS * CK, LN), F32),
            pltpu.SemaphoreType.DMA((6,)),
        ],
        compiler_params=PARAMS,
        name="input_spectrum",
    )(me, got, d1h, d1l, twiddle, d2h, d2l, after, steps, wide, raw)


def correlate_kernel(
    got_hbm, d1h_hbm, d1l_hbm, twiddle_hbm, d2h_hbm, d2l_hbm, spec_hbm, d1th_hbm, d1tl_hbm,
    column_hbm, turn_hbm, steps_ref, pull_ref, m0, m1, m2, m3, send_hbm, after_ref,
    got_ref, d1h, d1l, twiddle, d2h, d2l, spec_ref, d1th, d1tl, column_ref, turn_ref,
    rows_ref, send_ref, sems, out_sems,
):
    loads = started(
        sems,
        (got_hbm.at[:, pl.ds(0, CK), :], got_ref),
        (d1h_hbm, d1h), (d1l_hbm, d1l), (twiddle_hbm, twiddle), (d2h_hbm, d2h), (d2l_hbm, d2l),
        (spec_hbm, spec_ref), (d1th_hbm, d1th), (d1tl_hbm, d1tl), (column_hbm, column_ref),
        (turn_hbm, turn_ref),
    )
    mixes = by_block([m[...] for m in (m0, m1, m2, m3)]).astype(BF16)
    for d in range(RANKS):
        send_ref[d, CK : 2 * CK, :] = mixes
    middle = pl.ds(CK, CK)
    stores = started(out_sems, (send_ref.at[:, middle, :], send_hbm.at[:, middle, :]))
    loads[0].wait()
    for d in range(RANKS):
        rows_ref[d * CK : (d + 1) * CK, :] = got_ref[d].astype(F32)
    g_rows = gather_rows(rows_ref, CK, 0)
    g_spec = forward_dft(
        g_rows, True, d1h, d1l, d2h, d2l, twiddle, steps_ref, waiting(loads[1:3]),
        waiting(loads[3:6]),
    )
    waiting(loads[6:7])()
    gr, gi = g_spec[:, :LN], g_spec[:, LN:]
    xr, xi = spec_ref[:, :LN], spec_ref[:, LN:]
    both = jnp.concatenate([xr * gr + xi * gi, xr * gi - xi * gr], 1)
    waiting(loads[7:])()
    kernel_rows = inverse_dft(both, d1th, d1tl, d2h, d2l, twiddle, steps_ref)
    for piece in range(BLOCK // COLS):
        for q in range(PER):
            rows_ref[pl.ds(piece * PER + q, RANKS, stride=CK), :] = kernel_rows[
                piece * RANKS : (piece + 1) * RANKS, q * LN : (q + 1) * LN
            ]
    for d in range(RANKS):
        send_ref[d, :CK, :] = rows_ref[d * CK : (d + 1) * CK, :].astype(BF16)
    stores.append(
        pltpu.make_async_copy(
            send_ref.at[:, pl.ds(0, CK), :], send_hbm.at[:, pl.ds(0, CK), :], out_sems.at[1]
        )
    )
    stores[-1].start()
    both = dot3(split(jnp.concatenate([kernel_rows, g_rows], 0)), split(column_ref[...]))
    inner = both[:ROWS]
    rr, ri = turn_ref[0], turn_ref[1]
    ids = lax.broadcasted_iota(jnp.int32, (ROWS, LN), 0)
    starts = ((ids % RANKS) * BLOCK + (ids // RANKS) * COLS).astype(F32)

    def total(values):
        return jnp.sum(values, 0, keepdims=True)

    by_r, by_i = rr * inner, ri * inner
    u, v = total(by_r), total(by_i)
    su, sv = total(starts * by_r), total(starts * by_i)
    gu, gv = total(rr * both[ROWS:]), total(ri * both[ROWS:])

    def block(row, k):
        moved = pltpu.roll(row, (LN - k * MODES) % LN, 1) if k else row
        return jnp.where(lane_block(row) == 0, moved, 0.0)

    cos_sum = block(u, 0) - block(v, 1)
    sin_sum = block(u, 1) + block(v, 0)
    cos_moment = block(u, 2) - block(v, 3) + block(su, 0) - block(sv, 1)
    sin_moment = block(u, 3) + block(v, 2) + block(su, 1) + block(sv, 0)
    grads = jnp.zeros((1, LN), F32)
    step = jnp.zeros((1, LN), F32)
    for k, value in enumerate((cos_sum, sin_sum, cos_moment, sin_moment)):
        grads = grads + pull_ref[k : k + 1, :] * repeated(value)
        step = step + pull_ref[4 + k : 5 + k, :] * value
    step_sum = jnp.sum(step, 1, keepdims=True)
    skip_sum = kernel_rows[0:1, 0:1]
    g_sum = jnp.sum(total(g_rows), 1, keepdims=True)
    back_sum = jnp.sum(
        pull_ref[8:9, :] * g_sum
        + pull_ref[9:10, :] * (block(gu, 0) - block(gv, 1))
        + pull_ref[10:11, :] * (block(gu, 1) + block(gv, 0)),
        1,
        keepdims=True,
    )
    lanes = lax.broadcasted_iota(jnp.int32, (1, LN), 1)
    scalars = (
        jnp.where(lanes == 0, step_sum, 0.0)
        + jnp.where(lanes == 1, skip_sum, 0.0)
        + jnp.where(lanes == 2, back_sum + pull_ref[11:12, :] * g_sum, 0.0)
    )
    small = jnp.concatenate([grads, scalars, jnp.zeros((6, LN), F32)], 0)
    after_ref[...] = small
    high, low = split(jnp.concatenate([small, small], 0))
    upper = lax.broadcasted_iota(jnp.int32, (16, LN), 0) < 8
    packed = jnp.where(upper, high.astype(F32), low.astype(F32)).astype(BF16)
    for d in range(RANKS):
        send_ref[d, 2 * CK :, :] = packed
    stores.append(
        pltpu.make_async_copy(
            send_ref.at[:, pl.ds(2 * CK, 16), :], send_hbm.at[:, pl.ds(2 * CK, 16), :],
            out_sems.at[2],
        )
    )
    stores[-1].start()
    for copy in stores:
        copy.wait()


def correlate(got, spec, tables, column, turns, pull, mixes):
    (d1h, d1l), (d1th, d1tl), (d2h, d2l), twiddle, steps = tables
    return pl.pallas_call(
        correlate_kernel,
        in_specs=[ANY] * 11 + [VMEM] * 6,
        out_specs=[ANY, VMEM],
        out_shape=(
            jax.ShapeDtypeStruct((RANKS, SEND3, LN), BF16),
            jax.ShapeDtypeStruct((8, LN), F32),
        ),
        scratch_shapes=[
            pltpu.VMEM((RANKS, CK, LN), BF16),
            pltpu.VMEM((2 * ROWS, ROWS), BF16),
            pltpu.VMEM((2 * ROWS, ROWS), BF16),
            pltpu.VMEM((2, ROWS, COLS), F32),
            pltpu.VMEM((2 * LN, 2 * LN), BF16),
            pltpu.VMEM((2 * LN, 2 * LN), BF16),
            pltpu.VMEM((PER * ROWS, 2 * LN), F32),
            pltpu.VMEM((ROWS, 2 * ROWS), BF16),
            pltpu.VMEM((ROWS, 2 * ROWS), BF16),
            pltpu.VMEM((COLS, LN), F32),
            pltpu.VMEM((2, ROWS, LN), F32),
            pltpu.VMEM((RANKS * CK, LN), F32),
            pltpu.VMEM((RANKS, SEND3, LN), BF16),
            pltpu.SemaphoreType.DMA((11,)),
            pltpu.SemaphoreType.DMA((3,)),
        ],
        compiler_params=PARAMS,
        name="correlation",
    )(got, d1h, d1l, twiddle, d2h, d2l, spec, d1th, d1tl, column, turns, steps, pull, *mixes)


def outputs_kernel(
    step_ref, group_ref, got_ref, kernel_ref, damping_ref, frequency_ref, re_ref, im_ref,
    size_ref, skip_ref, mix_ref, table_ref, rows_ref, turned_ref,
):
    mixes = jnp.zeros((CH, LN), F32)
    for c in range(CH):
        rows_ref[c * CK : (c + 1) * CK, :] = got_ref[c, :CK, :].astype(F32)
        mixes = mixes + got_ref[c, CK : 2 * CK, :].astype(F32)
    for i in range(CK):
        kernel_ref[:, i * LN : (i + 1) * LN] = rows_ref[pl.ds(i, CH, stride=CK), :]
    for c in range(CH):
        small = got_ref[c, 2 * CK :, :].astype(F32)
        rows_ref[c * 8 : (c + 1) * 8, :] = small[:8] + small[8:]
    grads = rows_ref[pl.ds(0, CH, stride=8), :]
    for k, ref in enumerate((damping_ref, frequency_ref, re_ref, im_ref)):
        ref[...] = grads[:, k * MODES : (k + 1) * MODES]
    scalars = rows_ref[pl.ds(1, CH, stride=8), :]
    turned = jnp.concatenate([scalars, jnp.zeros((LN - CH, LN), F32)], 0).T
    size_ref[...] = turned[0:1, :CH]
    skip_ref[...] = turned[1:2, :CH]
    picked = lax.broadcasted_iota(jnp.int32, table_ref.shape, 1) == step_ref[0]
    table_ref[...] = jnp.where(picked, scalars[:, 2:3], 0.0)
    turned_ref[...] = jnp.concatenate([mixes, jnp.zeros((LN - CH, LN), F32)], 0).T
    mix_ref[...] = jnp.concatenate(
        [
            turned_ref[pl.ds(pl.multiple_of((group_ref[0] ^ c) * CH, CH), CH), :][:, :CH]
            for c in range(LN // CH)
        ],
        1,
    )


def outputs(step, group, got, table_len):
    wide = jax.ShapeDtypeStruct((CH, MODES), F32)
    row = jax.ShapeDtypeStruct((1, CH), F32)
    return pl.pallas_call(
        outputs_kernel,
        in_specs=[SMEM, SMEM, VMEM],
        out_shape=(
            jax.ShapeDtypeStruct((CH, BLOCK), F32),
            wide, wide, wide, wide, row, row,
            jax.ShapeDtypeStruct((CH, LN), F32),
            jax.ShapeDtypeStruct((CH, table_len), F32),
        ),
        scratch_shapes=[pltpu.VMEM((CH * CK, LN), F32), pltpu.VMEM((LN, LN), F32)],
        compiler_params=PARAMS,
        name="outputs",
    )(step, group, got)


def exchange(values):
    return lax.all_to_all(values, "tm", split_axis=0, concat_axis=0, tiled=True)


def shards(
    signal,
    cotangent,
    log_step,
    damping,
    frequency,
    coef_re,
    coef_im,
    skip_gain,
    mix_weight,
    embed_table,
    diffusion_step,
):
    me = lax.axis_index("tm").reshape(1)
    group = lax.axis_index("chan").reshape(1)
    tables = dft_tables()

    def swap(values, mask):
        return lax.ppermute(values, "chan", [(i, i ^ mask) for i in range(4)])

    send1, own, sr, si, terms, raw, wide = first(
        diffusion_step, signal, cotangent, mix_weight, log_step[None],
        (damping, frequency, coef_re, coef_im), skip_gain[None], embed_table.T,
    )
    got1 = exchange(send1)
    own, across = lax.optimization_barrier((own, swap(own, 2)))
    parts = (own, swap(own, 1), across, swap(across, 1))
    out, far_r, far_i = within(send1, terms, wide)
    far = (far_r, far_i)
    send2, grad, mix, br, bi = second(me, group, parts, out, got1, send1, terms, wide, far, sr, si)
    got2 = exchange(send2)
    mixes = [mix] + [swap(mix, m) for m in range(1, 4)]
    spec, column, turns, pull = spectrum(me, got1, mix, wide, raw, tables)
    send3, after = correlate(got2, spec, tables, column, turns, pull, mixes)
    got3 = exchange(send3)
    grad_signal = signal_grad(me, got2, grad, terms, wide, far, br, bi, cotangent, after)
    kernel, g_damping, g_frequency, g_re, g_im, g_size, g_skip, g_mix, g_table = outputs(
        diffusion_step, group, got3, embed_table.shape[0]
    )
    return (
        grad_signal,
        kernel,
        g_size[0],
        g_damping,
        g_frequency,
        g_re,
        g_im,
        g_skip[0],
        g_mix,
        g_table.T,
    )


def solution(mesh):
    placed = (
        P("chan", "tm"),
        P("chan", "tm"),
        P("chan"),
        P("chan", None),
        P("chan", None),
        P("chan", None),
        P("chan", None),
        P("chan"),
        P("chan", None),
        P(None, "chan"),
        P(),
    )
    return jax.shard_map(
        shards,
        mesh=mesh,
        in_specs=placed,
        out_specs=(
            P("chan", "tm"),
            P("chan", "tm"),
            P("chan"),
            P("chan", None),
            P("chan", None),
            P("chan", None),
            P("chan", None),
            P("chan"),
            P("chan", None),
            P(None, "chan"),
        ),
        check_vma=False,
    )
```

time: 118 us -> 87.4 us (0.74)
  local copies, waits for them, and re-layouts: 29.6 us -> 2.61 us
  Pallas kernels: 27.5 us -> 39.1 us
  other arithmetic: 8.93 us -> 0 us
  starting transfers between devices: 29 us -> 24.7 us
    unnamed x78 -> x22, local copies, waits for them, and re-layouts: 22.9 us -> 2.61 us
    pallas_call x7, Pallas kernels: 27.5 us -> 39.1 us  [the longest x1 8.27 us: correlate(): pl.pallas_call(correlate_kernel, in_specs=[ANY] * 11 + [VMEM] * 6, out_sp...]
    mul x6 -> x0, other arithmetic: 5.02 us -> none  [the longest x2 2.41 us: mode_powers(): return (size * jnp.cos(turned), size * jnp.sin(turned))]
    all_to_all x3, starting transfers between devices: 25.1 us -> 20.5 us  [exchange(): return lax.all_to_all(values, 'tm', split_axis=0, concat_axis=0, tiled=True)]
    concatenate x5 -> x0, other arithmetic: 1.9 us -> none  [the longest x1 0.98 us: shards(): column = jnp.concatenate([cr, ci, cr * col, ci * col], 1)]
    dynamic_slice x8 -> x0, local copies, waits for them, and re-layouts: 1.7 us -> none  [the longest x2 1.17 us: mine(): return lax.dynamic_slice_in_dim(values, me, 1, 0)]
    slice x5 -> x0, local copies, waits for them, and re-layouts: 1.6 us -> none  [the longest x1 0.7 us: shards(): scalars[:, 1]]
  transfers between devices with their start and end apart: 9 -> 9, of which waited for: 3 -> 3; matrix products, arithmetic and copies ran while one was open for 9% -> 0% of each run, Pallas kernels for 17% -> 20%
where the time goes in v1:
time: 87.4 us; the launch traced here: 86.4 us
  Pallas kernels  39.1 us (45%)
  starting transfers between devices  24.7 us (28%)
  waiting for transfers between devices  18.5 us (21%)
  local copies, waits for them, and re-layouts  2.61 us (3%)
  between operations  1.5 us (2%)
    all_to_all x3, starting transfers between devices, exchange(): return lax.all_to_all(values, 'tm', split_axis=0, concat_axis=0, tiled=True)  20.5 us
    all_to_all x3, waiting for transfers between devices, exchange(): return lax.all_to_all(values, 'tm', split_axis=0, concat_axis=0, tiled=True)  18.5 us
    pallas_call x1, Pallas kernels, correlate(): pl.pallas_call(correlate_kernel, in_specs=[ANY] * 11 + [VMEM] * 6, out_sp...  8.27 us
    pallas_call x1, Pallas kernels, signal_grad(): pl.pallas_call(signal_kernel, in_specs=[SMEM] + [ANY] * 4 + [VMEM] * 6, o...  6.99 us
    pallas_call x1, Pallas kernels, second(): pl.pallas_call(second_kernel, in_specs=[SMEM] * 2 + [ANY] * 7 + [VMEM] *...  6.69 us
    pallas_call x1, Pallas kernels, spectrum(): pl.pallas_call(spectrum_kernel, in_specs=[SMEM] + [ANY] * 7 + [VMEM] * 3,...  5.13 us
    pallas_call x1, Pallas kernels, within(): pl.pallas_call(within_kernel, in_specs=[ANY, VMEM, VMEM], out_shape=(jax....  5.1 us
    pallas_call x1, Pallas kernels, first(): pl.pallas_call(first_kernel, in_specs=[SMEM] + [ANY] * 3 + [VMEM] * 7, ou...  4.55 us
  transfers between devices with their start and end apart: 9, of which 3 were waited for; matrix products, arithmetic and copies ran while one was open for 0% of the time, Pallas kernels for 20%

profile of v1, /device:TPU:0, one launch (start us, length us, event | category | flops | bytes accessed | tf_op | source)
XLA Modules:
  0.0 86.4 jit_solution(14293503481773878810)
XLA Ops:
  1.3 4.5 %block_states.1 = (bf16[32,64,128]{2,1,0:T(8,128)(2,1)}, bf16[32,4224]{1,0:T(8,128)(2,1)}, f32[256,128]{1,0:T(8,128)}, f32[256,128]{1,0:T(8,128)}, f32[4,8,128]{...) custom-call(s32[1]{0:T(128)S(6)} %copy.29.step_ref, bf16[32,4096]{1,0:T(8,128)(2,1)} %signal_hbm.1, ...), custom_call_target="tpu_custom_call" | custom-call | tf_op jit(solution)/shard_map/block_states/pallas_call | solution.py:267
  5.8 1.7 %collective-permute-start = (bf16[32,4224]{1,0:T(8,128)(2,1)}, bf16[32,4224]{1,0:T(8,128)(2,1)S(1)}, u32[]{:S(2)}, u32[]{:S(2)}) collective-permute-start(bf16[32,4224]{1,0:T(8,128)(2,1)} %get-tuple-element.43.c0h), channel_id=1, source_target_pairs={{0,2},{1,3},{2,0},{3,1},{4,6},{5,7},{6,4},{7,5},{8,10},{9,11},{10,... | collective-permute-start | bytes 811016 | tf_op jit(solution)/shard_map/ppermute | solution.py:977
  7.6 0.0 copy-start.3
  7.6 10.6 %all-to-all-start = ((bf16[32,64,128]{2,1,0:T(8,128)(2,1)}), bf16[32,64,128]{2,1,0:T(8,128)(2,1)S(1)}, u32[]{:S(2)}, u32[]{:S(2)}) async-start(bf16[32,64,128]{2,1,0:T(8,128)(2,1)} %get-tuple-element.45.x_hbm), calls=%async_computation | async-start | bytes 1048576 | tf_op jit(solution)/shard_map/all_to_all | solution.py:956
  18.2 0.0 collective-permute-done.c2h
  18.2 0.0 copy-done.3
  18.3 0.0 copy-start.4
  18.3 0.1 collective-permute-start.1
  18.4 0.5 collective-permute-start.2
  18.9 5.1 %within_chunks.1 = (f32[1024,128]{1,0:T(8,128)}, f32[32,8,128]{2,1,0:T(8,128)}, f32[32,8,128]{2,1,0:T(8,128)}) custom-call(bf16[32,64,128]{2,1,0:T(8,128)(2,1)} %get-tuple-element.45.x_hbm, f32[4,8,128]{2,1,0:T(8,128)} %get-tuple-element.46.terms_ref, f32[2,32,128]{2,1,0:T(8,128)} %get-tuple-element.47.wide_ref), custom_call_target="tpu_custom_call" | custom-call | tf_op jit(solution)/shard_map/within_chunks/pallas_call | solution.py:329
  24.0 0.0 copy-done.4
  24.0 6.7 %all-to-all-done.got_hbm = bf16[32,64,128]{2,1,0:T(8,128)(2,1)S(1)} async-done(((bf16[32,64,128]{2,1,0:T(8,128)(2,1)}), bf16[32,64,128]{2,1,0:T(8,128)(2,1)S(1)}, u32[]{:S(2)}, u32[]{:S(2)}) %all-to-all-start) | async-done | bytes 524320 | tf_op jit(solution)/shard_map/all_to_all | solution.py:956
  30.7 0.0 copy-start.1
  30.7 0.0 collective-permute-done.1.c1h
  30.7 0.0 copy-start.5
  30.7 0.0 collective-permute-done.2.c3h
  30.7 0.0 copy-start.6
  30.7 0.8 copy-done.1
  31.5 0.1 copy-done.5
  31.6 0.1 copy-done.6
  31.7 6.7 %activation_and_states.1 = (bf16[32,64,128]{2,1,0:T(8,128)(2,1)}, f32[1024,128]{1,0:T(8,128)}, f32[32,128]{1,0:T(8,128)}, f32[256,128]{1,0:T(8,128)}, f32[256,128]{1,0:T(8,128)}) custom-call(s32[1]{0:T(128)} %bitcast.me_ref, s32[1]{0:T(128)} %bitcast.1.group_ref, bf16[32,4224]{1,0:T(8,128)(2,1)} %get-tuple-element.43.c0h, bf16[32,4224]{1,0:T(8,128)(2,1)} %copy-done.5, ...), custom_call_target="tpu_custom_call" | custom-call | tf_op jit(solution)/shard_map/activation_and_states/pallas_call | solution.py:459
  38.4 0.0 copy-start.7
  38.4 4.5 %all-to-all-start.1 = ((bf16[32,64,128]{2,1,0:T(8,128)(2,1)}), bf16[32,64,128]{2,1,0:T(8,128)(2,1)S(1)}, u32[]{:S(2)}, u32[]{:S(2)}) async-start(bf16[32,64,128]{2,1,0:T(8,128)(2,1)} %get-tuple-element.53), calls=%async_computation.1 | async-start | bytes 1048576 | tf_op jit(solution)/shard_map/all_to_all | solution.py:956
  42.9 0.0 copy-done.7
  42.9 0.1 collective-permute-start.5
  43.0 0.2 collective-permute-start.4
  43.2 1.6 %collective-permute-start.3 = (f32[32,128]{1,0:T(8,128)S(1)}, f32[32,128]{1,0:T(8,128)S(1)}, u32[]{:S(2)}, u32[]{:S(2)}) collective-permute-start(f32[32,128]{1,0:T(8,128)S(1)} %copy-done.7), channel_id=1, source_target_pairs={{0,1},{1,0},{2,3},{3,2},{4,5},{5,4},{6,7},{7,6},{8,9},{9,8},{10,11... | collective-permute-start | bytes 49160 | tf_op jit(solution)/shard_map/ppermute | solution.py:977
  44.8 5.1 %input_spectrum.1 = (f32[1024,256]{1,0:T(8,128)}, f32[512,128]{1,0:T(8,128)}, f32[2,256,128]{2,1,0:T(8,128)}, f32[16,128]{1,0:T(8,128)}) custom-call(s32[1]{0:T(128)} %bitcast.me_ref, bf16[32,64,128]{2,1,0:T(8,128)(2,1)} %copy-done.1, bf16[512,256]{1,0:T(8,128)(2,1)} %constant.25.clone.d1h_hbm, bf16[512,256]{1,0:T(8,128)(2,1)} %constant.26.clone.d1l_hbm, ...), custom_call_target="tpu_custom_call" | custom-call | tf_op jit(solution)/shard_map/input_spectrum/pallas_call | solution.py:743
  50.0 0.0 collective-permute-done.5.m3
  50.0 0.0 copy-start.8
  50.0 0.0 collective-permute-done.4.m2
  50.0 0.0 copy-start.9
  50.0 0.0 collective-permute-done.3.m1
  50.0 0.0 copy-start.10
  50.1 4.5 %all-to-all-done.1.got_hbm = bf16[32,64,128]{2,1,0:T(8,128)(2,1)S(1)} async-done(((bf16[32,64,128]{2,1,0:T(8,128)(2,1)}), bf16[32,64,128]{2,1,0:T(8,128)(2,1)S(1)}, u32[]{:S(2)}, u32[]{:S(2)}) %all-to-all-start.1) | async-done | bytes 524320 | tf_op jit(solution)/shard_map/all_to_all | solution.py:956
  54.6 0.0 copy-start
  54.6 0.0 copy-done.8
  54.6 0.0 copy-done.9
  54.6 0.0 copy-done.10
  54.6 0.8 copy-done
  55.4 8.3 %correlation.1 = (bf16[32,80,128]{2,1,0:T(8,128)(2,1)}, f32[8,128]{1,0:T(8,128)}) custom-call(bf16[32,64,128]{2,1,0:T(8,128)(2,1)} %copy-done, bf16[512,256]{1,0:T(8,128)(2,1)} %constant.25.clone.d1h_hbm, bf16[512,256]{1,0:T(8,128)(2,1)} %constant.26.clone.d1l_hbm, f32[2,256,512]{2,1,0:T(8,128)} %constant.27.clone.twiddle_hbm, ...), custom_call_target="tpu_custom_call" | custom-call | tf_op jit(solution)/shard_map/correlation/pallas_call | solution.py:875
  63.6 5.3 %all-to-all-start.2 = ((bf16[32,80,128]{2,1,0:T(8,128)(2,1)}), bf16[32,80,128]{2,1,0:T(8,128)(2,1)S(1)}, u32[]{:S(2)}, u32[]{:S(2)}) async-start(bf16[32,80,128]{2,1,0:T(8,128)(2,1)} %get-tuple-element.64), calls=%async_computation.2 | async-start | bytes 1310720 | tf_op jit(solution)/shard_map/all_to_all | solution.py:956
  69.0 7.0 %signal_gradient.1 = bf16[32,4096]{1,0:T(8,128)(2,1)} custom-call(s32[1]{0:T(128)} %bitcast.me_ref, bf16[32,64,128]{2,1,0:T(8,128)(2,1)} %copy-done, f32[1024,128]{1,0:T(8,128)} %get-tuple-element.54.send_hbm, bf16[32,4096]{1,0:T(8,128)(2,1)} %cot_hbm.3, f32[8,128]{1,0:T(8,128)} %get-tuple-element.61.after_hbm, f32[4,8,128]{2,1,0:T(8,128)} %get-tuple-element.46.terms_ref, ...), custom_call_target="tpu_custom_call" | custom-call | tf_op jit(solution)/shard_map/signal_gradient/pallas_call | solution.py:535
  76.0 7.2 %all-to-all-done.2.got_ref = bf16[32,80,128]{2,1,0:T(8,128)(2,1)S(1)} async-done(((bf16[32,80,128]{2,1,0:T(8,128)(2,1)}), bf16[32,80,128]{2,1,0:T(8,128)(2,1)S(1)}, u32[]{:S(2)}, u32[]{:S(2)}) %all-to-all-start.2) | async-done | bytes 655392 | tf_op jit(solution)/shard_map/all_to_all | solution.py:956
  83.2 0.0 copy-start.2
  83.2 0.8 copy-done.2
  84.0 2.4 %outputs.1 = (f32[32,4096]{1,0:T(8,128)}, f32[32,32]{1,0:T(8,128)}, f32[32,32]{1,0:T(8,128)}, f32[32,32]{1,0:T(8,128)}, f32[32,32]{1,0:T(8,128)}, /*index=5*/f32...) custom-call(s32[1]{0:T(128)S(6)} %copy.29.step_ref, s32[1]{0:T(128)} %bitcast.1.group_ref, ...), custom_call_target="tpu_custom_call" | custom-call | tf_op jit(solution)/shard_map/outputs/pallas_call | solution.py:940
Async XLA Ops:
  5.8 12.4 %collective-permute-start = (bf16[32,4224]{1,0:T(8,128)(2,1)}, bf16[32,4224]{1,0:T(8,128)(2,1)S(1)}, u32[]{:S(2)}, u32[]{:S(2)}) collective-permute-start(bf16[32,4224]{1,0:T(8,128)(2,1)} %get-tuple-element.43.c0h), channel_id=1, source_target_pairs={{0,2},{1,3},{2,0},{3,1},{4,6},{5,7},{6,4},{7,5},{8,10},{9,11},{10,... | collective-permute-start | bytes 811016 | tf_op jit(solution)/shard_map/ppermute | solution.py:977
  7.6 10.7 %copy-start.3 = (bf16[32,4224]{1,0:T(8,128)(2,1)S(1)}, bf16[32,4224]{1,0:T(8,128)(2,1)}, u32[]{:S(2)}) copy-start(bf16[32,4224]{1,0:T(8,128)(2,1)} %get-tuple-element.43.c0h) | copy-start | bytes 811012
  7.6 23.1 %all-to-all-start = ((bf16[32,64,128]{2,1,0:T(8,128)(2,1)}), bf16[32,64,128]{2,1,0:T(8,128)(2,1)S(1)}, u32[]{:S(2)}, u32[]{:S(2)}) async-start(bf16[32,64,128]{2,1,0:T(8,128)(2,1)} %get-tuple-element.45.x_hbm), calls=%async_computation | async-start | bytes 1048576 | tf_op jit(solution)/shard_map/all_to_all | solution.py:956
  18.3 5.7 %copy-start.4 = (bf16[32,4224]{1,0:T(8,128)(2,1)}, bf16[32,4224]{1,0:T(8,128)(2,1)S(1)}, u32[]{:S(2)}) copy-start(bf16[32,4224]{1,0:T(8,128)(2,1)S(1)} %collective-permute-done.c2h) | copy-start | bytes 811012
  18.3 12.4 %collective-permute-start.1 = (bf16[32,4224]{1,0:T(8,128)(2,1)S(1)}, bf16[32,4224]{1,0:T(8,128)(2,1)S(1)}, u32[]{:S(2)}, u32[]{:S(2)}) collective-permute-start(bf16[32,4224]{1,0:T(8,128)(2,1)S(1)} %copy-done.3), channel_id=1, source_target_pairs={{0,1},{1,0},{2,3},{3,2},{4,5},{5,4},{6,7},{7,6},{8,9},{9,8},{10,11... | collective-permute-start | bytes 811016 | tf_op jit(solution)/shard_map/ppermute | solution.py:977
  18.4 12.3 %collective-permute-start.2 = (bf16[32,4224]{1,0:T(8,128)(2,1)S(1)}, bf16[32,4224]{1,0:T(8,128)(2,1)S(1)}, u32[]{:S(2)}, u32[]{:S(2)}) collective-permute-start(bf16[32,4224]{1,0:T(8,128)(2,1)S(1)} %collective-permute-done.c2h), channel_id=1, source_target_pairs={{0,1},{1,0},{2,3},{3,2},{4,5},{5,4},{6,7},{7,6},{8,9},{9,8},{10,11... | collective-permute-start | bytes 811016 | tf_op jit(solution)/shard_map/ppermute | solution.py:977
  30.7 0.8 copy-start.1
  30.7 0.9 %copy-start.5 = (bf16[32,4224]{1,0:T(8,128)(2,1)}, bf16[32,4224]{1,0:T(8,128)(2,1)S(1)}, u32[]{:S(2)}) copy-start(bf16[32,4224]{1,0:T(8,128)(2,1)S(1)} %collective-permute-done.1.c1h) | copy-start | bytes 811012
  30.7 1.0 %copy-start.6 = (bf16[32,4224]{1,0:T(8,128)(2,1)}, bf16[32,4224]{1,0:T(8,128)(2,1)S(1)}, u32[]{:S(2)}) copy-start(bf16[32,4224]{1,0:T(8,128)(2,1)S(1)} %collective-permute-done.2.c3h) | copy-start | bytes 811012
  38.4 4.5 %copy-start.7 = (f32[32,128]{1,0:T(8,128)S(1)}, f32[32,128]{1,0:T(8,128)}, u32[]{:S(2)}) copy-start(f32[32,128]{1,0:T(8,128)} %get-tuple-element.55.after_hbm.m0) | copy-start | bytes 49156
  38.4 16.2 %all-to-all-start.1 = ((bf16[32,64,128]{2,1,0:T(8,128)(2,1)}), bf16[32,64,128]{2,1,0:T(8,128)(2,1)S(1)}, u32[]{:S(2)}, u32[]{:S(2)}) async-start(bf16[32,64,128]{2,1,0:T(8,128)(2,1)} %get-tuple-element.53), calls=%async_computation.1 | async-start | bytes 1048576 | tf_op jit(solution)/shard_map/all_to_all | solution.py:956
  42.9 7.1 %collective-permute-start.5 = (f32[32,128]{1,0:T(8,128)S(1)}, f32[32,128]{1,0:T(8,128)S(1)}, u32[]{:S(2)}, u32[]{:S(2)}) collective-permute-start(f32[32,128]{1,0:T(8,128)S(1)} %copy-done.7), channel_id=1, source_target_pairs={{0,3},{1,2},{2,1},{3,0},{4,7},{5,6},{6,5},{7,4},{8,11},{9,10},{10,... | collective-permute-start | bytes 49160 | tf_op jit(solution)/shard_map/ppermute | solution.py:977
  43.0 7.0 %collective-permute-start.4 = (f32[32,128]{1,0:T(8,128)S(1)}, f32[32,128]{1,0:T(8,128)S(1)}, u32[]{:S(2)}, u32[]{:S(2)}) collective-permute-start(f32[32,128]{1,0:T(8,128)S(1)} %copy-done.7), channel_id=1, source_target_pairs={{0,2},{1,3},{2,0},{3,1},{4,6},{5,7},{6,4},{7,5},{8,10},{9,11},{10,... | collective-permute-start | bytes 49160 | tf_op jit(solution)/shard_map/ppermute | solution.py:977
  43.2 6.8 %collective-permute-start.3 = (f32[32,128]{1,0:T(8,128)S(1)}, f32[32,128]{1,0:T(8,128)S(1)}, u32[]{:S(2)}, u32[]{:S(2)}) collective-permute-start(f32[32,128]{1,0:T(8,128)S(1)} %copy-done.7), channel_id=1, source_target_pairs={{0,1},{1,0},{2,3},{3,2},{4,5},{5,4},{6,7},{7,6},{8,9},{9,8},{10,11... | collective-permute-start | bytes 49160 | tf_op jit(solution)/shard_map/ppermute | solution.py:977
  50.0 4.6 %copy-start.8 = (f32[32,128]{1,0:T(8,128)}, f32[32,128]{1,0:T(8,128)S(1)}, u32[]{:S(2)}) copy-start(f32[32,128]{1,0:T(8,128)S(1)} %collective-permute-done.5.m3) | copy-start | bytes 49156
  50.0 4.6 %copy-start.9 = (f32[32,128]{1,0:T(8,128)}, f32[32,128]{1,0:T(8,128)S(1)}, u32[]{:S(2)}) copy-start(f32[32,128]{1,0:T(8,128)S(1)} %collective-permute-done.4.m2) | copy-start | bytes 49156
  50.0 4.5 %copy-start.10 = (f32[32,128]{1,0:T(8,128)}, f32[32,128]{1,0:T(8,128)S(1)}, u32[]{:S(2)}) copy-start(f32[32,128]{1,0:T(8,128)S(1)} %collective-permute-done.3.m1) | copy-start | bytes 49156
  54.6 0.8 copy-start
  63.6 19.6 %all-to-all-start.2 = ((bf16[32,80,128]{2,1,0:T(8,128)(2,1)}), bf16[32,80,128]{2,1,0:T(8,128)(2,1)S(1)}, u32[]{:S(2)}, u32[]{:S(2)}) async-start(bf16[32,80,128]{2,1,0:T(8,128)(2,1)} %get-tuple-element.64), calls=%async_computation.2 | async-start | bytes 1310720 | tf_op jit(solution)/shard_map/all_to_all | solution.py:956
  83.2 0.8 copy-start.2

commit v2 on v1

--- a/solution.py
+++ b/solution.py
@@ -28,10 +28,11 @@
 SEND3 = 80
 NT = (((1,), (1,)), ((), ()))
 NN = (((1,), (0,)), ((), ()))
-PARAMS = pltpu.CompilerParams(vmem_limit_bytes=56 * 1024 * 1024)
+GRANT = 63.75
 SMEM = pl.BlockSpec(memory_space=pltpu.SMEM)
 VMEM = pl.BlockSpec(memory_space=pltpu.VMEM)
 ANY = pl.BlockSpec(memory_space=pl.ANY)
+HBM = pl.BlockSpec(memory_space=pltpu.HBM)
 
 
 def expm1_small(x):
@@ -69,9 +70,16 @@
 
 
 def dot3(left, right, dims=NN):
-    lh, ll = left
-    rh, rl = right
-    return dot(lh, rh, dims) + dot(ll, rh, dims) + dot(lh, rl, dims)
+    (lh, ll), (rh, rl) = left, right
+    (axis,), (other,) = dims[0]
+    return dot(
+        jnp.concatenate([lh, ll, lh], axis), jnp.concatenate([rh, rh, rl], other), dims
+    )
+
+
+def dot2(left, right, dims=NN):
+    (axis,), (other,) = dims[0]
+    return dot(jnp.concatenate([left, left], axis), jnp.concatenate(right, other), dims)
 
 
 def started(sems, *pairs):
@@ -79,6 +87,41 @@
     for copy in copies:
         copy.start()
     return copies
+
+
+def waiting(copies):
+    def wait():
+        for copy in copies:
+            copy.wait()
+
+    return wait
+
+
+def staged(
+    kernel, scalars, plain, small, *, out_specs, out_shape, scratch_shapes, name,
+    plain_spec=HBM, limit=GRANT,
+):
+    heads, outs = len(scalars) + len(plain), len(out_shape)
+
+    def body(*refs):
+        given, rest = refs[:heads], refs[heads:]
+        sources, rest = rest[: len(small)], rest[len(small) :]
+        results, rest = rest[:outs], rest[outs:]
+        held, sems, rest = rest[: len(small)], rest[len(small)], rest[len(small) + 1 :]
+        copies = started(sems, *zip(sources, held))
+        kernel(waiting(copies), *given, *held, *results, *rest)
+
+    return pl.pallas_call(
+        body,
+        in_specs=[SMEM] * len(scalars) + [plain_spec] * len(plain) + [HBM] * len(small),
+        out_specs=out_specs,
+        out_shape=out_shape,
+        scratch_shapes=[pltpu.VMEM(a.shape, a.dtype) for a in small]
+        + [pltpu.SemaphoreType.DMA((len(small),))]
+        + scratch_shapes,
+        compiler_params=pltpu.CompilerParams(vmem_limit_bytes=int(limit * 1024 * 1024)),
+        name=name,
+    )(*scalars, *plain, *small)
 
 
 def sin_cos(x):
@@ -150,17 +193,25 @@
     return dot3(split(left), split(table), NT)
 
 
-def scan_states(sr_ref, si_ref, power_r, power_i, start_r, start_i, order, keep):
-    hr, hi = start_r, start_i
+def scan_states(sr_ref, si_ref, power_r, power_i, order):
+    hr = jnp.zeros((GROUPS, LN), F32)
+    hi = jnp.zeros((GROUPS, LN), F32)
     for i in order:
         rows = pl.ds(i * GROUPS, GROUPS)
         own_r, own_i = sr_ref[rows, :], si_ref[rows, :]
-        if keep:
-            sr_ref[rows, :] = hr
-            si_ref[rows, :] = hi
+        sr_ref[rows, :] = hr
+        si_ref[rows, :] = hi
         nr, ni = cmul(power_r, power_i, hr, hi)
         hr, hi = nr + own_r, ni + own_i
     return hr, hi
+
+
+def add_entering(sr_ref, si_ref, sr_in, si_in, step_r, step_i, start, order):
+    for k, i in enumerate(order):
+        rows = pl.ds(i * GROUPS, GROUPS)
+        nr, ni = cmul(step_r[k], step_i[k], *start) if k else start
+        sr_ref[rows, :] = sr_in[rows, :] + nr
+        si_ref[rows, :] = si_in[rows, :] + ni
 
 
 def toeplitz(taps_row):
@@ -178,7 +229,7 @@
         lane_channel((8, LN)) == lax.broadcasted_iota(jnp.int32, (8, LN), 0)
     ).astype(BF16)
     high, low = split(real)
-    return dot(owner, high, NT) + dot(owner, low, NT)
+    return dot2(owner, (high, low), NT)
 
 
 def packed_lanes(ref):
@@ -192,8 +243,8 @@
 
 
 def first_kernel(
-    step_ref, signal_hbm, cot_hbm, mix_hbm, size_ref, damping_ref, frequency_ref, re_ref, im_ref,
-    skip_ref, table_ref, send_hbm, own_hbm, sr_ref, si_ref, terms_ref, raw_ref, wide_ref,
+    wait_small, step_ref, signal_hbm, cot_hbm, mix_hbm, size_ref, damping_ref, frequency_ref, re_ref, im_ref,
+    skip_ref, table_ref, send_hbm, own_hbm, sr_ref, si_ref, terms_ref, wide_ref,
     signal_ref, own_ref, send_ref, rows_ref, pack_ref, sems, out_sems,
 ):
     loads = started(
@@ -202,6 +253,7 @@
         (cot_hbm, own_ref.at[:, pl.ds(0, BLOCK)]),
         (mix_hbm, own_ref.at[:, pl.ds(BLOCK, LN)]),
     )
+    wait_small()
     picked = lax.broadcasted_iota(jnp.int32, table_ref.shape, 1) == step_ref[0]
     embed = jnp.sum(jnp.where(picked, table_ref[...], 0.0), 1, keepdims=True)
     wide_ref[0] = jnp.broadcast_to(embed, (CH, LN))
@@ -210,8 +262,6 @@
     embed_lanes = packed_lanes(pack_ref)
     pack_ref[...] = jnp.broadcast_to(as_column(jnp.exp(size_ref[...])), (CH, MODES))
     raw = [packed_lanes(r) for r in (pack_ref, damping_ref, frequency_ref, re_ref, im_ref)]
-    for k in range(5):
-        raw_ref[k] = raw[k]
     terms = mode_terms(*raw)
     for k in range(4):
         terms_ref[k] = terms[k]
@@ -234,13 +284,12 @@
         fr, fi = falling(decay, turn, doubles, g)
         table = jnp.concatenate([fr, fi], 1)
         th, tl = split(table)
-        pr, pi = gather_group(dot(x, th) + dot(x, tl))
+        pr, pi = gather_group(dot2(x, (th, tl)))
         level = embed_lanes[g : g + 1]
         sr_ref[pl.ds(g, CK, stride=GROUPS), :] = pr + level * jnp.sum(fr, 0, keepdims=True)
         si_ref[pl.ds(g, CK, stride=GROUPS), :] = pi + level * jnp.sum(fi, 0, keepdims=True)
     zr, zi = power(decay, turn, float(LN))
-    zero = jnp.zeros((GROUPS, LN), F32)
-    hr, hi = scan_states(sr_ref, si_ref, zr, zi, zero, zero, range(CK), False)
+    hr, hi = scan_states(sr_ref, si_ref, zr, zi, range(CK))
     packed = packed_states(hr, hi)
     for d in range(RANKS):
         send_ref[d, CK:, :] = packed
@@ -264,17 +313,18 @@
 
 
 def first(step, signal, cotangent, mix_weight, sizes, params, skip, table):
-    return pl.pallas_call(
+    return staged(
         first_kernel,
-        in_specs=[SMEM] + [ANY] * 3 + [VMEM] * 7,
-        out_specs=[ANY] * 2 + [VMEM] * 5,
+        (step,),
+        (signal, cotangent, mix_weight),
+        (sizes, *params, skip, table),
+        out_specs=[ANY] * 2 + [VMEM] * 4,
         out_shape=(
             jax.ShapeDtypeStruct((RANKS, SEND1, LN), BF16),
             jax.ShapeDtypeStruct((CH, BLOCK + LN), BF16),
             jax.ShapeDtypeStruct((CK * GROUPS, LN), F32),
             jax.ShapeDtypeStruct((CK * GROUPS, LN), F32),
             jax.ShapeDtypeStruct((4, GROUPS, LN), F32),
-            jax.ShapeDtypeStruct((5, GROUPS, LN), F32),
             jax.ShapeDtypeStruct((2, CH, LN), F32),
         ),
         scratch_shapes=[
@@ -286,19 +336,28 @@
             pltpu.SemaphoreType.DMA((3,)),
             pltpu.SemaphoreType.DMA((3,)),
         ],
-        compiler_params=PARAMS,
         name="block_states",
-    )(step, signal, cotangent, mix_weight, sizes, *params, skip, table)
+    )
+
+
+def wide_sin_cos(x):
+    turns = jnp.floor(x * np.float32(1.0 / (2.0 * np.pi)) + 0.5)
+    x = (x - turns * np.float32(6.28125)) - turns * np.float32(2.0 * np.pi - 6.28125)
+    s, c = sin_cos(0.5 * x)
+    return 2.0 * s * c, 1.0 - 2.0 * s * s
 
 
 def far_power(decay, turn, blocks):
     size = jnp.exp(-decay * (BLOCK * blocks))
-    angle = turn * (BLOCK * blocks)
-    return size * jnp.cos(angle), size * jnp.sin(angle)
-
-
-def within_kernel(x_hbm, terms_ref, wide_ref, out_ref, far_r, far_i, x_ref, sems):
+    s, c = wide_sin_cos(turn * (BLOCK * blocks))
+    return size * c, size * s
+
+
+def within_kernel(
+    wait_small, x_hbm, terms_ref, wide_ref, out_ref, far_r, far_i, step_r, step_i, x_ref, sems
+):
     loads = started(sems, (x_hbm.at[:, pl.ds(0, CK), :], x_ref))
+    wait_small()
     terms = terms_ref[0], terms_ref[1], terms_ref[2], terms_ref[3]
     decay, turn = terms[0], terms[1]
     near = [far_power(decay, turn, float(b)) for b in range(4)]
@@ -310,6 +369,11 @@
             )
             far_r[4 * a + b] = pr
             far_i[4 * a + b] = pi
+    near = [far_power(decay, turn, b * LN / BLOCK) for b in range(4)]
+    for a in range(CK // 4):
+        base = far_power(decay, turn, 4 * a * LN / BLOCK)
+        for b in range(4):
+            step_r[4 * a + b], step_i[4 * a + b] = cmul(*base, *near[b])
     doubles = doublings(decay, turn)
     loads[0].wait()
     for g in range(GROUPS):
@@ -321,35 +385,36 @@
             x = x_ref[c]
             level = wide_ref[0, c : c + 1, :]
             out_ref[c * CK : (c + 1) * CK, :] = (
-                dot(x, high) + dot(x, low) + level * jnp.sum(matrix, 0, keepdims=True)
+                dot2(x, (high, low)) + level * jnp.sum(matrix, 0, keepdims=True)
             )
 
 
 def within(send, terms, wide):
-    return pl.pallas_call(
+    return staged(
         within_kernel,
-        in_specs=[ANY, VMEM, VMEM],
+        (),
+        (send,),
+        (terms, wide),
+        out_specs=[VMEM] * 5,
         out_shape=(
             jax.ShapeDtypeStruct((CH * CK, LN), F32),
             jax.ShapeDtypeStruct((RANKS, GROUPS, LN), F32),
             jax.ShapeDtypeStruct((RANKS, GROUPS, LN), F32),
+            jax.ShapeDtypeStruct((CK, GROUPS, LN), F32),
+            jax.ShapeDtypeStruct((CK, GROUPS, LN), F32),
         ),
         scratch_shapes=[pltpu.VMEM((CH, CK, LN), BF16), pltpu.SemaphoreType.DMA((1,))],
-        compiler_params=PARAMS,
         name="within_chunks",
-    )(send, terms, wide)
-
-
-def mixed_back(group, parts, act_ref):
+    )
+
+
+def mixed_back(group, cot_ref, act_ref):
     mine = lax.broadcasted_iota(jnp.int32, (CH, LN), 1) == group * CH + lax.broadcasted_iota(
         jnp.int32, (CH, LN), 0
     )
-    weights = jnp.concatenate([c[:, BLOCK:] for c in parts], 0)
-    weights = dot(mine.astype(BF16), weights, NT).astype(BF16)
+    weights = dot(mine.astype(BF16), cot_ref[:, BLOCK:], NT).astype(BF16)
     for i in range(CK):
-        cols = slice(i * LN, (i + 1) * LN)
-        cot = jnp.concatenate([c[:, cols] for c in parts], 0)
-        act_ref[pl.ds(i, CH, stride=CK), :] = dot(weights, cot)
+        act_ref[pl.ds(i, CH, stride=CK), :] = dot(weights, cot_ref[:, i * LN : (i + 1) * LN])
 
 
 def gelu_both(x):
@@ -375,17 +440,18 @@
 
 
 def second_kernel(
-    me_ref, group_ref, c0h, c1h, c2h, c3h, out_hbm, got_hbm, x_hbm, terms_ref, wide_ref, far_r,
-    far_i, sr_in, si_in, send_hbm, grad_hbm, mix_ref, sr_ref, si_ref,
-    c0, c1, c2, c3, flat_ref, out_ref, got_ref, x_ref, act_ref, activation_ref, send_ref, grad_ref, sems, out_sems,
+    wait_small, me_ref, group_ref, c0h, c1h, c2h, c3h, out_hbm, got_hbm, x_hbm, terms_ref, wide_ref, far_r,
+    far_i, step_r, step_i, sr_in, si_in, send_hbm, grad_hbm, mix_ref, sr_ref, si_ref,
+    cot_ref, flat_ref, out_ref, got_ref, x_ref, act_ref, activation_ref, send_ref, grad_ref, sems, out_sems,
 ):
     loads = started(
         sems,
         (got_hbm.at[:, pl.ds(CK, CK), :], got_ref),
-        (c0h, c0), (c1h, c1), (c2h, c2), (c3h, c3),
         (x_hbm.at[:, pl.ds(0, CK), :], x_ref),
         (out_hbm, out_ref),
-    )
+        *[(c, cot_ref.at[pl.ds(m * CH, CH), :]) for m, c in enumerate((c0h, c1h, c2h, c3h))],
+    )
+    wait_small()
     me = me_ref[0]
     terms = terms_ref[0], terms_ref[1], terms_ref[2], terms_ref[3]
     decay, turn = terms[0], terms[1]
@@ -393,15 +459,13 @@
     zr, zi = power(decay, turn, float(LN))
     one_r, one_i = power(decay, turn, 1.0)
     ur, ui = cmul(2.0 * terms[2], 2.0 * terms[3], one_r, one_i)
-    sr_ref[...] = sr_in[...]
-    si_ref[...] = si_in[...]
     loads[0].wait()
     start = entering(lambda d: unpacked_states(got_ref[d]), far_r, far_i, lambda d: me - 1 - d)
-    scan_states(sr_ref, si_ref, zr, zi, start[0], start[1], range(CK), True)
-    for copy in loads[1:5]:
+    add_entering(sr_ref, si_ref, sr_in, si_in, step_r, step_i, start, range(CK))
+    for copy in loads[3:]:
         copy.wait()
-    mixed_back(group_ref[0], (c0, c1, c2, c3), act_ref)
-    for copy in loads[5:]:
+    mixed_back(group_ref[0], cot_ref, act_ref)
+    for copy in loads[1:3]:
         copy.wait()
     stores = []
     for g in range(GROUPS):
@@ -433,8 +497,7 @@
         pr, pi = gather_group(products)
         sr_ref[every, :] = pr
         si_ref[every, :] = pi
-    zero = jnp.zeros((GROUPS, LN), F32)
-    hr, hi = scan_states(sr_ref, si_ref, zr, zi, zero, zero, range(CK - 1, -1, -1), False)
+    hr, hi = scan_states(sr_ref, si_ref, zr, zi, range(CK - 1, -1, -1))
     packed = packed_states(hr, hi)
     for d in range(RANKS):
         send_ref[d, CK:, :] = packed
@@ -449,16 +512,17 @@
     stores[-1].start()
     for i in range(CK):
         flat_ref[:, i * LN : (i + 1) * LN] = activation_ref[pl.ds(i, CH, stride=CK), :].astype(BF16)
-    flat = flat_ref[...]
-    mix_ref[...] = jnp.concatenate([dot(flat, c[:, :BLOCK], NT) for c in (c0, c1, c2, c3)], 1)
+    mix_ref[...] = dot(flat_ref[...], cot_ref[:, :BLOCK], NT)
     for copy in stores:
         copy.wait()
 
 
-def second(me, group, parts, out, got, send, terms, wide, far, sr, si):
-    return pl.pallas_call(
+def second(me, group, parts, out, got, send, terms, wide, far, steps, sr, si):
+    return staged(
         second_kernel,
-        in_specs=[SMEM] * 2 + [ANY] * 7 + [VMEM] * 6,
+        (me, group),
+        (*parts, out, got, send),
+        (terms, wide, far[0], far[1], steps[0], steps[1], sr, si),
         out_specs=[ANY] * 2 + [VMEM] * 3,
         out_shape=(
             jax.ShapeDtypeStruct((RANKS, SEND2, LN), BF16),
@@ -467,8 +531,8 @@
             jax.ShapeDtypeStruct((CK * GROUPS, LN), F32),
             jax.ShapeDtypeStruct((CK * GROUPS, LN), F32),
         ),
-        scratch_shapes=[pltpu.VMEM((CH, BLOCK + LN), BF16)] * 4
-        + [
+        scratch_shapes=[
+            pltpu.VMEM((LN, BLOCK + LN), BF16),
             pltpu.VMEM((CH, BLOCK), BF16),
             pltpu.VMEM((CH * CK, LN), F32),
             pltpu.VMEM((RANKS, CK, LN), BF16),
@@ -480,14 +544,40 @@
             pltpu.SemaphoreType.DMA((7,)),
             pltpu.SemaphoreType.DMA((GROUPS + 2,)),
         ],
-        compiler_params=PARAMS,
         name="activation_and_states",
-    )(me, group, *parts, out, got, send, terms, wide, far[0], far[1], sr, si)
+    )
+
+
+def pull_table(size_ref, damping_ref, frequency_ref, re_ref, im_ref, pull_ref):
+    def tiled(values):
+        return jnp.concatenate([values] * LANE_CH, 1)
+
+    size = jnp.broadcast_to(as_column(jnp.exp(size_ref[...])), (CH, LN))
+    raw = [size] + [tiled(r[...]) for r in (damping_ref, frequency_ref, re_ref, im_ref)]
+    (d, th, mr, mi), pull = jax.vjp(mode_terms, *raw)
+    zero = jnp.zeros((CH, LN), F32)
+    pulled = [
+        pull((zero, zero, zero + 2.0, zero)),
+        pull((zero, zero, zero, zero - 2.0)),
+        pull((-2.0 * mr, -2.0 * mi, zero, zero)),
+        pull((2.0 * mi, -2.0 * mr, zero, zero)),
+    ]
+    inverse = 1.0 / (raw[1] * raw[1] + raw[2] * raw[2])
+    qr, qi = cmul(raw[3], raw[4], raw[1] * inverse, raw[2] * inverse)
+    one_r, one_i = power(d, th, 1.0)
+    er, ei = cmul(qr, qi, one_r, one_i)
+    first_lanes = lane_block(zero) == 0
+    for k, p in enumerate(pulled):
+        pull_ref[k] = by_block(p[1:])
+        pull_ref[4 + k] = jnp.where(first_lanes, p[0] * raw[0], 0.0)
+    for k, value in enumerate((2.0 * qr, -2.0 * er, 2.0 * ei)):
+        pull_ref[8 + k] = jnp.where(first_lanes, value, 0.0)
 
 
 def signal_kernel(
-    me_ref, got_hbm, send_hbm, cot_hbm, after_hbm, terms_ref, wide_ref, far_r, far_i, sr_in, si_in,
-    out_ref, sr_ref, si_ref, rows_ref, got_ref, send_ref, cot_ref, sems,
+    wait_small, me_ref, got_hbm, send_hbm, cot_hbm, after_hbm, terms_ref, wide_ref, far_r, far_i,
+    step_r, step_i, sr_in, si_in, size_ref, damping_ref, frequency_ref, re_ref, im_ref,
+    out_ref, pull_ref, sr_ref, si_ref, rows_ref, got_ref, send_ref, cot_ref, sems,
 ):
     loads = started(
         sems,
@@ -495,19 +585,17 @@
         (send_hbm, send_ref),
         (cot_hbm, cot_ref),
     )
+    wait_small()
+    pull_table(size_ref, damping_ref, frequency_ref, re_ref, im_ref, pull_ref)
     me = me_ref[0]
     terms = terms_ref[0], terms_ref[1], terms_ref[2], terms_ref[3]
     decay, turn = terms[0], terms[1]
     doubles = doublings(decay, turn)
-    zr, zi = power(decay, turn, float(LN))
     one_r, one_i = power(decay, turn, 1.0)
     ur, ui = cmul(2.0 * terms[2], 2.0 * terms[3], one_r, one_i)
-
-    sr_ref[...] = sr_in[...]
-    si_ref[...] = si_in[...]
     loads[0].wait()
     start = entering(lambda d: unpacked_states(got_ref[d]), far_r, far_i, lambda d: d - me - 1)
-    scan_states(sr_ref, si_ref, zr, zi, start[0], start[1], range(CK - 1, -1, -1), True)
+    add_entering(sr_ref, si_ref, sr_in, si_in, step_r, step_i, start, range(CK - 1, -1, -1))
     for copy in loads[1:]:
         copy.wait()
     for g in range(GROUPS):
@@ -531,11 +619,17 @@
         ).astype(BF16)
 
 
-def signal_grad(me, got, send, terms, wide, far, sr, si, cotangent, after):
-    return pl.pallas_call(
+def signal_grad(me, got, send, terms, wide, far, steps, sr, si, raw, cotangent, after):
+    return staged(
         signal_kernel,
-        in_specs=[SMEM] + [ANY] * 4 + [VMEM] * 6,
-        out_shape=jax.ShapeDtypeStruct((CH, BLOCK), BF16),
+        (me,),
+        (got, send, cotangent, after),
+        (terms, wide, far[0], far[1], steps[0], steps[1], sr, si, *raw),
+        out_specs=[VMEM] * 2,
+        out_shape=(
+            jax.ShapeDtypeStruct((CH, BLOCK), BF16),
+            jax.ShapeDtypeStruct((11, CH, LN), F32),
+        ),
         scratch_shapes=[
             pltpu.VMEM((CK * GROUPS, LN), F32),
             pltpu.VMEM((CK * GROUPS, LN), F32),
@@ -545,9 +639,9 @@
             pltpu.VMEM((CH, BLOCK), BF16),
             pltpu.SemaphoreType.DMA((3,)),
         ],
-        compiler_params=PARAMS,
         name="signal_gradient",
-    )(me, got, send, cotangent, after, terms, wide, far[0], far[1], sr, si)
+        limit=62.5,
+    )
 
 
 def dft_tables():
@@ -607,9 +701,10 @@
 def forward_dft(rows, exact, d1h, d1l, d2h, d2l, twiddle, steps, wait1, wait2):
     xh, xl = split(rows)
     wait1()
-    a = dot(d1h[...], xh) + dot(d1l[...], xh)
-    if not exact:
-        a = a + dot(d1h[...], xl)
+    if exact:
+        a = dot(jnp.concatenate([d1h[...], d1l[...]], 1), jnp.concatenate([xh, xh], 0))
+    else:
+        a = dot3((d1h[...], d1l[...]), (xh, xl))
     wait2()
     parts = []
     for q in range(PER):
@@ -640,7 +735,7 @@
     bh, bl = split(
         jnp.concatenate([jnp.concatenate(real, 1), jnp.concatenate(imag, 1)], 0)
     )
-    return dot(d1th[...], bh) + dot(d1th[...], bl) + dot(d1tl[...], bh)
+    return dot3((d1th[...], d1tl[...]), (bh, bl))
 
 
 def lane_block(row):
@@ -662,17 +757,9 @@
     return result
 
 
-def waiting(copies):
-    def wait():
-        for copy in copies:
-            copy.wait()
-
-    return wait
-
-
 def spectrum_kernel(
-    me_ref, got_hbm, d1h_hbm, d1l_hbm, twiddle_hbm, d2h_hbm, d2l_hbm, after_hbm,
-    steps_ref, wide_ref, raw_ref, spec_ref, column_ref, turn_ref, pull_ref,
+    wait_small, me_ref, got_hbm, d1h_hbm, d1l_hbm, twiddle_hbm, d2h_hbm, d2l_hbm, after_hbm,
+    steps_ref, wide_ref, terms_ref, spec_ref, column_ref, turn_ref,
     got_ref, d1h, d1l, twiddle, d2h, d2l, rows_ref, sems,
 ):
     loads = started(
@@ -680,6 +767,7 @@
         (got_hbm.at[:, pl.ds(0, CK), :], got_ref),
         (d1h_hbm, d1h), (d1l_hbm, d1l), (twiddle_hbm, twiddle), (d2h_hbm, d2h), (d2l_hbm, d2l),
     )
+    wait_small()
     me = me_ref[0]
     embed = wide_ref[0, pl.ds(me, 1), :]
     loads[0].wait()
@@ -694,31 +782,10 @@
     at, shift = me // LANE_CH, (me % LANE_CH) * MODES
 
     def own(k):
-        row = jnp.broadcast_to(raw_ref[k, pl.ds(at, 1), :], (8, LN))
+        row = jnp.broadcast_to(terms_ref[k, pl.ds(at, 1), :], (8, LN))
         return repeated(pltpu.roll(row, (LN - shift) % LN, 1)[:1])
 
-    raw = [own(k) for k in range(5)]
-    (d, th, mr, mi), pull = jax.vjp(mode_terms, *raw)
-    zero = jnp.zeros((1, LN), F32)
-    pulled = [
-        pull((zero, zero, zero + 2.0, zero)),
-        pull((zero, zero, zero, zero - 2.0)),
-        pull((-2.0 * mr, -2.0 * mi, zero, zero)),
-        pull((2.0 * mi, -2.0 * mr, zero, zero)),
-    ]
-    inverse = 1.0 / (raw[1] * raw[1] + raw[2] * raw[2])
-    qr, qi = cmul(raw[3], raw[4], raw[1] * inverse, raw[2] * inverse)
-    one_r, one_i = power(d, th, 1.0)
-    er, ei = cmul(qr, qi, one_r, one_i)
-    first_lanes = lane_block(zero) == 0
-    pull_ref[...] = jnp.concatenate(
-        [by_block(p[1:]) for p in pulled]
-        + [jnp.where(first_lanes, p[0] * raw[0], 0.0) for p in pulled]
-        + [jnp.where(first_lanes, v, 0.0) for v in (2.0 * qr, -2.0 * er, 2.0 * ei)]
-        + [wide_ref[1, pl.ds(me, 1), :]]
-        + [jnp.zeros((4, LN), F32)],
-        0,
-    )
+    d, th = own(0), own(1)
     steps = lax.broadcasted_iota(jnp.int32, (8, LN), 0).astype(F32)
     cr, ci = power(d, th, steps)
     for k in (8, 16, 32, 64, 128, 256):
@@ -738,16 +805,18 @@
         turn_ref[1, piece * RANKS : (piece + 1) * RANKS, :] = ni
 
 
-def spectrum(me, got, after, wide, raw, tables):
+def spectrum(me, got, after, wide, terms, tables):
     (d1h, d1l), unused, (d2h, d2l), twiddle, steps = tables
-    return pl.pallas_call(
+    return staged(
         spectrum_kernel,
-        in_specs=[SMEM] + [ANY] * 7 + [VMEM] * 3,
+        (me,),
+        (got, d1h, d1l, twiddle, d2h, d2l, after),
+        (steps, wide, terms),
+        out_specs=[VMEM] * 3,
         out_shape=(
             jax.ShapeDtypeStruct((PER * ROWS, 2 * LN), F32),
             jax.ShapeDtypeStruct((COLS, LN), F32),
             jax.ShapeDtypeStruct((2, ROWS, LN), F32),
-            jax.ShapeDtypeStruct((16, LN), F32),
         ),
         scratch_shapes=[
             pltpu.VMEM((RANKS, CK, LN), BF16),
@@ -759,14 +828,13 @@
             pltpu.VMEM((RANKS * CK, LN), F32),
             pltpu.SemaphoreType.DMA((6,)),
         ],
-        compiler_params=PARAMS,
         name="input_spectrum",
-    )(me, got, d1h, d1l, twiddle, d2h, d2l, after, steps, wide, raw)
+    )
 
 
 def correlate_kernel(
-    got_hbm, d1h_hbm, d1l_hbm, twiddle_hbm, d2h_hbm, d2l_hbm, spec_hbm, d1th_hbm, d1tl_hbm,
-    column_hbm, turn_hbm, steps_ref, pull_ref, m0, m1, m2, m3, send_hbm, after_ref,
+    wait_small, got_hbm, d1h_hbm, d1l_hbm, twiddle_hbm, d2h_hbm, d2l_hbm, spec_hbm, d1th_hbm, d1tl_hbm,
+    column_hbm, turn_hbm, steps_ref, m0, m1, m2, m3, send_hbm, after_ref,
     got_ref, d1h, d1l, twiddle, d2h, d2l, spec_ref, d1th, d1tl, column_ref, turn_ref,
     rows_ref, send_ref, sems, out_sems,
 ):
@@ -777,6 +845,7 @@
         (spec_hbm, spec_ref), (d1th_hbm, d1th), (d1tl_hbm, d1tl), (column_hbm, column_ref),
         (turn_hbm, turn_ref),
     )
+    wait_small()
     mixes = by_block([m[...] for m in (m0, m1, m2, m3)]).astype(BF16)
     for d in range(RANKS):
         send_ref[d, CK : 2 * CK, :] = mixes
@@ -809,8 +878,9 @@
         )
     )
     stores[-1].start()
-    both = dot3(split(jnp.concatenate([kernel_rows, g_rows], 0)), split(column_ref[...]))
-    inner = both[:ROWS]
+    column = split(column_ref[...])
+    inner = dot3(split(kernel_rows), column)
+    g_inner = dot2(g_rows.astype(BF16), column)
     rr, ri = turn_ref[0], turn_ref[1]
     ids = lax.broadcasted_iota(jnp.int32, (ROWS, LN), 0)
     starts = ((ids % RANKS) * BLOCK + (ids // RANKS) * COLS).astype(F32)
@@ -821,38 +891,13 @@
     by_r, by_i = rr * inner, ri * inner
     u, v = total(by_r), total(by_i)
     su, sv = total(starts * by_r), total(starts * by_i)
-    gu, gv = total(rr * both[ROWS:]), total(ri * both[ROWS:])
-
-    def block(row, k):
-        moved = pltpu.roll(row, (LN - k * MODES) % LN, 1) if k else row
-        return jnp.where(lane_block(row) == 0, moved, 0.0)
-
-    cos_sum = block(u, 0) - block(v, 1)
-    sin_sum = block(u, 1) + block(v, 0)
-    cos_moment = block(u, 2) - block(v, 3) + block(su, 0) - block(sv, 1)
-    sin_moment = block(u, 3) + block(v, 2) + block(su, 1) + block(sv, 0)
-    grads = jnp.zeros((1, LN), F32)
-    step = jnp.zeros((1, LN), F32)
-    for k, value in enumerate((cos_sum, sin_sum, cos_moment, sin_moment)):
-        grads = grads + pull_ref[k : k + 1, :] * repeated(value)
-        step = step + pull_ref[4 + k : 5 + k, :] * value
-    step_sum = jnp.sum(step, 1, keepdims=True)
-    skip_sum = kernel_rows[0:1, 0:1]
-    g_sum = jnp.sum(total(g_rows), 1, keepdims=True)
-    back_sum = jnp.sum(
-        pull_ref[8:9, :] * g_sum
-        + pull_ref[9:10, :] * (block(gu, 0) - block(gv, 1))
-        + pull_ref[10:11, :] * (block(gu, 1) + block(gv, 0)),
-        1,
-        keepdims=True,
-    )
+    gu, gv = total(rr * g_inner), total(ri * g_inner)
+
     lanes = lax.broadcasted_iota(jnp.int32, (1, LN), 1)
-    scalars = (
-        jnp.where(lanes == 0, step_sum, 0.0)
-        + jnp.where(lanes == 1, skip_sum, 0.0)
-        + jnp.where(lanes == 2, back_sum + pull_ref[11:12, :] * g_sum, 0.0)
-    )
-    small = jnp.concatenate([grads, scalars, jnp.zeros((6, LN), F32)], 0)
+    scalars = jnp.where(lanes == 0, kernel_rows[0:1, 0:1], 0.0) + jnp.where(
+        lanes == 1, jnp.sum(total(g_rows), 1, keepdims=True), 0.0
+    )
+    small = jnp.concatenate([u, v, su, sv, gu, gv, scalars, jnp.zeros((1, LN), F32)], 0)
     after_ref[...] = small
     high, low = split(jnp.concatenate([small, small], 0))
     upper = lax.broadcasted_iota(jnp.int32, (16, LN), 0) < 8
@@ -870,11 +915,13 @@
         copy.wait()
 
 
-def correlate(got, spec, tables, column, turns, pull, mixes):
+def correlate(got, spec, tables, column, turns, mixes):
     (d1h, d1l), (d1th, d1tl), (d2h, d2l), twiddle, steps = tables
-    return pl.pallas_call(
+    return staged(
         correlate_kernel,
-        in_specs=[ANY] * 11 + [VMEM] * 6,
+        (),
+        (got, d1h, d1l, twiddle, d2h, d2l, spec, d1th, d1tl, column, turns),
+        (steps, *mixes),
         out_specs=[ANY, VMEM],
         out_shape=(
             jax.ShapeDtypeStruct((RANKS, SEND3, LN), BF16),
@@ -897,13 +944,12 @@
             pltpu.SemaphoreType.DMA((11,)),
             pltpu.SemaphoreType.DMA((3,)),
         ],
-        compiler_params=PARAMS,
         name="correlation",
-    )(got, d1h, d1l, twiddle, d2h, d2l, spec, d1th, d1tl, column, turns, steps, pull, *mixes)
+    )
 
 
 def outputs_kernel(
-    step_ref, group_ref, got_ref, kernel_ref, damping_ref, frequency_ref, re_ref, im_ref,
+    wait_small, step_ref, group_ref, got_ref, pull_ref, wide_ref, kernel_ref, damping_ref, frequency_ref, re_ref, im_ref,
     size_ref, skip_ref, mix_ref, table_ref, rows_ref, turned_ref,
 ):
     mixes = jnp.zeros((CH, LN), F32)
@@ -915,15 +961,40 @@
     for c in range(CH):
         small = got_ref[c, 2 * CK :, :].astype(F32)
         rows_ref[c * 8 : (c + 1) * 8, :] = small[:8] + small[8:]
-    grads = rows_ref[pl.ds(0, CH, stride=8), :]
+    wait_small()
+    u, v, su, sv, gu, gv, scalars = (rows_ref[pl.ds(k, CH, stride=8), :] for k in range(7))
+
+    def block(row, k):
+        moved = pltpu.roll(row, (LN - k * MODES) % LN, 1) if k else row
+        return jnp.where(lane_block(row) == 0, moved, 0.0)
+
+    sums = (
+        block(u, 0) - block(v, 1),
+        block(u, 1) + block(v, 0),
+        block(u, 2) - block(v, 3) + block(su, 0) - block(sv, 1),
+        block(u, 3) + block(v, 2) + block(su, 1) + block(sv, 0),
+    )
+    grads = jnp.zeros((CH, LN), F32)
+    size = jnp.zeros((CH, LN), F32)
+    for k, value in enumerate(sums):
+        grads = grads + pull_ref[k] * repeated(value)
+        size = size + pull_ref[4 + k] * value
     for k, ref in enumerate((damping_ref, frequency_ref, re_ref, im_ref)):
         ref[...] = grads[:, k * MODES : (k + 1) * MODES]
-    scalars = rows_ref[pl.ds(1, CH, stride=8), :]
+    g_sum = scalars[:, 1:2]
+    back = (
+        pull_ref[8] * g_sum
+        + pull_ref[9] * (block(gu, 0) - block(gv, 1))
+        + pull_ref[10] * (block(gu, 1) + block(gv, 0))
+    )
+    back_sum = jnp.sum(back, 1, keepdims=True) + wide_ref[1][:, :1] * g_sum
+    lanes = lax.broadcasted_iota(jnp.int32, (CH, LN), 1)
+    scalars = jnp.where(lanes == 0, jnp.sum(size, 1, keepdims=True), scalars[:, 0:1])
     turned = jnp.concatenate([scalars, jnp.zeros((LN - CH, LN), F32)], 0).T
     size_ref[...] = turned[0:1, :CH]
     skip_ref[...] = turned[1:2, :CH]
     picked = lax.broadcasted_iota(jnp.int32, table_ref.shape, 1) == step_ref[0]
-    table_ref[...] = jnp.where(picked, scalars[:, 2:3], 0.0)
+    table_ref[...] = jnp.where(picked, back_sum, 0.0)
     turned_ref[...] = jnp.concatenate([mixes, jnp.zeros((LN - CH, LN), F32)], 0).T
     mix_ref[...] = jnp.concatenate(
         [
@@ -934,12 +1005,15 @@
     )
 
 
-def outputs(step, group, got, table_len):
+def outputs(step, group, got, pull, levels, table_len):
     wide = jax.ShapeDtypeStruct((CH, MODES), F32)
     row = jax.ShapeDtypeStruct((1, CH), F32)
-    return pl.pallas_call(
+    return staged(
         outputs_kernel,
-        in_specs=[SMEM, SMEM, VMEM],
+        (step, group),
+        (got,),
+        (pull, levels),
+        out_specs=[VMEM] * 9,
         out_shape=(
             jax.ShapeDtypeStruct((CH, BLOCK), F32),
             wide, wide, wide, wide, row, row,
@@ -947,9 +1021,10 @@
             jax.ShapeDtypeStruct((CH, table_len), F32),
         ),
         scratch_shapes=[pltpu.VMEM((CH * CK, LN), F32), pltpu.VMEM((LN, LN), F32)],
-        compiler_params=PARAMS,
         name="outputs",
-    )(step, group, got)
+        plain_spec=VMEM,
+        limit=8,
+    )
 
 
 def exchange(values):
@@ -976,24 +1051,30 @@
     def swap(values, mask):
         return lax.ppermute(values, "chan", [(i, i ^ mask) for i in range(4)])
 
-    send1, own, sr, si, terms, raw, wide = first(
-        diffusion_step, signal, cotangent, mix_weight, log_step[None],
-        (damping, frequency, coef_re, coef_im), skip_gain[None], embed_table.T,
+    send1, own, sr, si, terms, wide = first(
+        diffusion_step, signal, cotangent, mix_weight, log_step[None], (damping, frequency, coef_re, coef_im),
+        skip_gain[None], embed_table.T,
     )
     got1 = exchange(send1)
     own, across = lax.optimization_barrier((own, swap(own, 2)))
     parts = (own, swap(own, 1), across, swap(across, 1))
-    out, far_r, far_i = within(send1, terms, wide)
+    out, far_r, far_i, step_r, step_i = within(send1, terms, wide)
     far = (far_r, far_i)
-    send2, grad, mix, br, bi = second(me, group, parts, out, got1, send1, terms, wide, far, sr, si)
+    steps = (step_r, step_i)
+    send2, grad, mix, br, bi = second(
+        me, group, parts, out, got1, send1, terms, wide, far, steps, sr, si
+    )
     got2 = exchange(send2)
     mixes = [mix] + [swap(mix, m) for m in range(1, 4)]
-    spec, column, turns, pull = spectrum(me, got1, mix, wide, raw, tables)
-    send3, after = correlate(got2, spec, tables, column, turns, pull, mixes)
+    spec, column, turns = spectrum(me, got1, mix, wide, terms, tables)
+    send3, after = correlate(got2, spec, tables, column, turns, mixes)
     got3 = exchange(send3)
-    grad_signal = signal_grad(me, got2, grad, terms, wide, far, br, bi, cotangent, after)
+    grad_signal, pull = signal_grad(
+        me, got2, grad, terms, wide, far, steps, br, bi,
+        (log_step[None], damping, frequency, coef_re, coef_im), cotangent, after,
+    )
     kernel, g_damping, g_frequency, g_re, g_im, g_size, g_skip, g_mix, g_table = outputs(
-        diffusion_step, group, got3, embed_table.shape[0]
+        diffusion_step, group, got3, pull, wide, embed_table.shape[0]
     )
     return (
         grad_signal,

time: 87.4 us -> 84.3 us (0.965)
  Pallas kernels: 39.1 us -> 35 us
  waiting for transfers between devices: 18.5 us -> 21 us
  local copies, waits for them, and re-layouts: 2.61 us -> 0.95 us
    pallas_call x7, Pallas kernels: 39.1 us -> 35 us  [staged(): pl.pallas_call(body, in_specs=[SMEM] * len(scalars) + [plain_spec] * len(...]
    all_to_all x3, waiting for transfers between devices: 18.5 us -> 21 us  [exchange(): return lax.all_to_all(values, 'tm', split_axis=0, concat_axis=0, tiled=True)]
    unnamed x22 -> x12, local copies, waits for them, and re-layouts: 2.61 us -> 0.95 us
  transfers between devices with their start and end apart: 9 -> 9, of which waited for: 3 -> 3; matrix products, arithmetic and copies ran while one was open for 0% -> 0% of each run, Pallas kernels for 20% -> 17%
where the time goes in v2:
time: 84.3 us; the launch traced here: 83.6 us
  Pallas kernels  35 us (42%)
  starting transfers between devices  25 us (30%)
  waiting for transfers between devices  21 us (25%)
  between operations  1.63 us (2%)
  local copies, waits for them, and re-layouts  0.95 us (1%)
    pallas_call x7, Pallas kernels, staged(): pl.pallas_call(body, in_specs=[SMEM] * len(scalars) + [plain_spec] * len(...  35 us
    all_to_all x3, waiting for transfers between devices, exchange(): return lax.all_to_all(values, 'tm', split_axis=0, concat_axis=0, tiled=True)  21 us
    all_to_all x3, starting transfers between devices, exchange(): return lax.all_to_all(values, 'tm', split_axis=0, concat_axis=0, tiled=True)  20.7 us
    ppermute x6, starting transfers between devices, swap(): return lax.ppermute(values, 'chan', [(i, i ^ mask) for i in range(4)])  4.26 us
  transfers between devices with their start and end apart: 9, of which 3 were waited for; matrix products, arithmetic and copies ran while one was open for 0% of the time, Pallas kernels for 17%

profile of v2, /device:TPU:0, one launch (start us, length us, event | category | flops | bytes accessed | tf_op | source)
XLA Modules:
  0.0 83.6 jit_solution(2016798035379775930)
XLA Ops:
  1.3 4.0 %block_states.1 = (bf16[32,64,128]{2,1,0:T(8,128)(2,1)}, bf16[32,4224]{1,0:T(8,128)(2,1)}, f32[256,128]{1,0:T(8,128)}, f32[256,128]{1,0:T(8,128)}, f32[4,8,128]{2,1,0:T(8,128)}, /*index=5*/f32[2,32,128]{2,1,0:T(8,128)}) custom-call(s32[1]{0:T(128)S(6)} %copy.29.refs_0_, bf16[32,4096]{1,0:T(8,128)(2,1)} %refs_1_.2, bf16[32,4096]{1,0:T(8,128)(2,1)} %refs_3_.5, ...), custom_call_target="tpu_custom_call" | custom-call | tf_op jit(solution)/shard_map/block_states/pallas_call | solution.py:114
  5.3 1.7 %collective-permute-start = (bf16[32,4224]{1,0:T(8,128)(2,1)}, bf16[32,4224]{1,0:T(8,128)(2,1)}, u32[]{:S(2)}, u32[]{:S(2)}) collective-permute-start(bf16[32,4224]{1,0:T(8,128)(2,1)} %get-tuple-element.45.refs_2_), channel_id=1, source_target_pairs={{0,2},{1,3},{2,0},{3,1},{4,6},{5,7},{6,4},{7,5},{8,10},{9,11},{10,... | collective-permute-start | bytes 811016 | tf_op jit(solution)/shard_map/ppermute | solution.py:1052
  7.0 10.6 %all-to-all-start = ((bf16[32,64,128]{2,1,0:T(8,128)(2,1)}), bf16[32,64,128]{2,1,0:T(8,128)(2,1)}, u32[]{:S(2)}, u32[]{:S(2)}) async-start(bf16[32,64,128]{2,1,0:T(8,128)(2,1)} %get-tuple-element.47.refs_0_.refs_8_), calls=%async_computation | async-start | bytes 1048576 | tf_op jit(solution)/shard_map/all_to_all | solution.py:1031
  17.7 0.0 collective-permute-done.refs_4_
  17.7 0.1 collective-permute-start.1
  17.8 0.5 collective-permute-start.2
  18.3 4.0 %within_chunks.1 = (f32[1024,128]{1,0:T(8,128)}, f32[32,8,128]{2,1,0:T(8,128)}, f32[32,8,128]{2,1,0:T(8,128)}, f32[32,8,128]{2,1,0:T(8,128)}, f32[32,8,128]{2,1,0:T(8,128)}) custom-call(bf16[32,64,128]{2,1,0:T(8,128)(2,1)} %get-tuple-element.47.refs_0_.refs_8_, f32[4,8,128]{2,1,0:T(8,128)} %get-tuple-element.48.refs_1_.refs_9_.refs_10_.refs_5_, ...), custom_call_target="tpu_custom_call" | custom-call | tf_op jit(solution)/shard_map/within_chunks/pallas_call | solution.py:114
  22.3 7.8 %all-to-all-done.refs_7_.refs_1_ = bf16[32,64,128]{2,1,0:T(8,128)(2,1)} async-done(((bf16[32,64,128]{2,1,0:T(8,128)(2,1)}), bf16[32,64,128]{2,1,0:T(8,128)(2,1)}, u32[]{:S(2)}, u32[]{:S(2)}) %all-to-all-start) | async-done | bytes 524320 | tf_op jit(solution)/shard_map/all_to_all | solution.py:1031
  30.1 0.0 collective-permute-done.1.refs_3_
  30.1 0.0 collective-permute-done.2.refs_5_
  30.1 6.8 %activation_and_states.1 = (bf16[32,64,128]{2,1,0:T(8,128)(2,1)}, f32[1024,128]{1,0:T(8,128)}, f32[32,128]{1,0:T(8,128)}, f32[256,128]{1,0:T(8,128)}, f32[256,128]{1,0:T(8,128)}) custom-call(s32[1]{0:T(128)} %bitcast.refs_0_, s32[1]{0:T(128)} %bitcast.1.refs_1_, bf16[32,4224]{1,0:T(8,128)(2,1)} %get-tuple-element.45.refs_2_, ...), custom_call_target="tpu_custom_call" | custom-call | tf_op jit(solution)/shard_map/activation_and_states/pallas_call | solution.py:114
  36.9 0.0 copy-start.2
  36.9 4.6 %all-to-all-start.1 = ((bf16[32,64,128]{2,1,0:T(8,128)(2,1)}), bf16[32,64,128]{2,1,0:T(8,128)(2,1)}, u32[]{:S(2)}, u32[]{:S(2)}) async-start(bf16[32,64,128]{2,1,0:T(8,128)(2,1)} %get-tuple-element.57), calls=%async_computation.1 | async-start | bytes 1048576 | tf_op jit(solution)/shard_map/all_to_all | solution.py:1031
  41.5 0.0 copy-done.2
  41.5 0.1 collective-permute-start.5
  41.6 0.2 collective-permute-start.4
  41.9 1.6 %collective-permute-start.3 = (f32[32,128]{1,0:T(8,128)S(1)}, f32[32,128]{1,0:T(8,128)S(1)}, u32[]{:S(2)}, u32[]{:S(2)}) collective-permute-start(f32[32,128]{1,0:T(8,128)S(1)} %copy-done.2), channel_id=1, source_target_pairs={{0,1},{1,0},{2,3},{3,2},{4,5},{5,4},{6,7},{7,6},{8,9},{9,8},{10,11... | collective-permute-start | bytes 49160 | tf_op jit(solution)/shard_map/ppermute | solution.py:1052
  43.5 4.6 %input_spectrum.1 = (f32[1024,256]{1,0:T(8,128)}, f32[512,128]{1,0:T(8,128)}, f32[2,256,128]{2,1,0:T(8,128)}) custom-call(s32[1]{0:T(128)} %bitcast.refs_0_, bf16[32,64,128]{2,1,0:T(8,128)(2,1)} %all-to-all-done.refs_7_.refs_1_, bf16[512,256]{1,0:T(8,128)(2,1)} %constant.25.clone.refs_2_.refs_1_, bf16[512,256]{1,0:T(8,128)(2,1)} %constant.26.clone.refs_3_.refs_2_, ...), custom_call_target="tpu_custom_call" | custom-call | tf_op jit(solution)/shard_map/input_spectrum/pallas_call | solution.py:114
  48.1 0.0 collective-permute-done.5.refs_15_
  48.1 0.0 copy-start.3
  48.1 0.0 collective-permute-done.4.refs_14_
  48.1 0.0 copy-start.4
  48.1 0.0 collective-permute-done.3.refs_13_
  48.2 0.0 copy-start.5
  48.2 4.9 %all-to-all-done.1.refs_0_.refs_1_ = bf16[32,64,128]{2,1,0:T(8,128)(2,1)} async-done(((bf16[32,64,128]{2,1,0:T(8,128)(2,1)}), bf16[32,64,128]{2,1,0:T(8,128)(2,1)}, u32[]{:S(2)}, u32[]{:S(2)}) %all-to-all-start.1) | async-done | bytes 524320 | tf_op jit(solution)/shard_map/all_to_all | solution.py:1031
  53.1 0.0 copy-done.3
  53.1 0.0 copy-done.4
  53.1 0.0 copy-done.5
  53.1 8.0 %correlation.1 = (bf16[32,80,128]{2,1,0:T(8,128)(2,1)}, f32[8,128]{1,0:T(8,128)}) custom-call(bf16[32,64,128]{2,1,0:T(8,128)(2,1)} %all-to-all-done.1.refs_0_.refs_1_, bf16[512,256]{1,0:T(8,128)(2,1)} %constant.25.clone.refs_2_.refs_1_, bf16[512,256]{1,0:T(8,128)(2,1)} %constant.26.clone.refs_3_.refs_2_, f32[2,256,512]{2,1,0:T(8,128)} %constant.27.clone.refs_4_.refs_3_, ...), custom_call_target="tpu_custom_call" | custom-call | tf_op jit(solution)/shard_map/correlation/pallas_call | solution.py:114
  61.0 5.5 %all-to-all-start.2 = ((bf16[32,80,128]{2,1,0:T(8,128)(2,1)}), bf16[32,80,128]{2,1,0:T(8,128)(2,1)S(1)}, u32[]{:S(2)}, u32[]{:S(2)}) async-start(bf16[32,80,128]{2,1,0:T(8,128)(2,1)} %get-tuple-element.67), calls=%async_computation.2 | async-start | bytes 1310720 | tf_op jit(solution)/shard_map/all_to_all | solution.py:1031
  66.5 0.0 copy-start
  66.5 5.9 %signal_gradient.1 = (bf16[32,4096]{1,0:T(8,128)(2,1)}, f32[11,32,128]{2,1,0:T(8,128)}) custom-call(s32[1]{0:T(128)} %bitcast.refs_0_, bf16[32,64,128]{2,1,0:T(8,128)(2,1)} %all-to-all-done.1.refs_0_.refs_1_, f32[1024,128]{1,0:T(8,128)} %get-tuple-element.58.refs_2_, bf16[32,4096]{1,0:T(8,128)(2,1)} %refs_3_.5, f32[8,128]{1,0:T(8,128)} %get-tuple-element.63.refs_4_, ...), custom_call_target="tpu_custom_call" | custom-call | tf_op jit(solution)/shard_map/signal_gradient/pallas_call | solution.py:114
  72.4 8.3 %all-to-all-done.2.refs_2_ = bf16[32,80,128]{2,1,0:T(8,128)(2,1)S(1)} async-done(((bf16[32,80,128]{2,1,0:T(8,128)(2,1)}), bf16[32,80,128]{2,1,0:T(8,128)(2,1)S(1)}, u32[]{:S(2)}, u32[]{:S(2)}) %all-to-all-start.2) | async-done | bytes 655392 | tf_op jit(solution)/shard_map/all_to_all | solution.py:1031
  80.7 0.0 copy-done
  80.7 0.0 copy-start.1
  80.7 0.9 %copy-done.1 = f32[11,32,128]{2,1,0:T(8,128)S(1)} copy-done((f32[11,32,128]{2,1,0:T(8,128)S(1)}, f32[11,32,128]{2,1,0:T(8,128)}, u32[]{:S(2)}) %copy-start.1) | copy-done | bytes 180248
  81.6 1.8 %outputs.1 = (f32[32,4096]{1,0:T(8,128)}, f32[32,32]{1,0:T(8,128)}, f32[32,32]{1,0:T(8,128)}, f32[32,32]{1,0:T(8,128)}, f32[32,32]{1,0:T(8,128)}, /*index=5*/f32...) custom-call(s32[1]{0:T(128)S(6)} %copy.29.refs_0_, s32[1]{0:T(128)} %bitcast.1.refs_1_, ...), custom_call_target="tpu_custom_call" | custom-call | tf_op jit(solution)/shard_map/outputs/pallas_call | solution.py:114
Async XLA Ops:
  5.3 12.4 %collective-permute-start = (bf16[32,4224]{1,0:T(8,128)(2,1)}, bf16[32,4224]{1,0:T(8,128)(2,1)}, u32[]{:S(2)}, u32[]{:S(2)}) collective-permute-start(bf16[32,4224]{1,0:T(8,128)(2,1)} %get-tuple-element.45.refs_2_), channel_id=1, source_target_pairs={{0,2},{1,3},{2,0},{3,1},{4,6},{5,7},{6,4},{7,5},{8,10},{9,11},{10,... | collective-permute-start | bytes 811016 | tf_op jit(solution)/shard_map/ppermute | solution.py:1052
  7.0 23.1 %all-to-all-start = ((bf16[32,64,128]{2,1,0:T(8,128)(2,1)}), bf16[32,64,128]{2,1,0:T(8,128)(2,1)}, u32[]{:S(2)}, u32[]{:S(2)}) async-start(bf16[32,64,128]{2,1,0:T(8,128)(2,1)} %get-tuple-element.47.refs_0_.refs_8_), calls=%async_computation | async-start | bytes 1048576 | tf_op jit(solution)/shard_map/all_to_all | solution.py:1031
  17.7 12.4 %collective-permute-start.1 = (bf16[32,4224]{1,0:T(8,128)(2,1)}, bf16[32,4224]{1,0:T(8,128)(2,1)}, u32[]{:S(2)}, u32[]{:S(2)}) collective-permute-start(bf16[32,4224]{1,0:T(8,128)(2,1)} %get-tuple-element.45.refs_2_), channel_id=1, source_target_pairs={{0,1},{1,0},{2,3},{3,2},{4,5},{5,4},{6,7},{7,6},{8,9},{9,8},{10,11... | collective-permute-start | bytes 811016 | tf_op jit(solution)/shard_map/ppermute | solution.py:1052
  17.8 12.3 %collective-permute-start.2 = (bf16[32,4224]{1,0:T(8,128)(2,1)}, bf16[32,4224]{1,0:T(8,128)(2,1)}, u32[]{:S(2)}, u32[]{:S(2)}) collective-permute-start(bf16[32,4224]{1,0:T(8,128)(2,1)} %collective-permute-done.refs_4_), channel_id=1, source_target_pairs={{0,1},{1,0},{2,3},{3,2},{4,5},{5,4},{6,7},{7,6},{8,9},{9,8},{10,11... | collective-permute-start | bytes 811016 | tf_op jit(solution)/shard_map/ppermute | solution.py:1052
  36.9 4.7 %copy-start.2 = (f32[32,128]{1,0:T(8,128)S(1)}, f32[32,128]{1,0:T(8,128)}, u32[]{:S(2)}) copy-start(f32[32,128]{1,0:T(8,128)} %get-tuple-element.59.refs_7_.refs_12_) | copy-start | bytes 49156
  36.9 16.2 %all-to-all-start.1 = ((bf16[32,64,128]{2,1,0:T(8,128)(2,1)}), bf16[32,64,128]{2,1,0:T(8,128)(2,1)}, u32[]{:S(2)}, u32[]{:S(2)}) async-start(bf16[32,64,128]{2,1,0:T(8,128)(2,1)} %get-tuple-element.57), calls=%async_computation.1 | async-start | bytes 1048576 | tf_op jit(solution)/shard_map/all_to_all | solution.py:1031
  41.5 6.6 %collective-permute-start.5 = (f32[32,128]{1,0:T(8,128)S(1)}, f32[32,128]{1,0:T(8,128)S(1)}, u32[]{:S(2)}, u32[]{:S(2)}) collective-permute-start(f32[32,128]{1,0:T(8,128)S(1)} %copy-done.2), channel_id=1, source_target_pairs={{0,3},{1,2},{2,1},{3,0},{4,7},{5,6},{6,5},{7,4},{8,11},{9,10},{10,... | collective-permute-start | bytes 49160 | tf_op jit(solution)/shard_map/ppermute | solution.py:1052
  41.6 6.5 %collective-permute-start.4 = (f32[32,128]{1,0:T(8,128)S(1)}, f32[32,128]{1,0:T(8,128)S(1)}, u32[]{:S(2)}, u32[]{:S(2)}) collective-permute-start(f32[32,128]{1,0:T(8,128)S(1)} %copy-done.2), channel_id=1, source_target_pairs={{0,2},{1,3},{2,0},{3,1},{4,6},{5,7},{6,4},{7,5},{8,10},{9,11},{10,... | collective-permute-start | bytes 49160 | tf_op jit(solution)/shard_map/ppermute | solution.py:1052
  41.9 6.3 %collective-permute-start.3 = (f32[32,128]{1,0:T(8,128)S(1)}, f32[32,128]{1,0:T(8,128)S(1)}, u32[]{:S(2)}, u32[]{:S(2)}) collective-permute-start(f32[32,128]{1,0:T(8,128)S(1)} %copy-done.2), channel_id=1, source_target_pairs={{0,1},{1,0},{2,3},{3,2},{4,5},{5,4},{6,7},{7,6},{8,9},{9,8},{10,11... | collective-permute-start | bytes 49160 | tf_op jit(solution)/shard_map/ppermute | solution.py:1052
  48.1 4.9 %copy-start.3 = (f32[32,128]{1,0:T(8,128)}, f32[32,128]{1,0:T(8,128)S(1)}, u32[]{:S(2)}) copy-start(f32[32,128]{1,0:T(8,128)S(1)} %collective-permute-done.5.refs_15_) | copy-start | bytes 49156
  48.1 4.9 %copy-start.4 = (f32[32,128]{1,0:T(8,128)}, f32[32,128]{1,0:T(8,128)S(1)}, u32[]{:S(2)}) copy-start(f32[32,128]{1,0:T(8,128)S(1)} %collective-permute-done.4.refs_14_) | copy-start | bytes 49156
  48.2 4.9 %copy-start.5 = (f32[32,128]{1,0:T(8,128)}, f32[32,128]{1,0:T(8,128)S(1)}, u32[]{:S(2)}) copy-start(f32[32,128]{1,0:T(8,128)S(1)} %collective-permute-done.3.refs_13_) | copy-start | bytes 49156
  61.0 19.7 %all-to-all-start.2 = ((bf16[32,80,128]{2,1,0:T(8,128)(2,1)}), bf16[32,80,128]{2,1,0:T(8,128)(2,1)S(1)}, u32[]{:S(2)}, u32[]{:S(2)}) async-start(bf16[32,80,128]{2,1,0:T(8,128)(2,1)} %get-tuple-element.67), calls=%async_computation.2 | async-start | bytes 1310720 | tf_op jit(solution)/shard_map/all_to_all | solution.py:1031
  66.5 14.2 %copy-start = (f32[2,32,128]{2,1,0:T(8,128)S(1)}, f32[2,32,128]{2,1,0:T(8,128)}, u32[]{:S(2)}) copy-start(f32[2,32,128]{2,1,0:T(8,128)} %get-tuple-element.49.refs_2_.refs_10_.refs_9_.refs_6_.refs_4_) | copy-start | bytes 98308
  80.7 0.9 %copy-start.1 = (f32[11,32,128]{2,1,0:T(8,128)S(1)}, f32[11,32,128]{2,1,0:T(8,128)}, u32[]{:S(2)}) copy-start(f32[11,32,128]{2,1,0:T(8,128)} %get-tuple-element.68.refs_3_) | copy-start | bytes 540676

commit v3 on v2

--- a/solution.py
+++ b/solution.py
@@ -90,8 +90,8 @@
 
 
 def waiting(copies):
-    def wait():
-        for copy in copies:
+    def wait(first=0, last=None):
+        for copy in copies[first:last]:
             copy.wait()
 
     return wait
@@ -99,25 +99,53 @@
 
 def staged(
     kernel, scalars, plain, small, *, out_specs, out_shape, scratch_shapes, name,
-    plain_spec=HBM, limit=GRANT,
+    plain_spec=HBM, limit=GRANT, eager=None, early=(),
 ):
     heads, outs = len(scalars) + len(plain), len(out_shape)
 
     def body(*refs):
         given, rest = refs[:heads], refs[heads:]
         sources, rest = rest[: len(small)], rest[len(small) :]
-        results, rest = rest[:outs], rest[outs:]
+        results, rest = list(rest[:outs]), rest[outs:]
         held, sems, rest = rest[: len(small)], rest[len(small)], rest[len(small) + 1 :]
-        copies = started(sems, *zip(sources, held))
-        kernel(waiting(copies), *given, *held, *results, *rest)
+        written, out_sems, rest = rest[: len(early)], rest[len(early)], rest[len(early) + 1 :]
+        copies = [
+            pltpu.make_async_copy(a, b, sems.at[k]) for k, (a, b) in enumerate(zip(sources, held))
+        ]
+        leaving = {
+            k: pltpu.make_async_copy(written[n], results[k], out_sems.at[n])
+            for n, k in enumerate(early)
+        }
+        for n, k in enumerate(early):
+            results[k] = written[n]
+        gone = set()
+
+        def start(first=0, last=None):
+            for copy in copies[first:last]:
+                copy.start()
+
+        def store(*which):
+            for k in which:
+                leaving[k].start()
+                gone.add(k)
+
+        wait = waiting(copies)
+        wait.start, wait.store = start, store
+        start(0, eager)
+        kernel(wait, *given, *held, *results, *rest)
+        store(*[k for k in early if k not in gone])
+        for copy in leaving.values():
+            copy.wait()
 
     return pl.pallas_call(
         body,
         in_specs=[SMEM] * len(scalars) + [plain_spec] * len(plain) + [HBM] * len(small),
-        out_specs=out_specs,
+        out_specs=[HBM if k in early else spec for k, spec in enumerate(out_specs)],
         out_shape=out_shape,
         scratch_shapes=[pltpu.VMEM(a.shape, a.dtype) for a in small]
         + [pltpu.SemaphoreType.DMA((len(small),))]
+        + [pltpu.VMEM(out_shape[k].shape, out_shape[k].dtype) for k in early]
+        + [pltpu.SemaphoreType.DMA((max(len(early), 1),))]
         + scratch_shapes,
         compiler_params=pltpu.CompilerParams(vmem_limit_bytes=int(limit * 1024 * 1024)),
         name=name,
@@ -190,7 +218,7 @@
         ],
         0,
     )
-    return dot3(split(left), split(table), NT)
+    return dot3(split(left), table, NT)
 
 
 def scan_states(sr_ref, si_ref, power_r, power_i, order):
@@ -265,6 +293,7 @@
     terms = mode_terms(*raw)
     for k in range(4):
         terms_ref[k] = terms[k]
+    wait_small.store(4, 5)
     decay, turn = terms[0], terms[1]
     doubles = doublings(decay, turn)
     loads[0].wait()
@@ -290,6 +319,7 @@
         si_ref[pl.ds(g, CK, stride=GROUPS), :] = pi + level * jnp.sum(fi, 0, keepdims=True)
     zr, zi = power(decay, turn, float(LN))
     hr, hi = scan_states(sr_ref, si_ref, zr, zi, range(CK))
+    wait_small.store(2, 3)
     packed = packed_states(hr, hi)
     for d in range(RANKS):
         send_ref[d, CK:, :] = packed
@@ -337,6 +367,7 @@
             pltpu.SemaphoreType.DMA((3,)),
         ],
         name="block_states",
+        early=(2, 3, 4, 5),
     )
 
 
@@ -353,11 +384,39 @@
     return size * c, size * s
 
 
+def pull_table(size_ref, damping_ref, frequency_ref, re_ref, im_ref, pull_ref):
+    def tiled(values):
+        return jnp.concatenate([values] * LANE_CH, 1)
+
+    size = jnp.broadcast_to(as_column(jnp.exp(size_ref[...])), (CH, LN))
+    raw = [size] + [tiled(r[...]) for r in (damping_ref, frequency_ref, re_ref, im_ref)]
+    (d, th, mr, mi), pull = jax.vjp(mode_terms, *raw)
+    zero = jnp.zeros((CH, LN), F32)
+    pulled = [
+        pull((zero, zero, zero + 2.0, zero)),
+        pull((zero, zero, zero, zero - 2.0)),
+        pull((-2.0 * mr, -2.0 * mi, zero, zero)),
+        pull((2.0 * mi, -2.0 * mr, zero, zero)),
+    ]
+    inverse = 1.0 / (raw[1] * raw[1] + raw[2] * raw[2])
+    qr, qi = cmul(raw[3], raw[4], raw[1] * inverse, raw[2] * inverse)
+    one_r, one_i = power(d, th, 1.0)
+    er, ei = cmul(qr, qi, one_r, one_i)
+    first_lanes = lane_block(zero) == 0
+    for k, p in enumerate(pulled):
+        pull_ref[k] = by_block(p[1:])
+        pull_ref[4 + k] = jnp.where(first_lanes, p[0] * raw[0], 0.0)
+    for k, value in enumerate((2.0 * qr, -2.0 * er, 2.0 * ei)):
+        pull_ref[8 + k] = jnp.where(first_lanes, value, 0.0)
+
+
 def within_kernel(
-    wait_small, x_hbm, terms_ref, wide_ref, out_ref, far_r, far_i, step_r, step_i, x_ref, sems
+    wait_small, x_hbm, terms_ref, wide_ref, size_ref, damping_ref, frequency_ref, re_ref, im_ref,
+    out_ref, far_r, far_i, step_r, step_i, pull_ref, x_ref, sems,
 ):
     loads = started(sems, (x_hbm.at[:, pl.ds(0, CK), :], x_ref))
     wait_small()
+    pull_table(size_ref, damping_ref, frequency_ref, re_ref, im_ref, pull_ref)
     terms = terms_ref[0], terms_ref[1], terms_ref[2], terms_ref[3]
     decay, turn = terms[0], terms[1]
     near = [far_power(decay, turn, float(b)) for b in range(4)]
@@ -389,19 +448,20 @@
             )
 
 
-def within(send, terms, wide):
+def within(send, terms, wide, raw):
     return staged(
         within_kernel,
         (),
         (send,),
-        (terms, wide),
-        out_specs=[VMEM] * 5,
+        (terms, wide, *raw),
+        out_specs=[VMEM] * 6,
         out_shape=(
             jax.ShapeDtypeStruct((CH * CK, LN), F32),
             jax.ShapeDtypeStruct((RANKS, GROUPS, LN), F32),
             jax.ShapeDtypeStruct((RANKS, GROUPS, LN), F32),
             jax.ShapeDtypeStruct((CK, GROUPS, LN), F32),
             jax.ShapeDtypeStruct((CK, GROUPS, LN), F32),
+            jax.ShapeDtypeStruct((11, CH, LN), F32),
         ),
         scratch_shapes=[pltpu.VMEM((CH, CK, LN), BF16), pltpu.SemaphoreType.DMA((1,))],
         name="within_chunks",
@@ -442,16 +502,17 @@
 def second_kernel(
     wait_small, me_ref, group_ref, c0h, c1h, c2h, c3h, out_hbm, got_hbm, x_hbm, terms_ref, wide_ref, far_r,
     far_i, step_r, step_i, sr_in, si_in, send_hbm, grad_hbm, mix_ref, sr_ref, si_ref,
-    cot_ref, flat_ref, out_ref, got_ref, x_ref, act_ref, activation_ref, send_ref, grad_ref, sems, out_sems,
+    cot_ref, flat_ref, out_ref, got_ref, x_ref, act_ref, activation_ref, send_ref, grad_ref, table_ref, sems, out_sems,
 ):
     loads = started(
         sems,
+        *[(c, cot_ref.at[pl.ds(m * CH, CH), :]) for m, c in enumerate((c0h, c1h, c2h, c3h))],
         (got_hbm.at[:, pl.ds(CK, CK), :], got_ref),
         (x_hbm.at[:, pl.ds(0, CK), :], x_ref),
         (out_hbm, out_ref),
-        *[(c, cot_ref.at[pl.ds(m * CH, CH), :]) for m, c in enumerate((c0h, c1h, c2h, c3h))],
-    )
-    wait_small()
+    )
+    wait_small.start(1)
+    wait_small(0, 1)
     me = me_ref[0]
     terms = terms_ref[0], terms_ref[1], terms_ref[2], terms_ref[3]
     decay, turn = terms[0], terms[1]
@@ -459,20 +520,26 @@
     zr, zi = power(decay, turn, float(LN))
     one_r, one_i = power(decay, turn, 1.0)
     ur, ui = cmul(2.0 * terms[2], 2.0 * terms[3], one_r, one_i)
-    loads[0].wait()
+    for g in range(GROUPS):
+        er, ei = rising(decay, turn, doubles, g)
+        wr, wi = cmul(er, ei, ur[g : g + 1], ui[g : g + 1])
+        table_ref[4 * g], table_ref[4 * g + 1] = split(jnp.concatenate([er, ei], 1))
+        table_ref[4 * g + 2], table_ref[4 * g + 3] = split(jnp.concatenate([wr, wi], 1))
+    for copy in loads[:4]:
+        copy.wait()
+    mixed_back(group_ref[0], cot_ref, act_ref)
+    wait_small(1)
+    loads[4].wait()
     start = entering(lambda d: unpacked_states(got_ref[d]), far_r, far_i, lambda d: me - 1 - d)
     add_entering(sr_ref, si_ref, sr_in, si_in, step_r, step_i, start, range(CK))
-    for copy in loads[3:]:
-        copy.wait()
-    mixed_back(group_ref[0], cot_ref, act_ref)
-    for copy in loads[1:3]:
+    for copy in loads[5:]:
         copy.wait()
     stores = []
     for g in range(GROUPS):
         every = pl.ds(g, CK, stride=GROUPS)
-        er, ei = rising(decay, turn, doubles, g)
-        wr, wi = cmul(er, ei, ur[g : g + 1], ui[g : g + 1])
-        inter = spread_group(sr_ref[every, :], si_ref[every, :], jnp.concatenate([wr, wi], 1))
+        inter = spread_group(
+            sr_ref[every, :], si_ref[every, :], (table_ref[4 * g + 2], table_ref[4 * g + 3])
+        )
         left = []
         for k in range(LANE_CH):
             c = g * LANE_CH + k
@@ -493,11 +560,19 @@
             )
         )
         stores[-1].start()
-        products = dot3(split(jnp.concatenate(left, 0)), split(jnp.concatenate([er, ei], 1)))
+        mine = pl.ds(g * LN, LN)
+        stores.append(
+            pltpu.make_async_copy(
+                grad_ref.at[mine, :], grad_hbm.at[mine, :], out_sems.at[GROUPS + 1 + g]
+            )
+        )
+        stores[-1].start()
+        products = dot3(split(jnp.concatenate(left, 0)), (table_ref[4 * g], table_ref[4 * g + 1]))
         pr, pi = gather_group(products)
         sr_ref[every, :] = pr
         si_ref[every, :] = pi
     hr, hi = scan_states(sr_ref, si_ref, zr, zi, range(CK - 1, -1, -1))
+    wait_small.store(3, 4)
     packed = packed_states(hr, hi)
     for d in range(RANKS):
         send_ref[d, CK:, :] = packed
@@ -508,11 +583,10 @@
         )
     )
     stores[-1].start()
-    stores.append(pltpu.make_async_copy(grad_ref, grad_hbm, out_sems.at[GROUPS + 1]))
-    stores[-1].start()
     for i in range(CK):
         flat_ref[:, i * LN : (i + 1) * LN] = activation_ref[pl.ds(i, CH, stride=CK), :].astype(BF16)
     mix_ref[...] = dot(flat_ref[...], cot_ref[:, :BLOCK], NT)
+    wait_small.store(2)
     for copy in stores:
         copy.wait()
 
@@ -541,43 +615,19 @@
             pltpu.VMEM((CH * CK, LN), F32),
             pltpu.VMEM((RANKS, SEND2, LN), BF16),
             pltpu.VMEM((CH * CK, LN), F32),
+            pltpu.VMEM((4 * GROUPS, LN, 2 * LN), BF16),
             pltpu.SemaphoreType.DMA((7,)),
-            pltpu.SemaphoreType.DMA((GROUPS + 2,)),
+            pltpu.SemaphoreType.DMA((2 * GROUPS + 1,)),
         ],
         name="activation_and_states",
-    )
-
-
-def pull_table(size_ref, damping_ref, frequency_ref, re_ref, im_ref, pull_ref):
-    def tiled(values):
-        return jnp.concatenate([values] * LANE_CH, 1)
-
-    size = jnp.broadcast_to(as_column(jnp.exp(size_ref[...])), (CH, LN))
-    raw = [size] + [tiled(r[...]) for r in (damping_ref, frequency_ref, re_ref, im_ref)]
-    (d, th, mr, mi), pull = jax.vjp(mode_terms, *raw)
-    zero = jnp.zeros((CH, LN), F32)
-    pulled = [
-        pull((zero, zero, zero + 2.0, zero)),
-        pull((zero, zero, zero, zero - 2.0)),
-        pull((-2.0 * mr, -2.0 * mi, zero, zero)),
-        pull((2.0 * mi, -2.0 * mr, zero, zero)),
-    ]
-    inverse = 1.0 / (raw[1] * raw[1] + raw[2] * raw[2])
-    qr, qi = cmul(raw[3], raw[4], raw[1] * inverse, raw[2] * inverse)
-    one_r, one_i = power(d, th, 1.0)
-    er, ei = cmul(qr, qi, one_r, one_i)
-    first_lanes = lane_block(zero) == 0
-    for k, p in enumerate(pulled):
-        pull_ref[k] = by_block(p[1:])
-        pull_ref[4 + k] = jnp.where(first_lanes, p[0] * raw[0], 0.0)
-    for k, value in enumerate((2.0 * qr, -2.0 * er, 2.0 * ei)):
-        pull_ref[8 + k] = jnp.where(first_lanes, value, 0.0)
+        eager=1,
+        early=(2, 3, 4),
+    )
 
 
 def signal_kernel(
     wait_small, me_ref, got_hbm, send_hbm, cot_hbm, after_hbm, terms_ref, wide_ref, far_r, far_i,
-    step_r, step_i, sr_in, si_in, size_ref, damping_ref, frequency_ref, re_ref, im_ref,
-    out_ref, pull_ref, sr_ref, si_ref, rows_ref, got_ref, send_ref, cot_ref, sems,
+    step_r, step_i, sr_in, si_in, out_ref, sr_ref, si_ref, rows_ref, got_ref, send_ref, cot_ref, sems,
 ):
     loads = started(
         sems,
@@ -586,7 +636,6 @@
         (cot_hbm, cot_ref),
     )
     wait_small()
-    pull_table(size_ref, damping_ref, frequency_ref, re_ref, im_ref, pull_ref)
     me = me_ref[0]
     terms = terms_ref[0], terms_ref[1], terms_ref[2], terms_ref[3]
     decay, turn = terms[0], terms[1]
@@ -602,7 +651,7 @@
         every = pl.ds(g, CK, stride=GROUPS)
         fr, fi = falling(decay, turn, doubles, g)
         wr, wi = cmul(fr, fi, ur[g : g + 1], ui[g : g + 1])
-        inter = spread_group(sr_ref[every, :], si_ref[every, :], jnp.concatenate([wr, wi], 1))
+        inter = spread_group(sr_ref[every, :], si_ref[every, :], split(jnp.concatenate([wr, wi], 1)))
         taps = group_taps(terms, rising(decay, turn, doubles, g), g)
         for k in range(LANE_CH):
             c = g * LANE_CH + k
@@ -619,16 +668,15 @@
         ).astype(BF16)
 
 
-def signal_grad(me, got, send, terms, wide, far, steps, sr, si, raw, cotangent, after):
+def signal_grad(me, got, send, terms, wide, far, steps, sr, si, cotangent, after):
     return staged(
         signal_kernel,
         (me,),
         (got, send, cotangent, after),
-        (terms, wide, far[0], far[1], steps[0], steps[1], sr, si, *raw),
-        out_specs=[VMEM] * 2,
+        (terms, wide, far[0], far[1], steps[0], steps[1], sr, si),
+        out_specs=[VMEM],
         out_shape=(
             jax.ShapeDtypeStruct((CH, BLOCK), BF16),
-            jax.ShapeDtypeStruct((11, CH, LN), F32),
         ),
         scratch_shapes=[
             pltpu.VMEM((CK * GROUPS, LN), F32),
@@ -834,7 +882,7 @@
 
 def correlate_kernel(
     wait_small, got_hbm, d1h_hbm, d1l_hbm, twiddle_hbm, d2h_hbm, d2l_hbm, spec_hbm, d1th_hbm, d1tl_hbm,
-    column_hbm, turn_hbm, steps_ref, m0, m1, m2, m3, send_hbm, after_ref,
+    column_hbm, turn_hbm, steps_ref, m0, m1, m2, m3, send_hbm,
     got_ref, d1h, d1l, twiddle, d2h, d2l, spec_ref, d1th, d1tl, column_ref, turn_ref,
     rows_ref, send_ref, sems, out_sems,
 ):
@@ -872,12 +920,14 @@
             ]
     for d in range(RANKS):
         send_ref[d, :CK, :] = rows_ref[d * CK : (d + 1) * CK, :].astype(BF16)
-    stores.append(
-        pltpu.make_async_copy(
-            send_ref.at[:, pl.ds(0, CK), :], send_hbm.at[:, pl.ds(0, CK), :], out_sems.at[1]
-        )
-    )
-    stores[-1].start()
+        if d % 8 == 7:
+            part = pl.ds(d - 7, 8), pl.ds(0, CK)
+            stores.append(
+                pltpu.make_async_copy(
+                    send_ref.at[part], send_hbm.at[part], out_sems.at[2 + d // 8]
+                )
+            )
+            stores[-1].start()
     column = split(column_ref[...])
     inner = dot3(split(kernel_rows), column)
     g_inner = dot2(g_rows.astype(BF16), column)
@@ -898,7 +948,6 @@
         lanes == 1, jnp.sum(total(g_rows), 1, keepdims=True), 0.0
     )
     small = jnp.concatenate([u, v, su, sv, gu, gv, scalars, jnp.zeros((1, LN), F32)], 0)
-    after_ref[...] = small
     high, low = split(jnp.concatenate([small, small], 0))
     upper = lax.broadcasted_iota(jnp.int32, (16, LN), 0) < 8
     packed = jnp.where(upper, high.astype(F32), low.astype(F32)).astype(BF16)
@@ -907,7 +956,7 @@
     stores.append(
         pltpu.make_async_copy(
             send_ref.at[:, pl.ds(2 * CK, 16), :], send_hbm.at[:, pl.ds(2 * CK, 16), :],
-            out_sems.at[2],
+            out_sems.at[1],
         )
     )
     stores[-1].start()
@@ -922,10 +971,9 @@
         (),
         (got, d1h, d1l, twiddle, d2h, d2l, spec, d1th, d1tl, column, turns),
         (steps, *mixes),
-        out_specs=[ANY, VMEM],
+        out_specs=[ANY],
         out_shape=(
             jax.ShapeDtypeStruct((RANKS, SEND3, LN), BF16),
-            jax.ShapeDtypeStruct((8, LN), F32),
         ),
         scratch_shapes=[
             pltpu.VMEM((RANKS, CK, LN), BF16),
@@ -942,7 +990,7 @@
             pltpu.VMEM((RANKS * CK, LN), F32),
             pltpu.VMEM((RANKS, SEND3, LN), BF16),
             pltpu.SemaphoreType.DMA((11,)),
-            pltpu.SemaphoreType.DMA((3,)),
+            pltpu.SemaphoreType.DMA((6,)),
         ],
         name="correlation",
     )
@@ -1058,7 +1106,8 @@
     got1 = exchange(send1)
     own, across = lax.optimization_barrier((own, swap(own, 2)))
     parts = (own, swap(own, 1), across, swap(across, 1))
-    out, far_r, far_i, step_r, step_i = within(send1, terms, wide)
+    raw = (log_step[None], damping, frequency, coef_re, coef_im)
+    out, far_r, far_i, step_r, step_i, pull = within(send1, terms, wide, raw)
     far = (far_r, far_i)
     steps = (step_r, step_i)
     send2, grad, mix, br, bi = second(
@@ -1067,11 +1116,10 @@
     got2 = exchange(send2)
     mixes = [mix] + [swap(mix, m) for m in range(1, 4)]
     spec, column, turns = spectrum(me, got1, mix, wide, terms, tables)
-    send3, after = correlate(got2, spec, tables, column, turns, mixes)
+    (send3,) = correlate(got2, spec, tables, column, turns, mixes)
     got3 = exchange(send3)
-    grad_signal, pull = signal_grad(
-        me, got2, grad, terms, wide, far, steps, br, bi,
-        (log_step[None], damping, frequency, coef_re, coef_im), cotangent, after,
+    (grad_signal,) = signal_grad(
+        me, got2, grad, terms, wide, far, steps, br, bi, cotangent, send3
     )
     kernel, g_damping, g_frequency, g_re, g_im, g_size, g_skip, g_mix, g_table = outputs(
         diffusion_step, group, got3, pull, wide, embed_table.shape[0]

time: 84.3 us -> 81.1 us (0.962)
  Pallas kernels: 35 us -> 33.2 us
  local copies, waits for them, and re-layouts: 0.95 us -> 0.04 us
    pallas_call x7, Pallas kernels: 35 us -> 33.2 us  [staged(): pl.pallas_call(body, in_specs=[SMEM] * len(scalars) + [plain_spec] * len(...]
    unnamed x12, local copies, waits for them, and re-layouts: 0.95 us -> 0.04 us
  transfers between devices with their start and end apart: 9 -> 9, of which waited for: 3 -> 3; matrix products, arithmetic and copies ran while one was open for 0% -> 0% of each run, Pallas kernels for 17% -> 18%
where the time goes in v3:
time: 81.1 us; the launch traced here: 80.6 us
  Pallas kernels  33.2 us (41%)
  starting transfers between devices  25 us (31%)
  waiting for transfers between devices  20.7 us (26%)
  between operations  1.63 us (2%)
    pallas_call x7, Pallas kernels, staged(): pl.pallas_call(body, in_specs=[SMEM] * len(scalars) + [plain_spec] * len(...  33.2 us
    all_to_all x3, starting transfers between devices, exchange(): return lax.all_to_all(values, 'tm', split_axis=0, concat_axis=0, tiled=True)  20.7 us
    all_to_all x3, waiting for transfers between devices, exchange(): return lax.all_to_all(values, 'tm', split_axis=0, concat_axis=0, tiled=True)  20.7 us
    ppermute x6, starting transfers between devices, swap(): return lax.ppermute(values, 'chan', [(i, i ^ mask) for i in range(4)])  4.26 us
  transfers between devices with their start and end apart: 9, of which 3 were waited for; matrix products, arithmetic and copies ran while one was open for 0% of the time, Pallas kernels for 18%

profile of v3, /device:TPU:0, one launch (start us, length us, event | category | flops | bytes accessed | tf_op | source)
XLA Modules:
  0.0 80.6 jit_solution(13122328731532442862)
XLA Ops:
  1.3 3.4 %block_states.1 = (bf16[32,64,128]{2,1,0:T(8,128)(2,1)}, bf16[32,4224]{1,0:T(8,128)(2,1)}, f32[256,128]{1,0:T(8,128)}, f32[256,128]{1,0:T(8,128)}, f32[4,8,128]{2,1,0:T(8,128)}, /*index=5*/f32[2,32,128]{2,1,0:T(8,128)}) custom-call(s32[1]{0:T(128)S(6)} %copy.29.refs_0_, bf16[32,4096]{1,0:T(8,128)(2,1)} %refs_1_.2, bf16[32,4096]{1,0:T(8,128)(2,1)} %refs_3_.5, ...), custom_call_target="tpu_custom_call" | custom-call | tf_op jit(solution)/shard_map/block_states/pallas_call | solution.py:140
  4.7 1.7 %collective-permute-start = (bf16[32,4224]{1,0:T(8,128)(2,1)}, bf16[32,4224]{1,0:T(8,128)(2,1)}, u32[]{:S(2)}, u32[]{:S(2)}) collective-permute-start(bf16[32,4224]{1,0:T(8,128)(2,1)} %get-tuple-element.42.refs_2_), channel_id=1, source_target_pairs={{0,2},{1,3},{2,0},{3,1},{4,6},{5,7},{6,4},{7,5},{8,10},{9,11},{10,... | collective-permute-start | bytes 811016 | tf_op jit(solution)/shard_map/ppermute | solution.py:1100
  6.4 10.6 %all-to-all-start = ((bf16[32,64,128]{2,1,0:T(8,128)(2,1)}), bf16[32,64,128]{2,1,0:T(8,128)(2,1)}, u32[]{:S(2)}, u32[]{:S(2)}) async-start(bf16[32,64,128]{2,1,0:T(8,128)(2,1)} %get-tuple-element.44.refs_0_.refs_8_), calls=%async_computation | async-start | bytes 1048576 | tf_op jit(solution)/shard_map/all_to_all | solution.py:1079
  17.0 0.0 collective-permute-done.refs_4_
  17.1 0.1 collective-permute-start.1
  17.1 0.5 collective-permute-start.2
  17.6 4.5 %within_chunks.1 = (f32[1024,128]{1,0:T(8,128)}, f32[32,8,128]{2,1,0:T(8,128)}, f32[32,8,128]{2,1,0:T(8,128)}, f32[32,8,128]{2,1,0:T(8,128)}, f32[32,8,128]{2,1,0:T(8,128)}, /*index=5*/f32[11,32,128]{2,1,0:T(8,128)}) custom-call(bf16[32,64,128]{2,1,0:T(8,128)(2,1)} %get-tuple-element.44.refs_0_.refs_8_, ...), custom_call_target="tpu_custom_call" | custom-call | tf_op jit(solution)/shard_map/within_chunks/pallas_call | solution.py:140
  22.2 7.3 %all-to-all-done.refs_7_.refs_1_ = bf16[32,64,128]{2,1,0:T(8,128)(2,1)} async-done(((bf16[32,64,128]{2,1,0:T(8,128)(2,1)}), bf16[32,64,128]{2,1,0:T(8,128)(2,1)}, u32[]{:S(2)}, u32[]{:S(2)}) %all-to-all-start) | async-done | bytes 524320 | tf_op jit(solution)/shard_map/all_to_all | solution.py:1079
  29.5 0.0 collective-permute-done.1.refs_3_
  29.5 0.0 collective-permute-done.2.refs_5_
  29.5 5.8 %activation_and_states.1 = (bf16[32,64,128]{2,1,0:T(8,128)(2,1)}, f32[1024,128]{1,0:T(8,128)}, f32[32,128]{1,0:T(8,128)}, f32[256,128]{1,0:T(8,128)}, f32[256,128]{1,0:T(8,128)}) custom-call(s32[1]{0:T(128)} %bitcast.refs_0_, s32[1]{0:T(128)} %bitcast.1.refs_1_, bf16[32,4224]{1,0:T(8,128)(2,1)} %get-tuple-element.42.refs_2_, ...), custom_call_target="tpu_custom_call" | custom-call | tf_op jit(solution)/shard_map/activation_and_states/pallas_call | solution.py:140
  35.3 0.0 copy-start.2
  35.3 4.6 %all-to-all-start.1 = ((bf16[32,64,128]{2,1,0:T(8,128)(2,1)}), bf16[32,64,128]{2,1,0:T(8,128)(2,1)}, u32[]{:S(2)}, u32[]{:S(2)}) async-start(bf16[32,64,128]{2,1,0:T(8,128)(2,1)} %get-tuple-element.54), calls=%async_computation.1 | async-start | bytes 1048576 | tf_op jit(solution)/shard_map/all_to_all | solution.py:1079
  39.9 0.0 copy-done.2
  39.9 0.1 collective-permute-start.5
  40.0 0.2 collective-permute-start.4
  40.2 1.6 %collective-permute-start.3 = (f32[32,128]{1,0:T(8,128)S(1)}, f32[32,128]{1,0:T(8,128)S(1)}, u32[]{:S(2)}, u32[]{:S(2)}) collective-permute-start(f32[32,128]{1,0:T(8,128)S(1)} %copy-done.2), channel_id=1, source_target_pairs={{0,1},{1,0},{2,3},{3,2},{4,5},{5,4},{6,7},{7,6},{8,9},{9,8},{10,11... | collective-permute-start | bytes 49160 | tf_op jit(solution)/shard_map/ppermute | solution.py:1100
  41.9 4.6 %input_spectrum.1 = (f32[1024,256]{1,0:T(8,128)}, f32[512,128]{1,0:T(8,128)}, f32[2,256,128]{2,1,0:T(8,128)}) custom-call(s32[1]{0:T(128)} %bitcast.refs_0_, bf16[32,64,128]{2,1,0:T(8,128)(2,1)} %all-to-all-done.refs_7_.refs_1_, bf16[512,256]{1,0:T(8,128)(2,1)} %constant.25.clone.refs_2_.refs_1_, bf16[512,256]{1,0:T(8,128)(2,1)} %constant.26.clone.refs_3_.refs_2_, ...), custom_call_target="tpu_custom_call" | custom-call | tf_op jit(solution)/shard_map/input_spectrum/pallas_call | solution.py:140
  46.5 0.0 collective-permute-done.5.refs_15_
  46.5 0.0 copy-start.3
  46.5 0.0 collective-permute-done.4.refs_14_
  46.5 0.0 copy-start.4
  46.6 0.0 collective-permute-done.3.refs_13_
  46.6 0.0 copy-start.5
  46.6 4.9 %all-to-all-done.1.refs_0_.refs_1_ = bf16[32,64,128]{2,1,0:T(8,128)(2,1)} async-done(((bf16[32,64,128]{2,1,0:T(8,128)(2,1)}), bf16[32,64,128]{2,1,0:T(8,128)(2,1)}, u32[]{:S(2)}, u32[]{:S(2)}) %all-to-all-start.1) | async-done | bytes 524320 | tf_op jit(solution)/shard_map/all_to_all | solution.py:1079
  51.4 0.0 copy-done.3
  51.4 0.0 copy-done.4
  51.5 0.0 copy-done.5
  51.5 7.4 %correlation.1.refs_4_ = bf16[32,80,128]{2,1,0:T(8,128)(2,1)} custom-call(bf16[32,64,128]{2,1,0:T(8,128)(2,1)} %all-to-all-done.1.refs_0_.refs_1_, bf16[512,256]{1,0:T(8,128)(2,1)} %constant.25.clone.refs_2_.refs_1_, bf16[512,256]{1,0:T(8,128)(2,1)} %constant.26.clone.refs_3_.refs_2_, f32[2,256,512]{2,1,0:T(8,128)} %constant.27.clone.refs_4_.refs_3_, ...), custom_call_target="tpu_custom_call" | custom-call | tf_op jit(solution)/shard_map/correlation/pallas_call | solution.py:140
  58.9 5.5 %all-to-all-start.2 = ((bf16[32,80,128]{2,1,0:T(8,128)(2,1)}), bf16[32,80,128]{2,1,0:T(8,128)(2,1)S(1)}, u32[]{:S(2)}, u32[]{:S(2)}) async-start(bf16[32,80,128]{2,1,0:T(8,128)(2,1)} %correlation.1.refs_4_), calls=%async_computation.2 | async-start | bytes 1310720 | tf_op jit(solution)/shard_map/all_to_all | solution.py:1079
  64.3 0.0 copy-start
  64.3 0.0 copy-start.1
  64.4 5.7 %signal_gradient.1 = bf16[32,4096]{1,0:T(8,128)(2,1)} custom-call(s32[1]{0:T(128)} %bitcast.refs_0_, bf16[32,64,128]{2,1,0:T(8,128)(2,1)} %all-to-all-done.1.refs_0_.refs_1_, f32[1024,128]{1,0:T(8,128)} %get-tuple-element.55.refs_2_, bf16[32,4096]{1,0:T(8,128)(2,1)} %refs_3_.5, bf16[32,80,128]{2,1,0:T(8,128)(2,1)} %correlation.1.refs_4_, ...), custom_call_target="tpu_custom_call" | custom-call | tf_op jit(solution)/shard_map/signal_gradient/pallas_call | solution.py:140
  70.0 8.5 %all-to-all-done.2.refs_2_ = bf16[32,80,128]{2,1,0:T(8,128)(2,1)S(1)} async-done(((bf16[32,80,128]{2,1,0:T(8,128)(2,1)}), bf16[32,80,128]{2,1,0:T(8,128)(2,1)S(1)}, u32[]{:S(2)}, u32[]{:S(2)}) %all-to-all-start.2) | async-done | bytes 655392 | tf_op jit(solution)/shard_map/all_to_all | solution.py:1079
  78.5 0.0 copy-done
  78.5 0.0 copy-done.1
  78.5 1.9 %outputs.1 = (f32[32,4096]{1,0:T(8,128)}, f32[32,32]{1,0:T(8,128)}, f32[32,32]{1,0:T(8,128)}, f32[32,32]{1,0:T(8,128)}, f32[32,32]{1,0:T(8,128)}, /*index=5*/f32...) custom-call(s32[1]{0:T(128)S(6)} %copy.29.refs_0_, s32[1]{0:T(128)} %bitcast.1.refs_1_, ...), custom_call_target="tpu_custom_call" | custom-call | tf_op jit(solution)/shard_map/outputs/pallas_call | solution.py:140
Async XLA Ops:
  4.7 12.4 %collective-permute-start = (bf16[32,4224]{1,0:T(8,128)(2,1)}, bf16[32,4224]{1,0:T(8,128)(2,1)}, u32[]{:S(2)}, u32[]{:S(2)}) collective-permute-start(bf16[32,4224]{1,0:T(8,128)(2,1)} %get-tuple-element.42.refs_2_), channel_id=1, source_target_pairs={{0,2},{1,3},{2,0},{3,1},{4,6},{5,7},{6,4},{7,5},{8,10},{9,11},{10,... | collective-permute-start | bytes 811016 | tf_op jit(solution)/shard_map/ppermute | solution.py:1100
  6.4 23.1 %all-to-all-start = ((bf16[32,64,128]{2,1,0:T(8,128)(2,1)}), bf16[32,64,128]{2,1,0:T(8,128)(2,1)}, u32[]{:S(2)}, u32[]{:S(2)}) async-start(bf16[32,64,128]{2,1,0:T(8,128)(2,1)} %get-tuple-element.44.refs_0_.refs_8_), calls=%async_computation | async-start | bytes 1048576 | tf_op jit(solution)/shard_map/all_to_all | solution.py:1079
  17.1 12.4 %collective-permute-start.1 = (bf16[32,4224]{1,0:T(8,128)(2,1)}, bf16[32,4224]{1,0:T(8,128)(2,1)}, u32[]{:S(2)}, u32[]{:S(2)}) collective-permute-start(bf16[32,4224]{1,0:T(8,128)(2,1)} %get-tuple-element.42.refs_2_), channel_id=1, source_target_pairs={{0,1},{1,0},{2,3},{3,2},{4,5},{5,4},{6,7},{7,6},{8,9},{9,8},{10,11... | collective-permute-start | bytes 811016 | tf_op jit(solution)/shard_map/ppermute | solution.py:1100
  17.1 12.3 %collective-permute-start.2 = (bf16[32,4224]{1,0:T(8,128)(2,1)}, bf16[32,4224]{1,0:T(8,128)(2,1)}, u32[]{:S(2)}, u32[]{:S(2)}) collective-permute-start(bf16[32,4224]{1,0:T(8,128)(2,1)} %collective-permute-done.refs_4_), channel_id=1, source_target_pairs={{0,1},{1,0},{2,3},{3,2},{4,5},{5,4},{6,7},{7,6},{8,9},{9,8},{10,11... | collective-permute-start | bytes 811016 | tf_op jit(solution)/shard_map/ppermute | solution.py:1100
  35.3 4.7 %copy-start.2 = (f32[32,128]{1,0:T(8,128)S(1)}, f32[32,128]{1,0:T(8,128)}, u32[]{:S(2)}) copy-start(f32[32,128]{1,0:T(8,128)} %get-tuple-element.56.refs_7_.refs_12_) | copy-start | bytes 49156
  35.3 16.2 %all-to-all-start.1 = ((bf16[32,64,128]{2,1,0:T(8,128)(2,1)}), bf16[32,64,128]{2,1,0:T(8,128)(2,1)}, u32[]{:S(2)}, u32[]{:S(2)}) async-start(bf16[32,64,128]{2,1,0:T(8,128)(2,1)} %get-tuple-element.54), calls=%async_computation.1 | async-start | bytes 1048576 | tf_op jit(solution)/shard_map/all_to_all | solution.py:1079
  39.9 6.6 %collective-permute-start.5 = (f32[32,128]{1,0:T(8,128)S(1)}, f32[32,128]{1,0:T(8,128)S(1)}, u32[]{:S(2)}, u32[]{:S(2)}) collective-permute-start(f32[32,128]{1,0:T(8,128)S(1)} %copy-done.2), channel_id=1, source_target_pairs={{0,3},{1,2},{2,1},{3,0},{4,7},{5,6},{6,5},{7,4},{8,11},{9,10},{10,... | collective-permute-start | bytes 49160 | tf_op jit(solution)/shard_map/ppermute | solution.py:1100
  40.0 6.5 %collective-permute-start.4 = (f32[32,128]{1,0:T(8,128)S(1)}, f32[32,128]{1,0:T(8,128)S(1)}, u32[]{:S(2)}, u32[]{:S(2)}) collective-permute-start(f32[32,128]{1,0:T(8,128)S(1)} %copy-done.2), channel_id=1, source_target_pairs={{0,2},{1,3},{2,0},{3,1},{4,6},{5,7},{6,4},{7,5},{8,10},{9,11},{10,... | collective-permute-start | bytes 49160 | tf_op jit(solution)/shard_map/ppermute | solution.py:1100
  40.2 6.3 %collective-permute-start.3 = (f32[32,128]{1,0:T(8,128)S(1)}, f32[32,128]{1,0:T(8,128)S(1)}, u32[]{:S(2)}, u32[]{:S(2)}) collective-permute-start(f32[32,128]{1,0:T(8,128)S(1)} %copy-done.2), channel_id=1, source_target_pairs={{0,1},{1,0},{2,3},{3,2},{4,5},{5,4},{6,7},{7,6},{8,9},{9,8},{10,11... | collective-permute-start | bytes 49160 | tf_op jit(solution)/shard_map/ppermute | solution.py:1100
  46.5 4.9 %copy-start.3 = (f32[32,128]{1,0:T(8,128)}, f32[32,128]{1,0:T(8,128)S(1)}, u32[]{:S(2)}) copy-start(f32[32,128]{1,0:T(8,128)S(1)} %collective-permute-done.5.refs_15_) | copy-start | bytes 49156
  46.5 4.9 %copy-start.4 = (f32[32,128]{1,0:T(8,128)}, f32[32,128]{1,0:T(8,128)S(1)}, u32[]{:S(2)}) copy-start(f32[32,128]{1,0:T(8,128)S(1)} %collective-permute-done.4.refs_14_) | copy-start | bytes 49156
  46.6 4.9 %copy-start.5 = (f32[32,128]{1,0:T(8,128)}, f32[32,128]{1,0:T(8,128)S(1)}, u32[]{:S(2)}) copy-start(f32[32,128]{1,0:T(8,128)S(1)} %collective-permute-done.3.refs_13_) | copy-start | bytes 49156
  58.9 19.7 %all-to-all-start.2 = ((bf16[32,80,128]{2,1,0:T(8,128)(2,1)}), bf16[32,80,128]{2,1,0:T(8,128)(2,1)S(1)}, u32[]{:S(2)}, u32[]{:S(2)}) async-start(bf16[32,80,128]{2,1,0:T(8,128)(2,1)} %correlation.1.refs_4_), calls=%async_computation.2 | async-start | bytes 1310720 | tf_op jit(solution)/shard_map/all_to_all | solution.py:1079
  64.3 14.2 %copy-start = (f32[2,32,128]{2,1,0:T(8,128)S(1)}, f32[2,32,128]{2,1,0:T(8,128)}, u32[]{:S(2)}) copy-start(f32[2,32,128]{2,1,0:T(8,128)} %get-tuple-element.46.refs_2_.refs_10_.refs_9_.refs_6_.refs_4_) | copy-start | bytes 98308
  64.3 14.2 %copy-start.1 = (f32[11,32,128]{2,1,0:T(8,128)S(1)}, f32[11,32,128]{2,1,0:T(8,128)}, u32[]{:S(2)}) copy-start(f32[11,32,128]{2,1,0:T(8,128)} %get-tuple-element.62.refs_3_) | copy-start | bytes 540676

commit v4 on v3

--- a/solution.py
+++ b/solution.py
@@ -23,6 +23,8 @@
 COLS = 512
 PER = COLS // LN
 ROWS = RANKS * BLOCK // COLS
+PIECES = BLOCK // COLS
+PLACE = [i % PER * PIECES + i // PER for i in range(CK)]
 SEND1 = 64
 SEND2 = 64
 SEND3 = 80
@@ -225,7 +227,7 @@
     hr = jnp.zeros((GROUPS, LN), F32)
     hi = jnp.zeros((GROUPS, LN), F32)
     for i in order:
-        rows = pl.ds(i * GROUPS, GROUPS)
+        rows = pl.ds(PLACE[i] * GROUPS, GROUPS)
         own_r, own_i = sr_ref[rows, :], si_ref[rows, :]
         sr_ref[rows, :] = hr
         si_ref[rows, :] = hi
@@ -236,7 +238,7 @@
 
 def add_entering(sr_ref, si_ref, sr_in, si_in, step_r, step_i, start, order):
     for k, i in enumerate(order):
-        rows = pl.ds(i * GROUPS, GROUPS)
+        rows = pl.ds(PLACE[i] * GROUPS, GROUPS)
         nr, ni = cmul(step_r[k], step_i[k], *start) if k else start
         sr_ref[rows, :] = sr_in[rows, :] + nr
         si_ref[rows, :] = si_in[rows, :] + ni
@@ -298,7 +300,9 @@
     doubles = doublings(decay, turn)
     loads[0].wait()
     for i in range(CK):
-        rows_ref[pl.ds(i, CH, stride=CK), :] = signal_ref[:, i * LN : (i + 1) * LN].astype(F32)
+        rows_ref[pl.ds(PLACE[i], CH, stride=CK), :] = signal_ref[
+            :, i * LN : (i + 1) * LN
+        ].astype(F32)
     for c in range(CH):
         send_ref[c, :CK, :] = rows_ref[c * CK : (c + 1) * CK, :].astype(BF16)
     loads[1].wait()
@@ -474,7 +478,9 @@
     )
     weights = dot(mine.astype(BF16), cot_ref[:, BLOCK:], NT).astype(BF16)
     for i in range(CK):
-        act_ref[pl.ds(i, CH, stride=CK), :] = dot(weights, cot_ref[:, i * LN : (i + 1) * LN])
+        act_ref[pl.ds(PLACE[i], CH, stride=CK), :] = dot(
+            weights, cot_ref[:, i * LN : (i + 1) * LN]
+        )
 
 
 def gelu_both(x):
@@ -584,7 +590,9 @@
     )
     stores[-1].start()
     for i in range(CK):
-        flat_ref[:, i * LN : (i + 1) * LN] = activation_ref[pl.ds(i, CH, stride=CK), :].astype(BF16)
+        flat_ref[:, i * LN : (i + 1) * LN] = activation_ref[
+            pl.ds(PLACE[i], CH, stride=CK), :
+        ].astype(BF16)
     mix_ref[...] = dot(flat_ref[...], cot_ref[:, :BLOCK], NT)
     wait_small.store(2)
     for copy in stores:
@@ -664,7 +672,7 @@
     for i in range(CK):
         cols = slice(i * LN, (i + 1) * LN)
         out_ref[:, cols] = (
-            cot_ref[:, cols].astype(F32) + rows_ref[pl.ds(i, CH, stride=CK), :]
+            cot_ref[:, cols].astype(F32) + rows_ref[pl.ds(PLACE[i], CH, stride=CK), :]
         ).astype(BF16)
 
 
@@ -695,11 +703,10 @@
 def dft_tables():
     full_len = RANKS * BLOCK
     row = np.arange(ROWS)
-    time_row = (row % RANKS) * (BLOCK // COLS) + row // RANKS
     first_ids = np.arange(ROWS)
     column = np.arange(COLS)
     angle1 = (
-        2.0 * np.pi * (((4 * first_ids[:, None] + 1) * time_row[None, :]) % (4 * ROWS)) / (4 * ROWS)
+        2.0 * np.pi * (((4 * first_ids[:, None] + 1) * row[None, :]) % (4 * ROWS)) / (4 * ROWS)
     )
     angle_t = 2.0 * np.pi * ((4 * first_ids[:, None] + 1) * column[None, :]) / (4 * full_len)
     lane = np.arange(LN)
@@ -721,20 +728,14 @@
     return halves(stage1), halves(stage1.T / full_len), halves(stage2), twiddle, steps
 
 
-def gather_rows(ref, stride, base):
-    return jnp.concatenate(
-        [
-            jnp.concatenate(
-                [
-                    ref[pl.ds(base + piece * PER + q, RANKS, stride=stride), :]
-                    for q in range(PER)
-                ],
-                1,
-            )
-            for piece in range(BLOCK // COLS)
-        ],
-        0,
-    )
+def gather_rows(ref):
+    result = []
+    for d in range(RANKS):
+        block = ref[d].astype(F32)
+        result.append(
+            jnp.concatenate([block[q * PIECES : (q + 1) * PIECES] for q in range(PER)], 1)
+        )
+    return jnp.concatenate(result, 0)
 
 
 def butterfly(parts, sign):
@@ -808,7 +809,7 @@
 def spectrum_kernel(
     wait_small, me_ref, got_hbm, d1h_hbm, d1l_hbm, twiddle_hbm, d2h_hbm, d2l_hbm, after_hbm,
     steps_ref, wide_ref, terms_ref, spec_ref, column_ref, turn_ref,
-    got_ref, d1h, d1l, twiddle, d2h, d2l, rows_ref, sems,
+    got_ref, d1h, d1l, twiddle, d2h, d2l, sems,
 ):
     loads = started(
         sems,
@@ -819,9 +820,7 @@
     me = me_ref[0]
     embed = wide_ref[0, pl.ds(me, 1), :]
     loads[0].wait()
-    for d in range(RANKS):
-        rows_ref[d * CK : (d + 1) * CK, :] = got_ref[d].astype(F32) + embed
-    rows = gather_rows(rows_ref, CK, 0)
+    rows = gather_rows(got_ref) + jnp.concatenate([embed] * PER, 1)
     spec_ref[...] = forward_dft(
         rows, False, d1h, d1l, d2h, d2l, twiddle, steps_ref, waiting(loads[1:3]),
         waiting(loads[3:6]),
@@ -846,11 +845,13 @@
     column_ref[...] = jnp.where(block < 2, table, table * col)
     ranks = lax.broadcasted_iota(jnp.int32, (RANKS, LN), 0).astype(F32)
     br, bi = far_power(d, th, ranks)
-    for piece in range(BLOCK // COLS):
-        zr, zi = far_power(d, th, float(piece * COLS) / BLOCK)
-        nr, ni = cmul(br, bi, zr, zi) if piece else (br, bi)
-        turn_ref[0, piece * RANKS : (piece + 1) * RANKS, :] = nr
-        turn_ref[1, piece * RANKS : (piece + 1) * RANKS, :] = ni
+    pieces = lax.broadcasted_iota(jnp.int32, (PIECES, LN), 0).astype(F32) * (COLS / BLOCK)
+    pr, pi = far_power(d, th, pieces)
+    for k in range(RANKS):
+        rows = slice(k * PIECES, (k + 1) * PIECES)
+        turn_ref[0, rows, :], turn_ref[1, rows, :] = cmul(
+            pr, pi, br[k : k + 1], bi[k : k + 1]
+        )
 
 
 def spectrum(me, got, after, wide, terms, tables):
@@ -873,7 +874,6 @@
             pltpu.VMEM((2, ROWS, COLS), F32),
             pltpu.VMEM((2 * LN, 2 * LN), BF16),
             pltpu.VMEM((2 * LN, 2 * LN), BF16),
-            pltpu.VMEM((RANKS * CK, LN), F32),
             pltpu.SemaphoreType.DMA((6,)),
         ],
         name="input_spectrum",
@@ -884,7 +884,7 @@
     wait_small, got_hbm, d1h_hbm, d1l_hbm, twiddle_hbm, d2h_hbm, d2l_hbm, spec_hbm, d1th_hbm, d1tl_hbm,
     column_hbm, turn_hbm, steps_ref, m0, m1, m2, m3, send_hbm,
     got_ref, d1h, d1l, twiddle, d2h, d2l, spec_ref, d1th, d1tl, column_ref, turn_ref,
-    rows_ref, send_ref, sems, out_sems,
+    send_ref, sems, out_sems,
 ):
     loads = started(
         sems,
@@ -900,9 +900,7 @@
     middle = pl.ds(CK, CK)
     stores = started(out_sems, (send_ref.at[:, middle, :], send_hbm.at[:, middle, :]))
     loads[0].wait()
-    for d in range(RANKS):
-        rows_ref[d * CK : (d + 1) * CK, :] = got_ref[d].astype(F32)
-    g_rows = gather_rows(rows_ref, CK, 0)
+    g_rows = gather_rows(got_ref)
     g_spec = forward_dft(
         g_rows, True, d1h, d1l, d2h, d2l, twiddle, steps_ref, waiting(loads[1:3]),
         waiting(loads[3:6]),
@@ -913,13 +911,11 @@
     both = jnp.concatenate([xr * gr + xi * gi, xr * gi - xi * gr], 1)
     waiting(loads[7:])()
     kernel_rows = inverse_dft(both, d1th, d1tl, d2h, d2l, twiddle, steps_ref)
-    for piece in range(BLOCK // COLS):
-        for q in range(PER):
-            rows_ref[pl.ds(piece * PER + q, RANKS, stride=CK), :] = kernel_rows[
-                piece * RANKS : (piece + 1) * RANKS, q * LN : (q + 1) * LN
-            ]
     for d in range(RANKS):
-        send_ref[d, :CK, :] = rows_ref[d * CK : (d + 1) * CK, :].astype(BF16)
+        piece = kernel_rows[d * PIECES : (d + 1) * PIECES]
+        send_ref[d, :CK, :] = jnp.concatenate(
+            [piece[:, q * LN : (q + 1) * LN] for q in range(PER)], 0
+        ).astype(BF16)
         if d % 8 == 7:
             part = pl.ds(d - 7, 8), pl.ds(0, CK)
             stores.append(
@@ -933,7 +929,7 @@
     g_inner = dot2(g_rows.astype(BF16), column)
     rr, ri = turn_ref[0], turn_ref[1]
     ids = lax.broadcasted_iota(jnp.int32, (ROWS, LN), 0)
-    starts = ((ids % RANKS) * BLOCK + (ids // RANKS) * COLS).astype(F32)
+    starts = (ids * COLS).astype(F32)
 
     def total(values):
         return jnp.sum(values, 0, keepdims=True)
@@ -987,7 +983,6 @@
             pltpu.VMEM((ROWS, 2 * ROWS), BF16),
             pltpu.VMEM((COLS, LN), F32),
             pltpu.VMEM((2, ROWS, LN), F32),
-            pltpu.VMEM((RANKS * CK, LN), F32),
             pltpu.VMEM((RANKS, SEND3, LN), BF16),
             pltpu.SemaphoreType.DMA((11,)),
             pltpu.SemaphoreType.DMA((6,)),
@@ -1005,7 +1000,7 @@
         rows_ref[c * CK : (c + 1) * CK, :] = got_ref[c, :CK, :].astype(F32)
         mixes = mixes + got_ref[c, CK : 2 * CK, :].astype(F32)
     for i in range(CK):
-        kernel_ref[:, i * LN : (i + 1) * LN] = rows_ref[pl.ds(i, CH, stride=CK), :]
+        kernel_ref[:, i * LN : (i + 1) * LN] = rows_ref[pl.ds(PLACE[i], CH, stride=CK), :]
     for c in range(CH):
         small = got_ref[c, 2 * CK :, :].astype(F32)
         rows_ref[c * 8 : (c + 1) * 8, :] = small[:8] + small[8:]

time: 81.1 us -> 80.2 us (0.989)
  Pallas kernels: 33.2 us -> 32.3 us
    pallas_call x7, Pallas kernels: 33.2 us -> 32.3 us  [staged(): pl.pallas_call(body, in_specs=[SMEM] * len(scalars) + [plain_spec] * len(...]
where the time goes in v4:
time: 80.2 us; the launch traced here: 79.6 us
  Pallas kernels  32.3 us (40%)
  starting transfers between devices  24.7 us (31%)
  waiting for transfers between devices  21 us (26%)
  between operations  1.63 us (2%)
    pallas_call x7, Pallas kernels, staged(): pl.pallas_call(body, in_specs=[SMEM] * len(scalars) + [plain_spec] * len(...  32.3 us
    all_to_all x3, waiting for transfers between devices, exchange(): return lax.all_to_all(values, 'tm', split_axis=0, concat_axis=0, tiled=True)  21 us
    all_to_all x3, starting transfers between devices, exchange(): return lax.all_to_all(values, 'tm', split_axis=0, concat_axis=0, tiled=True)  20.4 us
    ppermute x6, starting transfers between devices, swap(): return lax.ppermute(values, 'chan', [(i, i ^ mask) for i in range(4)])  4.25 us
  transfers between devices with their start and end apart: 9, of which 3 were waited for; matrix products, arithmetic and copies ran while one was open for 0% of the time, Pallas kernels for 18%

profile of v4, /device:TPU:0, one launch (start us, length us, event | category | flops | bytes accessed | tf_op | source)
XLA Modules:
  0.0 79.6 jit_solution(12353245693625972003)
XLA Ops:
  1.3 3.4 %block_states.1 = (bf16[32,64,128]{2,1,0:T(8,128)(2,1)}, bf16[32,4224]{1,0:T(8,128)(2,1)}, f32[256,128]{1,0:T(8,128)}, f32[256,128]{1,0:T(8,128)}, f32[4,8,128]{2,1,0:T(8,128)}, /*index=5*/f32[2,32,128]{2,1,0:T(8,128)}) custom-call(s32[1]{0:T(128)S(6)} %copy.29.refs_0_, bf16[32,4096]{1,0:T(8,128)(2,1)} %refs_1_.2, bf16[32,4096]{1,0:T(8,128)(2,1)} %refs_3_.5, ...), custom_call_target="tpu_custom_call" | custom-call | tf_op jit(solution)/shard_map/block_states/pallas_call | solution.py:142
  4.7 1.7 %collective-permute-start = (bf16[32,4224]{1,0:T(8,128)(2,1)}, bf16[32,4224]{1,0:T(8,128)(2,1)}, u32[]{:S(2)}, u32[]{:S(2)}) collective-permute-start(bf16[32,4224]{1,0:T(8,128)(2,1)} %get-tuple-element.42.refs_2_), channel_id=1, source_target_pairs={{0,2},{1,3},{2,0},{3,1},{4,6},{5,7},{6,4},{7,5},{8,10},{9,11},{10,... | collective-permute-start | bytes 811016 | tf_op jit(solution)/shard_map/ppermute | solution.py:1095
  6.4 10.6 %all-to-all-start = ((bf16[32,64,128]{2,1,0:T(8,128)(2,1)}), bf16[32,64,128]{2,1,0:T(8,128)(2,1)}, u32[]{:S(2)}, u32[]{:S(2)}) async-start(bf16[32,64,128]{2,1,0:T(8,128)(2,1)} %get-tuple-element.44.refs_0_.refs_8_), calls=%async_computation | async-start | bytes 1048576 | tf_op jit(solution)/shard_map/all_to_all | solution.py:1074
  17.0 0.0 collective-permute-done.refs_4_
  17.1 0.1 collective-permute-start.1
  17.2 0.5 collective-permute-start.2
  17.6 4.5 %within_chunks.1 = (f32[1024,128]{1,0:T(8,128)}, f32[32,8,128]{2,1,0:T(8,128)}, f32[32,8,128]{2,1,0:T(8,128)}, f32[32,8,128]{2,1,0:T(8,128)}, f32[32,8,128]{2,1,0:T(8,128)}, /*index=5*/f32[11,32,128]{2,1,0:T(8,128)}) custom-call(bf16[32,64,128]{2,1,0:T(8,128)(2,1)} %get-tuple-element.44.refs_0_.refs_8_, ...), custom_call_target="tpu_custom_call" | custom-call | tf_op jit(solution)/shard_map/within_chunks/pallas_call | solution.py:142
  22.2 7.3 %all-to-all-done.refs_7_.refs_1_ = bf16[32,64,128]{2,1,0:T(8,128)(2,1)} async-done(((bf16[32,64,128]{2,1,0:T(8,128)(2,1)}), bf16[32,64,128]{2,1,0:T(8,128)(2,1)}, u32[]{:S(2)}, u32[]{:S(2)}) %all-to-all-start) | async-done | bytes 524320 | tf_op jit(solution)/shard_map/all_to_all | solution.py:1074
  29.5 0.0 collective-permute-done.1.refs_3_
  29.5 0.0 collective-permute-done.2.refs_5_
  29.5 5.8 %activation_and_states.1 = (bf16[32,64,128]{2,1,0:T(8,128)(2,1)}, f32[1024,128]{1,0:T(8,128)}, f32[32,128]{1,0:T(8,128)}, f32[256,128]{1,0:T(8,128)}, f32[256,128]{1,0:T(8,128)}) custom-call(s32[1]{0:T(128)} %bitcast.refs_0_, s32[1]{0:T(128)} %bitcast.1.refs_1_, bf16[32,4224]{1,0:T(8,128)(2,1)} %get-tuple-element.42.refs_2_, ...), custom_call_target="tpu_custom_call" | custom-call | tf_op jit(solution)/shard_map/activation_and_states/pallas_call | solution.py:142
  35.3 0.0 copy-start.2
  35.3 4.6 %all-to-all-start.1 = ((bf16[32,64,128]{2,1,0:T(8,128)(2,1)}), bf16[32,64,128]{2,1,0:T(8,128)(2,1)}, u32[]{:S(2)}, u32[]{:S(2)}) async-start(bf16[32,64,128]{2,1,0:T(8,128)(2,1)} %get-tuple-element.54), calls=%async_computation.1 | async-start | bytes 1048576 | tf_op jit(solution)/shard_map/all_to_all | solution.py:1074
  39.9 0.0 copy-done.2
  39.9 0.1 collective-permute-start.5
  40.0 0.2 collective-permute-start.4
  40.2 1.6 %collective-permute-start.3 = (f32[32,128]{1,0:T(8,128)S(1)}, f32[32,128]{1,0:T(8,128)S(1)}, u32[]{:S(2)}, u32[]{:S(2)}) collective-permute-start(f32[32,128]{1,0:T(8,128)S(1)} %copy-done.2), channel_id=1, source_target_pairs={{0,1},{1,0},{2,3},{3,2},{4,5},{5,4},{6,7},{7,6},{8,9},{9,8},{10,11... | collective-permute-start | bytes 49160 | tf_op jit(solution)/shard_map/ppermute | solution.py:1095
  41.9 4.3 %input_spectrum.1 = (f32[1024,256]{1,0:T(8,128)}, f32[512,128]{1,0:T(8,128)}, f32[2,256,128]{2,1,0:T(8,128)}) custom-call(s32[1]{0:T(128)} %bitcast.refs_0_, bf16[32,64,128]{2,1,0:T(8,128)(2,1)} %all-to-all-done.refs_7_.refs_1_, bf16[512,256]{1,0:T(8,128)(2,1)} %constant.25.clone.refs_2_.refs_1_, bf16[512,256]{1,0:T(8,128)(2,1)} %constant.26.clone.refs_3_.refs_2_, ...), custom_call_target="tpu_custom_call" | custom-call | tf_op jit(solution)/shard_map/input_spectrum/pallas_call | solution.py:142
  46.2 0.0 collective-permute-done.5.refs_15_
  46.2 0.0 copy-start.3
  46.2 0.0 collective-permute-done.4.refs_14_
  46.2 0.0 copy-start.4
  46.2 0.0 collective-permute-done.3.refs_13_
  46.3 0.0 copy-start.5
  46.3 5.2 %all-to-all-done.1.refs_0_.refs_1_ = bf16[32,64,128]{2,1,0:T(8,128)(2,1)} async-done(((bf16[32,64,128]{2,1,0:T(8,128)(2,1)}), bf16[32,64,128]{2,1,0:T(8,128)(2,1)}, u32[]{:S(2)}, u32[]{:S(2)}) %all-to-all-start.1) | async-done | bytes 524320 | tf_op jit(solution)/shard_map/all_to_all | solution.py:1074
  51.4 0.0 copy-done.3
  51.5 0.0 copy-done.4
  51.5 0.0 copy-done.5
  51.5 6.8 %correlation.1.refs_4_ = bf16[32,80,128]{2,1,0:T(8,128)(2,1)} custom-call(bf16[32,64,128]{2,1,0:T(8,128)(2,1)} %all-to-all-done.1.refs_0_.refs_1_, bf16[512,256]{1,0:T(8,128)(2,1)} %constant.25.clone.refs_2_.refs_1_, bf16[512,256]{1,0:T(8,128)(2,1)} %constant.26.clone.refs_3_.refs_2_, f32[2,256,512]{2,1,0:T(8,128)} %constant.27.clone.refs_4_.refs_3_, ...), custom_call_target="tpu_custom_call" | custom-call | tf_op jit(solution)/shard_map/correlation/pallas_call | solution.py:142
  58.2 5.1 %all-to-all-start.2 = ((bf16[32,80,128]{2,1,0:T(8,128)(2,1)}), bf16[32,80,128]{2,1,0:T(8,128)(2,1)S(1)}, u32[]{:S(2)}, u32[]{:S(2)}) async-start(bf16[32,80,128]{2,1,0:T(8,128)(2,1)} %correlation.1.refs_4_), calls=%async_computation.2 | async-start | bytes 1310720 | tf_op jit(solution)/shard_map/all_to_all | solution.py:1074
  63.4 0.0 copy-start
  63.4 0.0 copy-start.1
  63.4 5.7 %signal_gradient.1 = bf16[32,4096]{1,0:T(8,128)(2,1)} custom-call(s32[1]{0:T(128)} %bitcast.refs_0_, bf16[32,64,128]{2,1,0:T(8,128)(2,1)} %all-to-all-done.1.refs_0_.refs_1_, f32[1024,128]{1,0:T(8,128)} %get-tuple-element.55.refs_2_, bf16[32,4096]{1,0:T(8,128)(2,1)} %refs_3_.5, bf16[32,80,128]{2,1,0:T(8,128)(2,1)} %correlation.1.refs_4_, ...), custom_call_target="tpu_custom_call" | custom-call | tf_op jit(solution)/shard_map/signal_gradient/pallas_call | solution.py:142
  69.1 8.5 %all-to-all-done.2.refs_2_ = bf16[32,80,128]{2,1,0:T(8,128)(2,1)S(1)} async-done(((bf16[32,80,128]{2,1,0:T(8,128)(2,1)}), bf16[32,80,128]{2,1,0:T(8,128)(2,1)S(1)}, u32[]{:S(2)}, u32[]{:S(2)}) %all-to-all-start.2) | async-done | bytes 655392 | tf_op jit(solution)/shard_map/all_to_all | solution.py:1074
  77.6 0.0 copy-done
  77.6 0.0 copy-done.1
  77.6 1.9 %outputs.1 = (f32[32,4096]{1,0:T(8,128)}, f32[32,32]{1,0:T(8,128)}, f32[32,32]{1,0:T(8,128)}, f32[32,32]{1,0:T(8,128)}, f32[32,32]{1,0:T(8,128)}, /*index=5*/f32...) custom-call(s32[1]{0:T(128)S(6)} %copy.29.refs_0_, s32[1]{0:T(128)} %bitcast.1.refs_1_, ...), custom_call_target="tpu_custom_call" | custom-call | tf_op jit(solution)/shard_map/outputs/pallas_call | solution.py:142
Async XLA Ops:
  4.7 12.4 %collective-permute-start = (bf16[32,4224]{1,0:T(8,128)(2,1)}, bf16[32,4224]{1,0:T(8,128)(2,1)}, u32[]{:S(2)}, u32[]{:S(2)}) collective-permute-start(bf16[32,4224]{1,0:T(8,128)(2,1)} %get-tuple-element.42.refs_2_), channel_id=1, source_target_pairs={{0,2},{1,3},{2,0},{3,1},{4,6},{5,7},{6,4},{7,5},{8,10},{9,11},{10,... | collective-permute-start | bytes 811016 | tf_op jit(solution)/shard_map/ppermute | solution.py:1095
  6.4 23.1 %all-to-all-start = ((bf16[32,64,128]{2,1,0:T(8,128)(2,1)}), bf16[32,64,128]{2,1,0:T(8,128)(2,1)}, u32[]{:S(2)}, u32[]{:S(2)}) async-start(bf16[32,64,128]{2,1,0:T(8,128)(2,1)} %get-tuple-element.44.refs_0_.refs_8_), calls=%async_computation | async-start | bytes 1048576 | tf_op jit(solution)/shard_map/all_to_all | solution.py:1074
  17.1 12.4 %collective-permute-start.1 = (bf16[32,4224]{1,0:T(8,128)(2,1)}, bf16[32,4224]{1,0:T(8,128)(2,1)}, u32[]{:S(2)}, u32[]{:S(2)}) collective-permute-start(bf16[32,4224]{1,0:T(8,128)(2,1)} %get-tuple-element.42.refs_2_), channel_id=1, source_target_pairs={{0,1},{1,0},{2,3},{3,2},{4,5},{5,4},{6,7},{7,6},{8,9},{9,8},{10,11... | collective-permute-start | bytes 811016 | tf_op jit(solution)/shard_map/ppermute | solution.py:1095
  17.2 12.3 %collective-permute-start.2 = (bf16[32,4224]{1,0:T(8,128)(2,1)}, bf16[32,4224]{1,0:T(8,128)(2,1)}, u32[]{:S(2)}, u32[]{:S(2)}) collective-permute-start(bf16[32,4224]{1,0:T(8,128)(2,1)} %collective-permute-done.refs_4_), channel_id=1, source_target_pairs={{0,1},{1,0},{2,3},{3,2},{4,5},{5,4},{6,7},{7,6},{8,9},{9,8},{10,11... | collective-permute-start | bytes 811016 | tf_op jit(solution)/shard_map/ppermute | solution.py:1095
  35.3 4.7 %copy-start.2 = (f32[32,128]{1,0:T(8,128)S(1)}, f32[32,128]{1,0:T(8,128)}, u32[]{:S(2)}) copy-start(f32[32,128]{1,0:T(8,128)} %get-tuple-element.56.refs_7_.refs_12_) | copy-start | bytes 49156
  35.3 16.2 %all-to-all-start.1 = ((bf16[32,64,128]{2,1,0:T(8,128)(2,1)}), bf16[32,64,128]{2,1,0:T(8,128)(2,1)}, u32[]{:S(2)}, u32[]{:S(2)}) async-start(bf16[32,64,128]{2,1,0:T(8,128)(2,1)} %get-tuple-element.54), calls=%async_computation.1 | async-start | bytes 1048576 | tf_op jit(solution)/shard_map/all_to_all | solution.py:1074
  39.9 6.3 %collective-permute-start.5 = (f32[32,128]{1,0:T(8,128)S(1)}, f32[32,128]{1,0:T(8,128)S(1)}, u32[]{:S(2)}, u32[]{:S(2)}) collective-permute-start(f32[32,128]{1,0:T(8,128)S(1)} %copy-done.2), channel_id=1, source_target_pairs={{0,3},{1,2},{2,1},{3,0},{4,7},{5,6},{6,5},{7,4},{8,11},{9,10},{10,... | collective-permute-start | bytes 49160 | tf_op jit(solution)/shard_map/ppermute | solution.py:1095
  40.0 6.2 %collective-permute-start.4 = (f32[32,128]{1,0:T(8,128)S(1)}, f32[32,128]{1,0:T(8,128)S(1)}, u32[]{:S(2)}, u32[]{:S(2)}) collective-permute-start(f32[32,128]{1,0:T(8,128)S(1)} %copy-done.2), channel_id=1, source_target_pairs={{0,2},{1,3},{2,0},{3,1},{4,6},{5,7},{6,4},{7,5},{8,10},{9,11},{10,... | collective-permute-start | bytes 49160 | tf_op jit(solution)/shard_map/ppermute | solution.py:1095
  40.2 6.0 %collective-permute-start.3 = (f32[32,128]{1,0:T(8,128)S(1)}, f32[32,128]{1,0:T(8,128)S(1)}, u32[]{:S(2)}, u32[]{:S(2)}) collective-permute-start(f32[32,128]{1,0:T(8,128)S(1)} %copy-done.2), channel_id=1, source_target_pairs={{0,1},{1,0},{2,3},{3,2},{4,5},{5,4},{6,7},{7,6},{8,9},{9,8},{10,11... | collective-permute-start | bytes 49160 | tf_op jit(solution)/shard_map/ppermute | solution.py:1095
  46.2 5.2 %copy-start.3 = (f32[32,128]{1,0:T(8,128)}, f32[32,128]{1,0:T(8,128)S(1)}, u32[]{:S(2)}) copy-start(f32[32,128]{1,0:T(8,128)S(1)} %collective-permute-done.5.refs_15_) | copy-start | bytes 49156
  46.2 5.2 %copy-start.4 = (f32[32,128]{1,0:T(8,128)}, f32[32,128]{1,0:T(8,128)S(1)}, u32[]{:S(2)}) copy-start(f32[32,128]{1,0:T(8,128)S(1)} %collective-permute-done.4.refs_14_) | copy-start | bytes 49156
  46.3 5.2 %copy-start.5 = (f32[32,128]{1,0:T(8,128)}, f32[32,128]{1,0:T(8,128)S(1)}, u32[]{:S(2)}) copy-start(f32[32,128]{1,0:T(8,128)S(1)} %collective-permute-done.3.refs_13_) | copy-start | bytes 49156
  58.2 19.4 %all-to-all-start.2 = ((bf16[32,80,128]{2,1,0:T(8,128)(2,1)}), bf16[32,80,128]{2,1,0:T(8,128)(2,1)S(1)}, u32[]{:S(2)}, u32[]{:S(2)}) async-start(bf16[32,80,128]{2,1,0:T(8,128)(2,1)} %correlation.1.refs_4_), calls=%async_computation.2 | async-start | bytes 1310720 | tf_op jit(solution)/shard_map/all_to_all | solution.py:1074
  63.4 14.2 %copy-start = (f32[2,32,128]{2,1,0:T(8,128)S(1)}, f32[2,32,128]{2,1,0:T(8,128)}, u32[]{:S(2)}) copy-start(f32[2,32,128]{2,1,0:T(8,128)} %get-tuple-element.46.refs_2_.refs_10_.refs_9_.refs_6_.refs_4_) | copy-start | bytes 98308
  63.4 14.2 %copy-start.1 = (f32[11,32,128]{2,1,0:T(8,128)S(1)}, f32[11,32,128]{2,1,0:T(8,128)}, u32[]{:S(2)}) copy-start(f32[11,32,128]{2,1,0:T(8,128)} %get-tuple-element.62.refs_3_) | copy-start | bytes 540676

commit v5 on v4

--- a/solution.py
+++ b/solution.py
@@ -84,9 +84,11 @@
     return dot(jnp.concatenate([left, left], axis), jnp.concatenate(right, other), dims)
 
 
-def started(sems, *pairs):
+def started(sems, *pairs, between=None, ahead=1):
     copies = [pltpu.make_async_copy(a, b, sems.at[k]) for k, (a, b) in enumerate(pairs)]
-    for copy in copies:
+    for k, copy in enumerate(copies):
+        if between is not None and k == ahead:
+            between()
         copy.start()
     return copies
 
@@ -282,6 +284,7 @@
         (signal_hbm, signal_ref),
         (cot_hbm, own_ref.at[:, pl.ds(0, BLOCK)]),
         (mix_hbm, own_ref.at[:, pl.ds(BLOCK, LN)]),
+        between=wait_small.start,
     )
     wait_small()
     picked = lax.broadcasted_iota(jnp.int32, table_ref.shape, 1) == step_ref[0]
@@ -371,6 +374,7 @@
             pltpu.SemaphoreType.DMA((3,)),
         ],
         name="block_states",
+        eager=0,
         early=(2, 3, 4, 5),
     )
 
@@ -516,8 +520,9 @@
         (got_hbm.at[:, pl.ds(CK, CK), :], got_ref),
         (x_hbm.at[:, pl.ds(0, CK), :], x_ref),
         (out_hbm, out_ref),
-    )
-    wait_small.start(1)
+        between=lambda: wait_small.start(1),
+        ahead=5,
+    )
     wait_small(0, 1)
     me = me_ref[0]
     terms = terms_ref[0], terms_ref[1], terms_ref[2], terms_ref[3]

time: 80.2 us -> 80.2 us (level)
  no operation moved by 1% of the time
where the time goes in v5:
time: 80.2 us; the launch traced here: 79.6 us
  Pallas kernels  32.3 us (40%)
  starting transfers between devices  24.7 us (31%)
  waiting for transfers between devices  21 us (26%)
  between operations  1.63 us (2%)
    pallas_call x7, Pallas kernels, staged(): pl.pallas_call(body, in_specs=[SMEM] * len(scalars) + [plain_spec] * len(...  32.3 us
    all_to_all x3, waiting for transfers between devices, exchange(): return lax.all_to_all(values, 'tm', split_axis=0, concat_axis=0, tiled=True)  21 us
    all_to_all x3, starting transfers between devices, exchange(): return lax.all_to_all(values, 'tm', split_axis=0, concat_axis=0, tiled=True)  20.4 us
    ppermute x6, starting transfers between devices, swap(): return lax.ppermute(values, 'chan', [(i, i ^ mask) for i in range(4)])  4.26 us
  transfers between devices with their start and end apart: 9, of which 3 were waited for; matrix products, arithmetic and copies ran while one was open for 0% of the time, Pallas kernels for 18%

profile of v5, /device:TPU:0, one launch (start us, length us, event | category | flops | bytes accessed | tf_op | source)
XLA Modules:
  0.0 79.6 jit_solution(2556000503678130702)
XLA Ops:
  1.3 3.4 %block_states.1 = (bf16[32,64,128]{2,1,0:T(8,128)(2,1)}, bf16[32,4224]{1,0:T(8,128)(2,1)}, f32[256,128]{1,0:T(8,128)}, f32[256,128]{1,0:T(8,128)}, f32[4,8,128]{2,1,0:T(8,128)}, /*index=5*/f32[2,32,128]{2,1,0:T(8,128)}) custom-call(s32[1]{0:T(128)S(6)} %copy.29.refs_0_, bf16[32,4096]{1,0:T(8,128)(2,1)} %refs_1_.2, bf16[32,4096]{1,0:T(8,128)(2,1)} %refs_3_.5, ...), custom_call_target="tpu_custom_call" | custom-call | tf_op jit(solution)/shard_map/block_states/pallas_call | solution.py:144
  4.7 1.7 %collective-permute-start = (bf16[32,4224]{1,0:T(8,128)(2,1)}, bf16[32,4224]{1,0:T(8,128)(2,1)}, u32[]{:S(2)}, u32[]{:S(2)}) collective-permute-start(bf16[32,4224]{1,0:T(8,128)(2,1)} %get-tuple-element.42.refs_2_), channel_id=1, source_target_pairs={{0,2},{1,3},{2,0},{3,1},{4,6},{5,7},{6,4},{7,5},{8,10},{9,11},{10,... | collective-permute-start | bytes 811016 | tf_op jit(solution)/shard_map/ppermute | solution.py:1100
  6.4 10.6 %all-to-all-start = ((bf16[32,64,128]{2,1,0:T(8,128)(2,1)}), bf16[32,64,128]{2,1,0:T(8,128)(2,1)}, u32[]{:S(2)}, u32[]{:S(2)}) async-start(bf16[32,64,128]{2,1,0:T(8,128)(2,1)} %get-tuple-element.44.refs_0_.refs_8_), calls=%async_computation | async-start | bytes 1048576 | tf_op jit(solution)/shard_map/all_to_all | solution.py:1079
  17.1 0.0 collective-permute-done.refs_4_
  17.1 0.1 collective-permute-start.1
  17.2 0.5 collective-permute-start.2
  17.7 4.5 %within_chunks.1 = (f32[1024,128]{1,0:T(8,128)}, f32[32,8,128]{2,1,0:T(8,128)}, f32[32,8,128]{2,1,0:T(8,128)}, f32[32,8,128]{2,1,0:T(8,128)}, f32[32,8,128]{2,1,0:T(8,128)}, /*index=5*/f32[11,32,128]{2,1,0:T(8,128)}) custom-call(bf16[32,64,128]{2,1,0:T(8,128)(2,1)} %get-tuple-element.44.refs_0_.refs_8_, ...), custom_call_target="tpu_custom_call" | custom-call | tf_op jit(solution)/shard_map/within_chunks/pallas_call | solution.py:144
  22.2 7.3 %all-to-all-done.refs_7_.refs_1_ = bf16[32,64,128]{2,1,0:T(8,128)(2,1)} async-done(((bf16[32,64,128]{2,1,0:T(8,128)(2,1)}), bf16[32,64,128]{2,1,0:T(8,128)(2,1)}, u32[]{:S(2)}, u32[]{:S(2)}) %all-to-all-start) | async-done | bytes 524320 | tf_op jit(solution)/shard_map/all_to_all | solution.py:1079
  29.5 0.0 collective-permute-done.1.refs_3_
  29.5 0.0 collective-permute-done.2.refs_5_
  29.5 5.8 %activation_and_states.1 = (bf16[32,64,128]{2,1,0:T(8,128)(2,1)}, f32[1024,128]{1,0:T(8,128)}, f32[32,128]{1,0:T(8,128)}, f32[256,128]{1,0:T(8,128)}, f32[256,128]{1,0:T(8,128)}) custom-call(s32[1]{0:T(128)} %bitcast.refs_0_, s32[1]{0:T(128)} %bitcast.1.refs_1_, bf16[32,4224]{1,0:T(8,128)(2,1)} %get-tuple-element.42.refs_2_, ...), custom_call_target="tpu_custom_call" | custom-call | tf_op jit(solution)/shard_map/activation_and_states/pallas_call | solution.py:144
  35.3 0.0 copy-start.2
  35.3 4.6 %all-to-all-start.1 = ((bf16[32,64,128]{2,1,0:T(8,128)(2,1)}), bf16[32,64,128]{2,1,0:T(8,128)(2,1)}, u32[]{:S(2)}, u32[]{:S(2)}) async-start(bf16[32,64,128]{2,1,0:T(8,128)(2,1)} %get-tuple-element.54), calls=%async_computation.1 | async-start | bytes 1048576 | tf_op jit(solution)/shard_map/all_to_all | solution.py:1079
  39.9 0.0 copy-done.2
  39.9 0.1 collective-permute-start.5
  40.0 0.2 collective-permute-start.4
  40.2 1.6 %collective-permute-start.3 = (f32[32,128]{1,0:T(8,128)S(1)}, f32[32,128]{1,0:T(8,128)S(1)}, u32[]{:S(2)}, u32[]{:S(2)}) collective-permute-start(f32[32,128]{1,0:T(8,128)S(1)} %copy-done.2), channel_id=1, source_target_pairs={{0,1},{1,0},{2,3},{3,2},{4,5},{5,4},{6,7},{7,6},{8,9},{9,8},{10,11... | collective-permute-start | bytes 49160 | tf_op jit(solution)/shard_map/ppermute | solution.py:1100
  41.9 4.3 %input_spectrum.1 = (f32[1024,256]{1,0:T(8,128)}, f32[512,128]{1,0:T(8,128)}, f32[2,256,128]{2,1,0:T(8,128)}) custom-call(s32[1]{0:T(128)} %bitcast.refs_0_, bf16[32,64,128]{2,1,0:T(8,128)(2,1)} %all-to-all-done.refs_7_.refs_1_, bf16[512,256]{1,0:T(8,128)(2,1)} %constant.25.clone.refs_2_.refs_1_, bf16[512,256]{1,0:T(8,128)(2,1)} %constant.26.clone.refs_3_.refs_2_, ...), custom_call_target="tpu_custom_call" | custom-call | tf_op jit(solution)/shard_map/input_spectrum/pallas_call | solution.py:144
  46.2 0.0 collective-permute-done.5.refs_15_
  46.2 0.0 copy-start.3
  46.2 0.0 collective-permute-done.4.refs_14_
  46.2 0.0 copy-start.4
  46.2 0.0 collective-permute-done.3.refs_13_
  46.3 0.0 copy-start.5
  46.3 5.2 %all-to-all-done.1.refs_0_.refs_1_ = bf16[32,64,128]{2,1,0:T(8,128)(2,1)} async-done(((bf16[32,64,128]{2,1,0:T(8,128)(2,1)}), bf16[32,64,128]{2,1,0:T(8,128)(2,1)}, u32[]{:S(2)}, u32[]{:S(2)}) %all-to-all-start.1) | async-done | bytes 524320 | tf_op jit(solution)/shard_map/all_to_all | solution.py:1079
  51.4 0.0 copy-done.3
  51.5 0.0 copy-done.4
  51.5 0.0 copy-done.5
  51.5 6.8 %correlation.1.refs_4_ = bf16[32,80,128]{2,1,0:T(8,128)(2,1)} custom-call(bf16[32,64,128]{2,1,0:T(8,128)(2,1)} %all-to-all-done.1.refs_0_.refs_1_, bf16[512,256]{1,0:T(8,128)(2,1)} %constant.25.clone.refs_2_.refs_1_, bf16[512,256]{1,0:T(8,128)(2,1)} %constant.26.clone.refs_3_.refs_2_, f32[2,256,512]{2,1,0:T(8,128)} %constant.27.clone.refs_4_.refs_3_, ...), custom_call_target="tpu_custom_call" | custom-call | tf_op jit(solution)/shard_map/correlation/pallas_call | solution.py:144
  58.2 5.1 %all-to-all-start.2 = ((bf16[32,80,128]{2,1,0:T(8,128)(2,1)}), bf16[32,80,128]{2,1,0:T(8,128)(2,1)S(1)}, u32[]{:S(2)}, u32[]{:S(2)}) async-start(bf16[32,80,128]{2,1,0:T(8,128)(2,1)} %correlation.1.refs_4_), calls=%async_computation.2 | async-start | bytes 1310720 | tf_op jit(solution)/shard_map/all_to_all | solution.py:1079
  63.4 0.0 copy-start
  63.4 0.0 copy-start.1
  63.4 5.7 %signal_gradient.1 = bf16[32,4096]{1,0:T(8,128)(2,1)} custom-call(s32[1]{0:T(128)} %bitcast.refs_0_, bf16[32,64,128]{2,1,0:T(8,128)(2,1)} %all-to-all-done.1.refs_0_.refs_1_, f32[1024,128]{1,0:T(8,128)} %get-tuple-element.55.refs_2_, bf16[32,4096]{1,0:T(8,128)(2,1)} %refs_3_.5, bf16[32,80,128]{2,1,0:T(8,128)(2,1)} %correlation.1.refs_4_, ...), custom_call_target="tpu_custom_call" | custom-call | tf_op jit(solution)/shard_map/signal_gradient/pallas_call | solution.py:144
  69.1 8.5 %all-to-all-done.2.refs_2_ = bf16[32,80,128]{2,1,0:T(8,128)(2,1)S(1)} async-done(((bf16[32,80,128]{2,1,0:T(8,128)(2,1)}), bf16[32,80,128]{2,1,0:T(8,128)(2,1)S(1)}, u32[]{:S(2)}, u32[]{:S(2)}) %all-to-all-start.2) | async-done | bytes 655392 | tf_op jit(solution)/shard_map/all_to_all | solution.py:1079
  77.6 0.0 copy-done
  77.6 0.0 copy-done.1
  77.6 1.9 %outputs.1 = (f32[32,4096]{1,0:T(8,128)}, f32[32,32]{1,0:T(8,128)}, f32[32,32]{1,0:T(8,128)}, f32[32,32]{1,0:T(8,128)}, f32[32,32]{1,0:T(8,128)}, /*index=5*/f32...) custom-call(s32[1]{0:T(128)S(6)} %copy.29.refs_0_, s32[1]{0:T(128)} %bitcast.1.refs_1_, ...), custom_call_target="tpu_custom_call" | custom-call | tf_op jit(solution)/shard_map/outputs/pallas_call | solution.py:144
Async XLA Ops:
  4.7 12.4 %collective-permute-start = (bf16[32,4224]{1,0:T(8,128)(2,1)}, bf16[32,4224]{1,0:T(8,128)(2,1)}, u32[]{:S(2)}, u32[]{:S(2)}) collective-permute-start(bf16[32,4224]{1,0:T(8,128)(2,1)} %get-tuple-element.42.refs_2_), channel_id=1, source_target_pairs={{0,2},{1,3},{2,0},{3,1},{4,6},{5,7},{6,4},{7,5},{8,10},{9,11},{10,... | collective-permute-start | bytes 811016 | tf_op jit(solution)/shard_map/ppermute | solution.py:1100
  6.4 23.1 %all-to-all-start = ((bf16[32,64,128]{2,1,0:T(8,128)(2,1)}), bf16[32,64,128]{2,1,0:T(8,128)(2,1)}, u32[]{:S(2)}, u32[]{:S(2)}) async-start(bf16[32,64,128]{2,1,0:T(8,128)(2,1)} %get-tuple-element.44.refs_0_.refs_8_), calls=%async_computation | async-start | bytes 1048576 | tf_op jit(solution)/shard_map/all_to_all | solution.py:1079
  17.1 12.4 %collective-permute-start.1 = (bf16[32,4224]{1,0:T(8,128)(2,1)}, bf16[32,4224]{1,0:T(8,128)(2,1)}, u32[]{:S(2)}, u32[]{:S(2)}) collective-permute-start(bf16[32,4224]{1,0:T(8,128)(2,1)} %get-tuple-element.42.refs_2_), channel_id=1, source_target_pairs={{0,1},{1,0},{2,3},{3,2},{4,5},{5,4},{6,7},{7,6},{8,9},{9,8},{10,11... | collective-permute-start | bytes 811016 | tf_op jit(solution)/shard_map/ppermute | solution.py:1100
  17.2 12.3 %collective-permute-start.2 = (bf16[32,4224]{1,0:T(8,128)(2,1)}, bf16[32,4224]{1,0:T(8,128)(2,1)}, u32[]{:S(2)}, u32[]{:S(2)}) collective-permute-start(bf16[32,4224]{1,0:T(8,128)(2,1)} %collective-permute-done.refs_4_), channel_id=1, source_target_pairs={{0,1},{1,0},{2,3},{3,2},{4,5},{5,4},{6,7},{7,6},{8,9},{9,8},{10,11... | collective-permute-start | bytes 811016 | tf_op jit(solution)/shard_map/ppermute | solution.py:1100
  35.3 4.7 %copy-start.2 = (f32[32,128]{1,0:T(8,128)S(1)}, f32[32,128]{1,0:T(8,128)}, u32[]{:S(2)}) copy-start(f32[32,128]{1,0:T(8,128)} %get-tuple-element.56.refs_7_.refs_12_) | copy-start | bytes 49156
  35.3 16.2 %all-to-all-start.1 = ((bf16[32,64,128]{2,1,0:T(8,128)(2,1)}), bf16[32,64,128]{2,1,0:T(8,128)(2,1)}, u32[]{:S(2)}, u32[]{:S(2)}) async-start(bf16[32,64,128]{2,1,0:T(8,128)(2,1)} %get-tuple-element.54), calls=%async_computation.1 | async-start | bytes 1048576 | tf_op jit(solution)/shard_map/all_to_all | solution.py:1079
  39.9 6.3 %collective-permute-start.5 = (f32[32,128]{1,0:T(8,128)S(1)}, f32[32,128]{1,0:T(8,128)S(1)}, u32[]{:S(2)}, u32[]{:S(2)}) collective-permute-start(f32[32,128]{1,0:T(8,128)S(1)} %copy-done.2), channel_id=1, source_target_pairs={{0,3},{1,2},{2,1},{3,0},{4,7},{5,6},{6,5},{7,4},{8,11},{9,10},{10,... | collective-permute-start | bytes 49160 | tf_op jit(solution)/shard_map/ppermute | solution.py:1100
  40.0 6.2 %collective-permute-start.4 = (f32[32,128]{1,0:T(8,128)S(1)}, f32[32,128]{1,0:T(8,128)S(1)}, u32[]{:S(2)}, u32[]{:S(2)}) collective-permute-start(f32[32,128]{1,0:T(8,128)S(1)} %copy-done.2), channel_id=1, source_target_pairs={{0,2},{1,3},{2,0},{3,1},{4,6},{5,7},{6,4},{7,5},{8,10},{9,11},{10,... | collective-permute-start | bytes 49160 | tf_op jit(solution)/shard_map/ppermute | solution.py:1100
  40.2 6.0 %collective-permute-start.3 = (f32[32,128]{1,0:T(8,128)S(1)}, f32[32,128]{1,0:T(8,128)S(1)}, u32[]{:S(2)}, u32[]{:S(2)}) collective-permute-start(f32[32,128]{1,0:T(8,128)S(1)} %copy-done.2), channel_id=1, source_target_pairs={{0,1},{1,0},{2,3},{3,2},{4,5},{5,4},{6,7},{7,6},{8,9},{9,8},{10,11... | collective-permute-start | bytes 49160 | tf_op jit(solution)/shard_map/ppermute | solution.py:1100
  46.2 5.2 %copy-start.3 = (f32[32,128]{1,0:T(8,128)}, f32[32,128]{1,0:T(8,128)S(1)}, u32[]{:S(2)}) copy-start(f32[32,128]{1,0:T(8,128)S(1)} %collective-permute-done.5.refs_15_) | copy-start | bytes 49156
  46.2 5.2 %copy-start.4 = (f32[32,128]{1,0:T(8,128)}, f32[32,128]{1,0:T(8,128)S(1)}, u32[]{:S(2)}) copy-start(f32[32,128]{1,0:T(8,128)S(1)} %collective-permute-done.4.refs_14_) | copy-start | bytes 49156
  46.3 5.2 %copy-start.5 = (f32[32,128]{1,0:T(8,128)}, f32[32,128]{1,0:T(8,128)S(1)}, u32[]{:S(2)}) copy-start(f32[32,128]{1,0:T(8,128)S(1)} %collective-permute-done.3.refs_13_) | copy-start | bytes 49156
  58.2 19.4 %all-to-all-start.2 = ((bf16[32,80,128]{2,1,0:T(8,128)(2,1)}), bf16[32,80,128]{2,1,0:T(8,128)(2,1)S(1)}, u32[]{:S(2)}, u32[]{:S(2)}) async-start(bf16[32,80,128]{2,1,0:T(8,128)(2,1)} %correlation.1.refs_4_), calls=%async_computation.2 | async-start | bytes 1310720 | tf_op jit(solution)/shard_map/all_to_all | solution.py:1079
  63.4 14.2 %copy-start = (f32[2,32,128]{2,1,0:T(8,128)S(1)}, f32[2,32,128]{2,1,0:T(8,128)}, u32[]{:S(2)}) copy-start(f32[2,32,128]{2,1,0:T(8,128)} %get-tuple-element.46.refs_2_.refs_10_.refs_9_.refs_6_.refs_4_) | copy-start | bytes 98308
  63.4 14.2 %copy-start.1 = (f32[11,32,128]{2,1,0:T(8,128)S(1)}, f32[11,32,128]{2,1,0:T(8,128)}, u32[]{:S(2)}) copy-start(f32[11,32,128]{2,1,0:T(8,128)} %get-tuple-element.62.refs_3_) | copy-start | bytes 540676
